TPU v7x, 256 devices: a whole 4x4x8 slice. The times are simulated.
256 devices in a mesh: expert: 32 (over y, x, core), etp: 8 (over z).
Axes of the slice: x: 4, y: 4, z: 8, core: 2. Of those that a mesh axis runs over, the one named last changes fastest.
Arguments:
- tokens: bfloat16 [8192, 2048], P('expert', 'etp'), may hold values from -6 to 6
- expert_ids: int32 [8192, 8], P('expert'), may hold values from 0 to 127, all different within a row; in each aligned block of 256 rows (0 to 255, 256 to 511, ...) at most 24 rows name the same one
- route_weights: float32 [8192, 8], P('expert'), may hold values from 0.05 to 0.3
- gate_weight: bfloat16 [256, 384, 2048], P(('expert', 'etp')), may hold values from -0.125 to 0.125
- up_weight: bfloat16 [256, 384, 2048], P(('expert', 'etp')), may hold values from -0.125 to 0.125
- down_weight: bfloat16 [256, 384, 2048], P(('expert', 'etp')), may hold values from -0.21875 to 0.21875
- grad_out: bfloat16 [8192, 2048], P('expert', 'etp'), may hold values from -6 to 6
Outputs:
- mixed: bfloat16 [8192, 2048], P('expert', 'etp')
- grad_tokens: bfloat16 [8192, 2048], P('expert', 'etp')
- grad_route: float32 [8192, 8], P('expert')
- grad_gate: bfloat16 [256, 384, 2048], P(('expert', 'etp'))
- grad_up: bfloat16 [256, 384, 2048], P(('expert', 'etp'))
- grad_down: bfloat16 [256, 384, 2048], P(('expert', 'etp'))
Inputs may be any that keep to these rules, and one draw needn't show every extreme that they name: `expert_ids`: each row names 8 different experts. Among the 256 rows of one index of expert (aligned blocks of rows), no expert is named by more than 24 rows, a bound that some block reaches.
All inputs are finite; a program needn't handle non-finite values.
Results may differ from a plain program's by a relative error of at most 0.0064.
Values may be sent and summed in bfloat16 or wider, within the bound.
No kernel may reach another device: no remote copies, remote signals or barrier semaphores. Data moves between devices by JAX's collectives and lax.ppermute only.
A program may use at most 128 MiB of HBM per device.

v0:
```python
import functools

import jax
import jax.numpy as jnp
from jax import lax
from jax.experimental import pallas as pl
from jax.experimental.pallas import tpu as pltpu
from jax.sharding import PartitionSpec as P

EXP_DEV = 4
ROW_CUTS = 3
VMEM_BYTES = 32 * 1024 * 1024
F32 = jnp.float32
BF16 = jnp.bfloat16
LAST = ((1,), (1,))
FLAT = ((1,), (0,))
TALL = ((0,), (0,))


def shift(value, step, lanes):
    return lax.ppermute(value, "etp", [(i, (i + step) % lanes) for i in range(lanes)])


def swap(value, lanes):
    return lax.ppermute(value, "etp", [(i, i ^ 1) for i in range(lanes)])


def dot(a, b, dims):
    return lax.dot_general(a, b, (dims, ((), ())), preferred_element_type=F32)


def across(rows, groups):
    slots, width = rows.shape
    cut = rows.reshape(groups, slots // groups, width)
    moved = lax.all_to_all(cut, "expert", split_axis=0, concat_axis=0, tiled=True)
    return moved.reshape(slots, width)


def call(body, scalars, grid, operands, in_blocks, outs, out_blocks, flops, scratch=()):
    def spec(block):
        return pl.BlockSpec(*block)

    moved = sum(x.size * x.dtype.itemsize for x in (*operands, *outs))
    return pl.pallas_call(
        body,
        grid_spec=pltpu.PrefetchScalarGridSpec(
            num_scalar_prefetch=1,
            grid=grid,
            in_specs=[spec(b) for b in in_blocks],
            out_specs=[spec(b) for b in out_blocks],
            scratch_shapes=list(scratch),
        ),
        out_shape=list(outs),
        compiler_params=pltpu.CompilerParams(vmem_limit_bytes=VMEM_BYTES),
        cost_estimate=pl.CostEstimate(flops=flops, bytes_accessed=moved, transcendentals=0),
    )(scalars, *operands)


def whole(array):
    return (array.shape, lambda i, s: (0,) * array.ndim)


def half_columns(ref, parity, shard, index):
    return ref[:, pl.ds(pl.multiple_of((2 * index + parity) * shard, shard), shard)]


def gather_body(shard, s_ref, select_ref, *refs):
    out_ref = refs[-1]
    local_expert = s_ref[0] // 2
    select = select_ref[...]
    for r, ref in enumerate(refs[:-1]):
        start = pl.multiple_of(lax.rem(local_expert - r + EXP_DEV, EXP_DEV) * shard, shard)
        out_ref[:, pl.ds(start, shard)] = dot(select, ref[...], TALL).astype(BF16)


def first_body(shard, s_ref, rows_ref, gate_ref, up_ref, gate_out, up_out):
    parity = lax.rem(s_ref[0], 2)
    for w_ref, out_ref in ((gate_ref, gate_out), (up_ref, up_out)):
        total = None
        for j in range(EXP_DEV):
            part = dot(
                rows_ref[:, j * shard : (j + 1) * shard],
                half_columns(w_ref, parity, shard, j),
                LAST,
            )
            total = part if total is None else total + part
        out_ref[...] = total


def second_body(
    shard, s_ref, rows_ref, gate_in, up_in, gate_ref, up_ref, down_ref,
    hidden_out, gate_slope, up_slope, part_out,
):
    other = 1 - lax.rem(s_ref[0], 2)
    acts = []
    for w_ref, in_ref in ((gate_ref, gate_in), (up_ref, up_in)):
        total = in_ref[...]
        for j in range(EXP_DEV):
            total = total + dot(
                rows_ref[:, j * shard : (j + 1) * shard],
                half_columns(w_ref, other, shard, j),
                LAST,
            )
        acts.append(total)
    gate_act, up_act = acts
    sig = jax.nn.sigmoid(gate_act)
    gated = gate_act * sig
    hidden = (gated * up_act).astype(BF16)
    hidden_out[...] = hidden
    up_slope[...] = gated
    gate_slope[...] = up_act * sig * (1.0 + gate_act * (1.0 - sig))
    part_out[...] = dot(hidden, down_ref[...], FLAT).astype(BF16)


def third_body(
    shard, s_ref, grad_ref, gate_slope, up_slope, gate_ref, up_ref, down_ref,
    gate_out, up_out, other_out,
):
    other = 1 - lax.rem(s_ref[0], 2)
    grad_hidden = dot(grad_ref[...], down_ref[...], LAST)
    grad_gate = (grad_hidden * gate_slope[...]).astype(BF16)
    grad_up = (grad_hidden * up_slope[...]).astype(BF16)
    gate_out[...] = grad_gate
    up_out[...] = grad_up
    for j in range(EXP_DEV):
        other_out[:, j * shard : (j + 1) * shard] = (
            dot(grad_gate, half_columns(gate_ref, other, shard, j), FLAT)
            + dot(grad_up, half_columns(up_ref, other, shard, j), FLAT)
        ).astype(BF16)


def mine_body(shard, s_ref, grad_gate, grad_up, gate_ref, up_ref, out_ref):
    parity = lax.rem(s_ref[0], 2)
    for j in range(EXP_DEV):
        out_ref[:, j * shard : (j + 1) * shard] = dot(
            grad_gate[...], half_columns(gate_ref, parity, shard, j), FLAT
        ) + dot(grad_up[...], half_columns(up_ref, parity, shard, j), FLAT)


def weights_body(
    s_ref, hidden_ref, grad_gate, grad_up, rows_mine, rows_other, grad_ref,
    gate_out, up_out, down_out,
):
    down_out[0] = dot(hidden_ref[...], grad_ref[...], TALL).astype(BF16)
    here = lax.rem(pl.program_id(0), 2) == lax.rem(s_ref[0], 2)

    def write(rows):
        gate_out[0] = dot(grad_gate[...], rows, TALL).astype(BF16)
        up_out[0] = dot(grad_up[...], rows, TALL).astype(BF16)

    @pl.when(here)
    def _():
        write(rows_mine[...])

    @pl.when(jnp.logical_not(here))
    def _():
        write(rows_other[...])


def mix_body(s_ref, high_ref, low_ref, rows_ref, grad_ref, mine_out, piece_out, product_out):
    step = pl.program_id(0)
    rows = rows_ref[...]
    part = dot(high_ref[...], rows, FLAT) + dot(low_ref[...], rows, FLAT)
    product = dot(grad_ref[...], rows, LAST)

    @pl.when(step == 0)
    def _():
        mine_out[...] = part
        product_out[...] = product

    @pl.when(step > 0)
    def _():
        product_out[...] += product

    piece_out[0] = part.astype(BF16)


def spread_body(s_ref, select_ref, rows_ref, mine_out, piece_out):
    part = dot(select_ref[...], rows_ref[...], FLAT)

    @pl.when(pl.program_id(0) == 0)
    def _():
        mine_out[...] = part

    piece_out[0] = part.astype(BF16)


def per_device(tokens, expert_ids, route_weights, gate_weight, up_weight, down_weight, grad_out):
    tok_count, top_count = expert_ids.shape
    units, model_width = gate_weight.shape[1:]
    shard = tokens.shape[1]
    groups = lax.axis_size("expert")
    lanes = lax.axis_size("etp")
    halves = lanes // EXP_DEV
    experts = EXP_DEV * groups
    capacity = max(2, tok_count * top_count * 3 // (2 * experts))
    slots = groups * capacity
    half = model_width // halves
    lane = lax.axis_index("etp")
    local_expert = lane // halves
    scalars = lane.astype(jnp.int32).reshape(1)
    w_gate = gate_weight[0]
    w_up = up_weight[0]
    w_down = down_weight[0]
    block = slots // ROW_CUTS
    row_grid = (ROW_CUTS,)
    unit_flops = 2 * slots * units * half

    def shape(rows, width, kind=BF16):
        return jax.ShapeDtypeStruct((rows, width), kind)

    def row_block(width):
        return ((block, width), lambda i, s: (i, 0))

    grad_full = lax.all_gather(grad_out, "etp", axis=1, tiled=True)
    own = [tokens] + [shift(tokens, halves * r, lanes) for r in range(1, EXP_DEV)]

    column = lax.broadcasted_iota(jnp.int32, (1, slots), 1)
    col_expert = column // capacity * EXP_DEV + local_expert
    col_slot = (column % capacity).astype(F32)
    hits = [expert_ids[:, k : k + 1] == col_expert for k in range(top_count)]
    member = hits[0]
    for hit in hits[1:]:
        member = member | hit
    member = member.astype(BF16)
    row = lax.broadcasted_iota(jnp.int32, (tok_count, tok_count), 0)
    earlier = (lax.broadcasted_iota(jnp.int32, (tok_count, tok_count), 1) < row).astype(BF16)
    rank = dot(earlier, member, FLAT)
    chosen = (member > 0) & (rank == col_slot)
    select = chosen.astype(BF16)
    weight = jnp.zeros((tok_count, slots), F32)
    for k in range(top_count):
        weight = jnp.where(hits[k], route_weights[:, k : k + 1], weight)
    weight = jnp.where(chosen, weight, 0.0)
    slot_weight = jnp.sum(weight, axis=0)[:, None]
    weight_high = lax.reduce_precision(weight, 8, 7)
    weight_low = (weight - weight_high).astype(BF16)
    weight_high = weight_high.astype(BF16)

    (sent,) = call(
        functools.partial(gather_body, shard), scalars, (1,),
        [select, *own], [whole(select)] + [whole(x) for x in own],
        [shape(slots, half)], [((slots, half), lambda i, s: (0, 0))],
        2 * slots * tok_count * half,
    )
    rows_mine = across(sent, groups)
    rows_other = swap(rows_mine, lanes)

    scaled = (dot(select, grad_full, TALL) * slot_weight).astype(BF16)
    grad_rows = across(scaled, groups)

    f32_rows = shape(slots, units, F32)
    bf16_rows = shape(slots, units)
    unit_block = row_block(units)
    gate_first, up_first = call(
        functools.partial(first_body, shard), scalars, row_grid,
        [rows_mine, w_gate, w_up], [row_block(half), whole(w_gate), whole(w_up)],
        [f32_rows, f32_rows], [unit_block, unit_block], 2 * unit_flops,
    )
    hidden, gate_slope, up_slope, expert_part = call(
        functools.partial(second_body, shard), scalars, row_grid,
        [rows_other, gate_first, up_first, w_gate, w_up, w_down],
        [row_block(half), unit_block, unit_block, whole(w_gate), whole(w_up), whole(w_down)],
        [bf16_rows, f32_rows, f32_rows, shape(slots, model_width)],
        [unit_block, unit_block, unit_block, row_block(model_width)], 4 * unit_flops,
    )
    returned = across(expert_part, groups)

    grad_gate_act, grad_up_act, input_other = call(
        functools.partial(third_body, shard), scalars, row_grid,
        [grad_rows, gate_slope, up_slope, w_gate, w_up, w_down],
        [row_block(model_width), unit_block, unit_block]
        + [whole(w_gate), whole(w_up), whole(w_down)],
        [bf16_rows, bf16_rows, shape(slots, half)],
        [unit_block, unit_block, row_block(half)], 4 * unit_flops,
    )
    input_swapped = swap(input_other, lanes)
    (input_mine,) = call(
        functools.partial(mine_body, shard), scalars, row_grid,
        [grad_gate_act, grad_up_act, w_gate, w_up],
        [unit_block, unit_block, whole(w_gate), whole(w_up)],
        [shape(slots, half, F32)], [row_block(half)], 2 * unit_flops,
    )
    input_half = (input_mine + input_swapped.astype(F32)).astype(BF16)
    grad_back = across(input_half, groups)

    pair_block = ((slots, shard), lambda i, s: (0, i // 2))
    grad_shape = jax.ShapeDtypeStruct((1, units, model_width), BF16)
    grad_block = ((1, units, shard), lambda i, s: (0, 0, i))
    grad_gate, grad_up, grad_down = call(
        weights_body, scalars, (lanes,),
        [hidden, grad_gate_act, grad_up_act, rows_mine, rows_other, grad_rows],
        [whole(hidden), whole(hidden), whole(hidden), pair_block, pair_block]
        + [((slots, shard), lambda i, s: (0, i))],
        [grad_shape] * 3, [grad_block] * 3, 6 * unit_flops,
    )

    def ahead(i, s):
        return (0, lax.rem(s[0] + i, lanes))

    own_block = ((tok_count, shard), lambda i, s: (0, 0))
    mixed, mixed_pieces, products = call(
        mix_body, scalars, (lanes,),
        [weight_high, weight_low, returned, grad_full],
        [whole(weight_high), whole(weight_low)]
        + [((slots, shard), ahead), ((tok_count, shard), ahead)],
        [shape(tok_count, shard, F32), jax.ShapeDtypeStruct((lanes, tok_count, shard), BF16)]
        + [shape(tok_count, slots, F32)],
        [own_block, ((1, tok_count, shard), lambda i, s: (i, 0, 0)), whole(select)],
        6 * tok_count * slots * model_width,
    )
    for r in range(1, lanes):
        mixed = mixed + shift(mixed_pieces[r], r, lanes).astype(F32)
    mixed = mixed.astype(BF16)

    products = jnp.where(chosen, products, 0.0)
    route_sum = jnp.stack(
        [jnp.sum(jnp.where(hits[k], products, 0.0), axis=1) for k in range(top_count)]
    )
    route_sum = route_sum + swap(route_sum, lanes)
    route_1 = lax.reduce_precision(route_sum, 8, 7)
    rest = route_sum - route_1
    route_2 = lax.reduce_precision(rest, 8, 7)
    route_3 = rest - route_2
    route_pack = jnp.concatenate([route_1, route_2, route_3], axis=0).astype(BF16)
    pack_rows = -(-3 * top_count // 16) * 16
    route_pack = jnp.pad(
        route_pack, ((0, pack_rows - 3 * top_count), (0, shard - tok_count))
    )

    grad_tokens, token_pieces = call(
        spread_body, scalars, (EXP_DEV,),
        [select, grad_back],
        [whole(select)]
        + [((slots, shard), lambda i, s: (0, lax.rem(s[0] // 2 + i, EXP_DEV)))],
        [shape(tok_count, shard, F32), jax.ShapeDtypeStruct((EXP_DEV, tok_count, shard), BF16)],
        [own_block, ((1, tok_count, shard), lambda i, s: (i, 0, 0))],
        2 * tok_count * slots * half,
    )
    for r in range(1, EXP_DEV):
        piece = jnp.concatenate([token_pieces[r], route_pack], axis=0)
        piece = shift(piece, halves * r, lanes).astype(F32)
        grad_tokens = grad_tokens + piece[:tok_count]
        got = piece[tok_count:, :tok_count]
        route_sum = route_sum + (
            got[:top_count] + got[top_count : 2 * top_count] + got[2 * top_count : 3 * top_count]
        )
    grad_tokens = grad_tokens.astype(BF16)
    grad_route = route_sum.T
    return (mixed, grad_tokens, grad_route, grad_gate, grad_up, grad_down)


def solution(mesh):
    placed = (
        P("expert", "etp"),
        P("expert", None),
        P("expert", None),
        P(("expert", "etp"), None, None),
        P(("expert", "etp"), None, None),
        P(("expert", "etp"), None, None),
        P("expert", "etp"),
    )
    return jax.shard_map(
        per_device,
        mesh=mesh,
        in_specs=placed,
        out_specs=(
            P("expert", "etp"),
            P("expert", "etp"),
            P("expert", None),
            P(("expert", "etp"), None, None),
            P(("expert", "etp"), None, None),
            P(("expert", "etp"), None, None),
        ),
        check_vma=False,
    )
```

profile of v0, /device:TPU:2, one launch (start us, length us, event | category | flops | bytes accessed | tf_op | source)
XLA Modules:
  0.0 254.4 jit_solution(97266629491866467)
XLA Ops:
  7.2 3.3 %collective-permute-start = (bf16[256,256]{1,0:T(8,128)(2,1)}, bf16[256,256]{1,0:T(8,128)(2,1)S(1)}, u32[]{:S(2)}, u32[]{:S(2)}) collective-permute-start(bf16[256,256]{1,0:T(8,128)(2,1)} %refs_0_.1), channel_id=1, source_target_pairs={{0,2},{1,3},{2,4},{3,5},{4,6},{5,7},{6,0},{7,1},{8,10},{9,11},{10,... | collective-permute-start | bytes 393224 | tf_op jit(solution)/shard_map/ppermute | solution.py:21
  10.6 5.4 %collective-permute-start.1 = (bf16[256,256]{1,0:T(8,128)(2,1)}, bf16[256,256]{1,0:T(8,128)(2,1)S(1)}, u32[]{:S(2)}, u32[]{:S(2)}) collective-permute-start(bf16[256,256]{1,0:T(8,128)(2,1)} %refs_0_.1), channel_id=1, source_target_pairs={{0,4},{1,5},{2,6},{3,7},{4,0},{5,1},{6,2},{7,3},{8,12},{9,13},{10,... | collective-permute-start | bytes 393224 | tf_op jit(solution)/shard_map/ppermute | solution.py:21
  15.9 2.7 %collective-permute-start.2 = (bf16[256,256]{1,0:T(8,128)(2,1)}, bf16[256,256]{1,0:T(8,128)(2,1)S(1)}, u32[]{:S(2)}, u32[]{:S(2)}) collective-permute-start(bf16[256,256]{1,0:T(8,128)(2,1)} %refs_0_.1), channel_id=1, source_target_pairs={{0,6},{1,7},{2,0},{3,1},{4,2},{5,3},{6,4},{7,5},{8,14},{9,15},{10,... | collective-permute-start | bytes 393224 | tf_op jit(solution)/shard_map/ppermute | solution.py:21
  20.8 2.7 %fusion.41 = (f32[768]{0:T(1024)S(1)}, f32[256,768]{1,0:T(8,128)}, pred[256,768]{1,0:T(32,128)(4,1)S(1)}) fusion(f32[256]{0:T(256)S(1)} %bitcast.107, s32[256]{0:T(256)S(1)} %bitcast.77, f32[256]{0:T(256)S(1)} %bitcast.108, s32[256]{0:T(256)S(1)} %bitcast.87, f32[256]{0:T(256)S(1)} %bitcast.102, s32[256]{0:T(256)S(1)} %bitcast.85, f32[256]{0:T(256)S(1)} %bitcast.103, ...), kind=kOutput, calls=%fused_computation.103 | convolution fusion | flops 109772032 | bytes 1008640 | tf_op jit(solution)/shard_map/dot_general | solution.py:29
  23.6 1.5 collective-permute-done.1.refs_2_
  25.1 3.3 %collective-permute-done.2.refs_3_ = bf16[256,256]{1,0:T(8,128)(2,1)S(1)} collective-permute-done((bf16[256,256]{1,0:T(8,128)(2,1)}, bf16[256,256]{1,0:T(8,128)(2,1)S(1)}, u32[]{:S(2)}, u32[]{:S(2)}) %collective-permute-start.2) | collective-permute-done | bytes 131104 | tf_op jit(solution)/shard_map/ppermute | solution.py:21
  28.4 1.7 shard_map.118
  30.1 7.6 %all-to-all-start = ((bf16[32,24,1024]{2,1,0:T(8,128)(2,1)}), bf16[32,24,1024]{2,1,0:T(8,128)(2,1)S(1)}, u32[]{:S(2)}, u32[]{:S(2)}) async-start(bf16[32,24,1024]{2,1,0:T(8,128)(2,1)} %bitcast.17), calls=%async_computation | async-start | bytes 3145728 | tf_op jit(solution)/shard_map/all_to_all | solution.py:35
  37.7 17.4 %all-gather.2.cloned.1.call-done.grad_ref = bf16[256,2048]{1,0:T(8,128)(2,1)} async-done(((bf16[256,256]{1,0:T(8,128)(2,1)}), bf16[256,2048]{1,0:T(8,128)(2,1)}) %all-gather.2.cloned.1.call-update) | async-done | bytes 1048592 | tf_op jit(solution)/shard_map/all_gather | solution.py:215
  55.2 3.9 %multiply_convert_fusion = bf16[768,2048]{1,0:T(8,128)(2,1)} fusion(pred[256,768]{1,0:T(32,128)(4,1)S(1)} %get-tuple-element.85, bf16[256,2048]{1,0:T(8,128)(2,1)} %all-gather.2.cloned.1.call-done.grad_ref, f32[768]{0:T(1024)S(1)} %get-tuple-element.48), kind=kOutput, calls=%fused_computation | convolution fusion | flops 808452096 | bytes 4393984 | tf_op jit(solution)/shard_map/dot_general | solution.py:29
  60.9 7.1 %all-to-all-start.2 = ((bf16[32,24,2048]{2,1,0:T(8,128)(2,1)}), bf16[32,24,2048]{2,1,0:T(8,128)(2,1)}, u32[]{:S(2)}, u32[]{:S(2)}) async-start(bf16[32,24,2048]{2,1,0:T(8,128)(2,1)} %bitcast.76), calls=%async_computation.2 | async-start | bytes 6291456 | tf_op jit(solution)/shard_map/all_to_all | solution.py:35
  71.0 2.2 shard_map.119
  73.2 31.6 %collective-permute-done.3.rows_ref.rows_other = bf16[768,1024]{1,0:T(8,128)(2,1)S(1)} collective-permute-done((bf16[768,1024]{1,0:T(8,128)(2,1)}, bf16[768,1024]{1,0:T(8,128)(2,1)S(1)}, u32[]{:S(2)}, u32[]{:S(2)}) %collective-permute-start.3) | collective-permute-done | bytes 1572896 | tf_op jit(solution)/shard_map/ppermute | solution.py:25
  104.8 4.2 %shard_map.120 = (bf16[768,384]{1,0:T(8,128)(2,1)S(1)}, f32[768,384]{1,0:T(8,128)S(1)}, f32[768,384]{1,0:T(8,128)S(1)}, bf16[768,2048]{1,0:T(8,128)(2,1)S(1)}) custom-call(s32[1]{0:T(128)} %bitcast.s_ref, bf16[768,1024]{1,0:T(8,128)(2,1)S(1)} %collective-permute-done.3.rows_ref.rows_other, f32[768,384]{1,0:T(8,128)S(1)} %get-tuple-element.23.gate_in, ...), custom_call_target="tpu_custom_call" | custom-call | flops 2415919104 | bytes 14745600 | tf_op jit(solution)/shard_map/pallas_call | solution.py:44
  109.0 1.7 copy-done.5
  114.7 7.4 %all-to-all-start.1 = ((bf16[32,24,2048]{2,1,0:T(8,128)(2,1)}), bf16[32,24,2048]{2,1,0:T(8,128)(2,1)}, u32[]{:S(2)}, u32[]{:S(2)}) async-start(bf16[32,24,2048]{2,1,0:T(8,128)(2,1)} %bitcast.72), calls=%async_computation.1 | async-start | bytes 6291456 | tf_op jit(solution)/shard_map/all_to_all | solution.py:35
  126.1 5.5 %shard_map.122 = (bf16[768,384]{1,0:T(8,128)(2,1)S(1)}, bf16[768,384]{1,0:T(8,128)(2,1)S(1)}, bf16[768,1024]{1,0:T(8,128)(2,1)S(1)}) custom-call(s32[1]{0:T(128)} %bitcast.s_ref, bf16[768,2048]{1,0:T(8,128)(2,1)} %bitcast.32.grad_ref, f32[768,384]{1,0:T(8,128)S(1)} %copy-done.9, f32[768,384]{1,0:T(8,128)S(1)} %copy-done.11, bf16[384,2048]{1,0:T(8,128)(2,1)S(1)} %bitcast.62, ...), custom_call_target="tpu_custom_call" | custom-call | flops 2415919104 | bytes 12976128 | tf_op jit(solution)/shard_map/pallas_call | solution.py:44
  131.6 1.6 collective-permute-start.11
  134.3 2.2 shard_map.123
  136.5 31.8 %collective-permute-done.11 = bf16[768,1024]{1,0:T(8,128)(2,1)S(1)} collective-permute-done((bf16[768,1024]{1,0:T(8,128)(2,1)S(1)}, bf16[768,1024]{1,0:T(8,128)(2,1)S(1)}, u32[]{:S(2)}, u32[]{:S(2)}) %collective-permute-start.11) | collective-permute-done | bytes 1572896 | tf_op jit(solution)/shard_map/ppermute | solution.py:25
  168.4 1.7 add_convert_fusion
  170.1 7.5 %all-to-all-start.3 = ((bf16[32,24,1024]{2,1,0:T(8,128)(2,1)}), bf16[32,24,1024]{2,1,0:T(8,128)(2,1)S(1)}, u32[]{:S(2)}, u32[]{:S(2)}) async-start(bf16[32,24,1024]{2,1,0:T(8,128)(2,1)} %bitcast.75), calls=%async_computation.3 | async-start | bytes 3145728 | tf_op jit(solution)/shard_map/all_to_all | solution.py:35
  182.2 10.3 %shard_map.125 = (bf16[1,384,2048]{2,1,0:T(8,128)(2,1)}, bf16[1,384,2048]{2,1,0:T(8,128)(2,1)}, bf16[1,384,2048]{2,1,0:T(8,128)(2,1)}) custom-call(s32[1]{0:T(128)} %bitcast.s_ref, bf16[768,384]{1,0:T(8,128)(2,1)S(1)} %copy-done.23, bf16[768,384]{1,0:T(8,128)(2,1)S(1)} %copy-done.13, bf16[768,384]{1,0:T(8,128)(2,1)S(1)} %copy-done.15, ...), custom_call_target="tpu_custom_call" | custom-call | flops 3623878656 | bytes 12779520 | tf_op jit(solution)/shard_map/pallas_call | solution.py:44
  192.6 7.2 %shard_map.121 = (f32[256,256]{1,0:T(8,128)S(1)}, bf16[8,256,256]{2,1,0:T(8,128)(2,1)S(1)}, f32[256,768]{1,0:T(8,128)S(1)}) custom-call(s32[1]{0:T(128)} %bitcast.s_ref, bf16[256,768]{1,0:T(8,128)(2,1)S(1)} %copy-done.17, bf16[256,768]{1,0:T(8,128)(2,1)S(1)} %copy-done.16, bf16[768,2048]{1,0:T(8,128)(2,1)} %bitcast.23.rows_ref, bf16[256,2048]{1,0:T(8,128)(2,1)S(1)} %copy-done.21), custom_call_target="tpu_custom_call" | custom-call | flops 2415919104 | bytes 7077888 | tf_op jit(solution)/shard_map/pallas_call | solution.py:44
  203.3 3.5 %collective-permute-start.10 = (bf16[256,256]{1,0:T(8,128)(2,1)}, bf16[256,256]{1,0:T(8,128)(2,1)S(1)}, u32[]{:S(2)}, u32[]{:S(2)}) collective-permute-start(bf16[256,256]{1,0:T(8,128)(2,1)} %get-tuple-element.53), channel_id=1, source_target_pairs={{0,7},{1,0},{2,1},{3,2},{4,3},{5,4},{6,5},{7,6},{8,15},{9,8},{10,9... | collective-permute-start | bytes 393224 | tf_op jit(solution)/shard_map/ppermute | solution.py:21
  207.1 2.2 collective-permute-start.8
  209.4 3.6 %collective-permute-start.7 = (bf16[256,256]{1,0:T(8,128)(2,1)}, bf16[256,256]{1,0:T(8,128)(2,1)S(1)}, u32[]{:S(2)}, u32[]{:S(2)}) collective-permute-start(bf16[256,256]{1,0:T(8,128)(2,1)} %get-tuple-element.56), channel_id=1, source_target_pairs={{0,4},{1,5},{2,6},{3,7},{4,0},{5,1},{6,2},{7,3},{8,12},{9,13},{10,... | collective-permute-start | bytes 393224 | tf_op jit(solution)/shard_map/ppermute | solution.py:21
  214.5 3.3 %collective-permute-start.5 = (bf16[256,256]{1,0:T(8,128)(2,1)S(1)}, bf16[256,256]{1,0:T(8,128)(2,1)S(1)}, u32[]{:S(2)}, u32[]{:S(2)}) collective-permute-start(bf16[256,256]{1,0:T(8,128)(2,1)S(1)} %get-tuple-element.58), channel_id=1, source_target_pairs={{0,2},{1,3},{2,4},{3,5},{4,6},{5,7},{6,0},{7,1},{8,10},{9,11},{10,... | collective-permute-start | bytes 393224 | tf_op jit(solution)/shard_map/ppermute | solution.py:21
  217.8 4.1 %collective-permute-done.9 = bf16[256,256]{1,0:T(8,128)(2,1)S(1)} collective-permute-done((bf16[256,256]{1,0:T(8,128)(2,1)}, bf16[256,256]{1,0:T(8,128)(2,1)S(1)}, u32[]{:S(2)}, u32[]{:S(2)}) %collective-permute-start.9) | collective-permute-done | bytes 131104 | tf_op jit(solution)/shard_map/ppermute | solution.py:21
  222.0 10.0 %collective-permute-done.8 = bf16[256,256]{1,0:T(8,128)(2,1)S(1)} collective-permute-done((bf16[256,256]{1,0:T(8,128)(2,1)}, bf16[256,256]{1,0:T(8,128)(2,1)S(1)}, u32[]{:S(2)}, u32[]{:S(2)}) %collective-permute-start.8) | collective-permute-done | bytes 131104 | tf_op jit(solution)/shard_map/ppermute | solution.py:21
  232.4 3.2 %collective-permute-start.14 = (bf16[288,256]{1,0:T(8,128)(2,1)S(1)}, bf16[288,256]{1,0:T(8,128)(2,1)S(1)}, u32[]{:S(2)}, u32[]{:S(2)}) collective-permute-start(bf16[288,256]{1,0:T(8,128)(2,1)S(1)} %get-tuple-element.65), channel_id=1, source_target_pairs={{0,4},{1,5},{2,6},{3,7},{4,0},{5,1},{6,2},{7,3},{8,12},{9,13},{10,... | collective-permute-start | bytes 442376 | tf_op jit(solution)/shard_map/ppermute | solution.py:21
  238.1 6.6 %collective-permute-done.14 = bf16[288,256]{1,0:T(8,128)(2,1)S(1)} collective-permute-done((bf16[288,256]{1,0:T(8,128)(2,1)S(1)}, bf16[288,256]{1,0:T(8,128)(2,1)S(1)}, u32[]{:S(2)}, u32[]{:S(2)}) %collective-permute-start.14) | collective-permute-done | bytes 147488 | tf_op jit(solution)/shard_map/ppermute | solution.py:21
  (116 shorter events, 31.6 us)
Async XLA Ops:
  7.2 48.0 %all-gather.2.cloned.1.call-start = ((), (), s32[]{:S(2)}) async-start(), calls=%async_computation.4 | async-start | bytes 1179648 | tf_op jit(solution)/shard_map/all_gather | solution.py:215
  7.2 16.4 %collective-permute-start = (bf16[256,256]{1,0:T(8,128)(2,1)}, bf16[256,256]{1,0:T(8,128)(2,1)S(1)}, u32[]{:S(2)}, u32[]{:S(2)}) collective-permute-start(bf16[256,256]{1,0:T(8,128)(2,1)} %refs_0_.1), channel_id=1, source_target_pairs={{0,2},{1,3},{2,4},{3,5},{4,6},{5,7},{6,0},{7,1},{8,10},{9,11},{10,... | collective-permute-start | bytes 393224 | tf_op jit(solution)/shard_map/ppermute | solution.py:21
  10.6 14.5 %collective-permute-start.1 = (bf16[256,256]{1,0:T(8,128)(2,1)}, bf16[256,256]{1,0:T(8,128)(2,1)S(1)}, u32[]{:S(2)}, u32[]{:S(2)}) collective-permute-start(bf16[256,256]{1,0:T(8,128)(2,1)} %refs_0_.1), channel_id=1, source_target_pairs={{0,4},{1,5},{2,6},{3,7},{4,0},{5,1},{6,2},{7,3},{8,12},{9,13},{10,... | collective-permute-start | bytes 393224 | tf_op jit(solution)/shard_map/ppermute | solution.py:21
  15.9 12.4 %collective-permute-start.2 = (bf16[256,256]{1,0:T(8,128)(2,1)}, bf16[256,256]{1,0:T(8,128)(2,1)S(1)}, u32[]{:S(2)}, u32[]{:S(2)}) collective-permute-start(bf16[256,256]{1,0:T(8,128)(2,1)} %refs_0_.1), channel_id=1, source_target_pairs={{0,6},{1,7},{2,0},{3,1},{4,2},{5,3},{6,4},{7,5},{8,14},{9,15},{10,... | collective-permute-start | bytes 393224 | tf_op jit(solution)/shard_map/ppermute | solution.py:21
  20.7 7.6 %copy-start.18 = (bf16[256,256]{1,0:T(8,128)(2,1)S(1)}, bf16[256,256]{1,0:T(8,128)(2,1)}, u32[]{:S(2)}) copy-start(bf16[256,256]{1,0:T(8,128)(2,1)} %refs_0_.1) | copy-start | bytes 393220
  23.5 31.7 %copy-start.25 = (pred[256,768]{1,0:T(32,128)(4,1)}, pred[256,768]{1,0:T(32,128)(4,1)S(1)}, u32[]{:S(2)}) copy-start(pred[256,768]{1,0:T(32,128)(4,1)S(1)} %get-tuple-element.85) | copy-start | bytes 589828
  30.1 29.7 %all-to-all-start = ((bf16[32,24,1024]{2,1,0:T(8,128)(2,1)}), bf16[32,24,1024]{2,1,0:T(8,128)(2,1)S(1)}, u32[]{:S(2)}, u32[]{:S(2)}) async-start(bf16[32,24,1024]{2,1,0:T(8,128)(2,1)} %bitcast.17), calls=%async_computation | async-start | bytes 3145728 | tf_op jit(solution)/shard_map/all_to_all | solution.py:35
  60.9 8.6 %copy-start = (bf16[1,384,2048]{2,1,0:T(8,128)(2,1)S(1)}, bf16[1,384,2048]{2,1,0:T(8,128)(2,1)}, u32[]{:S(2)}) copy-start(bf16[1,384,2048]{2,1,0:T(8,128)(2,1)} %param.10) | copy-start | bytes 4718596
  60.9 8.6 %copy-start.1 = (bf16[1,384,2048]{2,1,0:T(8,128)(2,1)S(1)}, bf16[1,384,2048]{2,1,0:T(8,128)(2,1)}, u32[]{:S(2)}) copy-start(bf16[1,384,2048]{2,1,0:T(8,128)(2,1)} %param.11) | copy-start | bytes 4718596
  60.9 53.8 %all-to-all-start.2 = ((bf16[32,24,2048]{2,1,0:T(8,128)(2,1)}), bf16[32,24,2048]{2,1,0:T(8,128)(2,1)}, u32[]{:S(2)}, u32[]{:S(2)}) async-start(bf16[32,24,2048]{2,1,0:T(8,128)(2,1)} %bitcast.76), calls=%async_computation.2 | async-start | bytes 6291456 | tf_op jit(solution)/shard_map/all_to_all | solution.py:35
  68.1 36.7 %collective-permute-start.3 = (bf16[768,1024]{1,0:T(8,128)(2,1)}, bf16[768,1024]{1,0:T(8,128)(2,1)S(1)}, u32[]{:S(2)}, u32[]{:S(2)}) collective-permute-start(bf16[768,1024]{1,0:T(8,128)(2,1)} %bitcast.69), channel_id=1, source_target_pairs={{0,1},{1,0},{2,3},{3,2},{4,5},{5,4},{6,7},{7,6},{8,9},{9,8},{10,11... | collective-permute-start | bytes 4718600 | tf_op jit(solution)/shard_map/ppermute | solution.py:25
  71.0 33.8 %copy-start.6 = (bf16[1,384,2048]{2,1,0:T(8,128)(2,1)S(1)}, bf16[1,384,2048]{2,1,0:T(8,128)(2,1)}, u32[]{:S(2)}) copy-start(bf16[1,384,2048]{2,1,0:T(8,128)(2,1)} %param.12) | copy-start | bytes 4718596
  114.7 55.4 %all-to-all-start.1 = ((bf16[32,24,2048]{2,1,0:T(8,128)(2,1)}), bf16[32,24,2048]{2,1,0:T(8,128)(2,1)}, u32[]{:S(2)}, u32[]{:S(2)}) async-start(bf16[32,24,2048]{2,1,0:T(8,128)(2,1)} %bitcast.72), calls=%async_computation.1 | async-start | bytes 6291456 | tf_op jit(solution)/shard_map/all_to_all | solution.py:35
  131.6 36.7 %collective-permute-start.11 = (bf16[768,1024]{1,0:T(8,128)(2,1)S(1)}, bf16[768,1024]{1,0:T(8,128)(2,1)S(1)}, u32[]{:S(2)}, u32[]{:S(2)}) collective-permute-start(bf16[768,1024]{1,0:T(8,128)(2,1)S(1)} %get-tuple-element.32), channel_id=1, source_target_pairs={{0,1},{1,0},{2,3},{3,2},{4,5},{5,4},{6,7},{7,6},{8,9},{9,8},{10,11... | collective-permute-start | bytes 4718600 | tf_op jit(solution)/shard_map/ppermute | solution.py:25
  170.1 7.5 %copy-start.4 = (bf16[32,24,1024]{2,1,0:T(8,128)(2,1)S(1)}, bf16[32,24,1024]{2,1,0:T(8,128)(2,1)}, u32[]{:S(2)}) copy-start(bf16[32,24,1024]{2,1,0:T(8,128)(2,1)} %copy-done.2) | copy-start | bytes 4718596
  170.1 42.9 %all-to-all-start.3 = ((bf16[32,24,1024]{2,1,0:T(8,128)(2,1)}), bf16[32,24,1024]{2,1,0:T(8,128)(2,1)S(1)}, u32[]{:S(2)}, u32[]{:S(2)}) async-start(bf16[32,24,1024]{2,1,0:T(8,128)(2,1)} %bitcast.75), calls=%async_computation.3 | async-start | bytes 3145728 | tf_op jit(solution)/shard_map/all_to_all | solution.py:35
  182.2 10.4 %copy-start.16 = (bf16[256,768]{1,0:T(8,128)(2,1)S(1)}, bf16[256,768]{1,0:T(8,128)(2,1)}, u32[]{:S(2)}) copy-start(bf16[256,768]{1,0:T(8,128)(2,1)} %get-tuple-element.59.low_ref) | copy-start | bytes 1179652
  182.2 10.4 %copy-start.17 = (bf16[256,768]{1,0:T(8,128)(2,1)S(1)}, bf16[256,768]{1,0:T(8,128)(2,1)}, u32[]{:S(2)}) copy-start(bf16[256,768]{1,0:T(8,128)(2,1)} %get-tuple-element.60.high_ref) | copy-start | bytes 1179652
  182.2 10.4 %copy-start.21 = (bf16[256,2048]{1,0:T(8,128)(2,1)S(1)}, bf16[256,2048]{1,0:T(8,128)(2,1)}, u32[]{:S(2)}) copy-start(bf16[256,2048]{1,0:T(8,128)(2,1)} %all-gather.2.cloned.1.call-done.grad_ref) | copy-start | bytes 3145732
  192.6 7.3 %copy-start.26 = (pred[256,768]{1,0:T(32,128)(4,1)S(1)}, pred[256,768]{1,0:T(32,128)(4,1)}, u32[]{:S(2)}) copy-start(pred[256,768]{1,0:T(32,128)(4,1)} %copy-done.25) | copy-start | bytes 589828
  192.6 7.3 %copy-start.28 = (s32[256,1]{0,1:T(1,128)S(1)}, s32[256,1]{0,1:T(1,128)}, u32[]{:S(2)}) copy-start(s32[256,1]{0,1:T(1,128)} %copy-done.27) | copy-start | bytes 3076
  201.1 11.9 %collective-permute-start.12 = (f32[8,256]{1,0:T(8,128)S(1)}, f32[8,256]{1,0:T(8,128)S(1)}, u32[]{:S(2)}, u32[]{:S(2)}) collective-permute-start(f32[8,256]{1,0:T(8,128)S(1)} %stack.35), channel_id=1, source_target_pairs={{0,1},{1,0},{2,3},{3,2},{4,5},{5,4},{6,7},{7,6},{8,9},{9,8},{10,11... | collective-permute-start | bytes 24584 | tf_op jit(solution)/shard_map/ppermute | solution.py:25
  203.3 11.2 %collective-permute-start.10 = (bf16[256,256]{1,0:T(8,128)(2,1)}, bf16[256,256]{1,0:T(8,128)(2,1)S(1)}, u32[]{:S(2)}, u32[]{:S(2)}) collective-permute-start(bf16[256,256]{1,0:T(8,128)(2,1)} %get-tuple-element.53), channel_id=1, source_target_pairs={{0,7},{1,0},{2,1},{3,2},{4,3},{5,4},{6,5},{7,6},{8,15},{9,8},{10,9... | collective-permute-start | bytes 393224 | tf_op jit(solution)/shard_map/ppermute | solution.py:21
  206.8 15.1 %collective-permute-start.9 = (bf16[256,256]{1,0:T(8,128)(2,1)}, bf16[256,256]{1,0:T(8,128)(2,1)S(1)}, u32[]{:S(2)}, u32[]{:S(2)}) collective-permute-start(bf16[256,256]{1,0:T(8,128)(2,1)} %get-tuple-element.54), channel_id=1, source_target_pairs={{0,6},{1,7},{2,0},{3,1},{4,2},{5,3},{6,4},{7,5},{8,14},{9,15},{10,... | collective-permute-start | bytes 393224 | tf_op jit(solution)/shard_map/ppermute | solution.py:21
  207.1 24.8 %collective-permute-start.8 = (bf16[256,256]{1,0:T(8,128)(2,1)}, bf16[256,256]{1,0:T(8,128)(2,1)S(1)}, u32[]{:S(2)}, u32[]{:S(2)}) collective-permute-start(bf16[256,256]{1,0:T(8,128)(2,1)} %get-tuple-element.55), channel_id=1, source_target_pairs={{0,5},{1,6},{2,7},{3,0},{4,1},{5,2},{6,3},{7,4},{8,13},{9,14},{10,... | collective-permute-start | bytes 393224 | tf_op jit(solution)/shard_map/ppermute | solution.py:21
  209.4 23.0 %collective-permute-start.7 = (bf16[256,256]{1,0:T(8,128)(2,1)}, bf16[256,256]{1,0:T(8,128)(2,1)S(1)}, u32[]{:S(2)}, u32[]{:S(2)}) collective-permute-start(bf16[256,256]{1,0:T(8,128)(2,1)} %get-tuple-element.56), channel_id=1, source_target_pairs={{0,4},{1,5},{2,6},{3,7},{4,0},{5,1},{6,2},{7,3},{8,12},{9,13},{10,... | collective-permute-start | bytes 393224 | tf_op jit(solution)/shard_map/ppermute | solution.py:21
  213.0 22.7 %collective-permute-start.6 = (bf16[256,256]{1,0:T(8,128)(2,1)}, bf16[256,256]{1,0:T(8,128)(2,1)S(1)}, u32[]{:S(2)}, u32[]{:S(2)}) collective-permute-start(bf16[256,256]{1,0:T(8,128)(2,1)} %get-tuple-element.57), channel_id=1, source_target_pairs={{0,3},{1,4},{2,5},{3,6},{4,7},{5,0},{6,1},{7,2},{8,11},{9,12},{10,... | collective-permute-start | bytes 393224 | tf_op jit(solution)/shard_map/ppermute | solution.py:21
  214.5 21.1 %collective-permute-start.5 = (bf16[256,256]{1,0:T(8,128)(2,1)S(1)}, bf16[256,256]{1,0:T(8,128)(2,1)S(1)}, u32[]{:S(2)}, u32[]{:S(2)}) collective-permute-start(bf16[256,256]{1,0:T(8,128)(2,1)S(1)} %get-tuple-element.58), channel_id=1, source_target_pairs={{0,2},{1,3},{2,4},{3,5},{4,6},{5,7},{6,0},{7,1},{8,10},{9,11},{10,... | collective-permute-start | bytes 393224 | tf_op jit(solution)/shard_map/ppermute | solution.py:21
  221.9 15.2 %collective-permute-start.4 = (bf16[256,256]{1,0:T(8,128)(2,1)S(1)}, bf16[256,256]{1,0:T(8,128)(2,1)S(1)}, u32[]{:S(2)}, u32[]{:S(2)}) collective-permute-start(bf16[256,256]{1,0:T(8,128)(2,1)S(1)} %get-tuple-element.52), channel_id=1, source_target_pairs={{0,1},{1,2},{2,3},{3,4},{4,5},{5,6},{6,7},{7,0},{8,9},{9,10},{10,1... | collective-permute-start | bytes 393224 | tf_op jit(solution)/shard_map/ppermute | solution.py:21
  231.9 6.1 %collective-permute-start.15 = (bf16[288,256]{1,0:T(8,128)(2,1)S(1)}, bf16[288,256]{1,0:T(8,128)(2,1)S(1)}, u32[]{:S(2)}, u32[]{:S(2)}) collective-permute-start(bf16[288,256]{1,0:T(8,128)(2,1)S(1)} %get-tuple-element.66), channel_id=1, source_target_pairs={{0,6},{1,7},{2,0},{3,1},{4,2},{5,3},{6,4},{7,5},{8,14},{9,15},{10,... | collective-permute-start | bytes 442376 | tf_op jit(solution)/shard_map/ppermute | solution.py:21
  232.4 12.4 %collective-permute-start.14 = (bf16[288,256]{1,0:T(8,128)(2,1)S(1)}, bf16[288,256]{1,0:T(8,128)(2,1)S(1)}, u32[]{:S(2)}, u32[]{:S(2)}) collective-permute-start(bf16[288,256]{1,0:T(8,128)(2,1)S(1)} %get-tuple-element.65), channel_id=1, source_target_pairs={{0,4},{1,5},{2,6},{3,7},{4,0},{5,1},{6,2},{7,3},{8,12},{9,13},{10,... | collective-permute-start | bytes 442376 | tf_op jit(solution)/shard_map/ppermute | solution.py:21
  235.6 10.6 %collective-permute-start.13 = (bf16[288,256]{1,0:T(8,128)(2,1)S(1)}, bf16[288,256]{1,0:T(8,128)(2,1)S(1)}, u32[]{:S(2)}, u32[]{:S(2)}) collective-permute-start(bf16[288,256]{1,0:T(8,128)(2,1)S(1)} %get-tuple-element.64), channel_id=1, source_target_pairs={{0,2},{1,3},{2,4},{3,5},{4,6},{5,7},{6,0},{7,1},{8,10},{9,11},{10,... | collective-permute-start | bytes 442376 | tf_op jit(solution)/shard_map/ppermute | solution.py:21
  (26 other events, 76.7 us)
Sparse Core Ops, SparseCore 0:
  18.8 36.3 all-gather.1
where the time goes:
time: 258 us; the launch traced here: 254 us
  waiting for transfers between devices  110 us (43%)
  starting transfers between devices  62.3 us (24%)
  Pallas kernels  35 us (14%)
  local copies, waits for them, and re-layouts  19.8 us (8%)
  between operations  14.5 us (6%)
  matrix products  6.61 us (3%)
  other arithmetic  6.16 us (2%)
    ppermute x3, waiting for transfers between devices, swap(): return lax.ppermute(value, 'etp', [(i, i ^ 1) for i in range(lanes)])  63.4 us
    pallas_call x8, Pallas kernels, call(): pl.pallas_call(body, grid_spec=pltpu.PrefetchScalarGridSpec(num_scalar_pr...  35 us
    all_to_all x4, starting transfers between devices, across(): lax.all_to_all(cut, 'expert', split_axis=0, concat_axis=0, tiled=True)  29.7 us
    ppermute x13, waiting for transfers between devices, shift(): lax.ppermute(value, 'etp', [(i, (i + step) % lanes) for i in range(lanes)])  28.6 us
    ppermute x13, starting transfers between devices, shift(): lax.ppermute(value, 'etp', [(i, (i + step) % lanes) for i in range(lanes)])  28.1 us
    all_gather x1, waiting for transfers between devices, per_device(): grad_full = lax.all_gather(grad_out, 'etp', axis=1, tiled=True)  17.4 us
    unnamed x74, local copies, waits for them, and re-layouts  16.9 us
    dot_general x2, matrix products, dot(): return lax.dot_general(a, b, (dims, ((), ())), preferred_element_type=F32)  6.61 us
  transfers between devices with their start and end apart: 21, of which 12 were waited for; matrix products, arithmetic and copies ran while one was open for 6% of the time, Pallas kernels for 14%

commit v1 on v0

v1 whole, which is shorter than its diff:
```python
import functools

import jax
import jax.numpy as jnp
from jax import lax
from jax.experimental import pallas as pl
from jax.experimental.pallas import tpu as pltpu
from jax.sharding import PartitionSpec as P

EXP_DEV = 4
ROW_CUTS = 3
SWAP_CUTS = 2
VMEM_BYTES = 63 * 1024 * 1024
F32 = jnp.float32
BF16 = jnp.bfloat16
LAST = ((1,), (1,))
FLAT = ((1,), (0,))
TALL = ((0,), (0,))


def shift(value, step, lanes):
    return lax.ppermute(value, "etp", [(i, (i + step) % lanes) for i in range(lanes)])


def swap(value, lanes):
    return lax.ppermute(value, "etp", [(i, i ^ 1) for i in range(lanes)])


def dot(a, b, dims):
    return lax.dot_general(a, b, (dims, ((), ())), preferred_element_type=F32)


def across(rows, groups):
    slots, width = rows.shape
    cut = rows.reshape(groups, slots // groups, width)
    moved = lax.all_to_all(cut, "expert", split_axis=0, concat_axis=0, tiled=True)
    return moved.reshape(slots, width)


def call(body, scalars, grid, operands, in_blocks, outs, out_blocks, flops, aliases=None):
    def spec(block):
        return block[0] if len(block) == 1 else pl.BlockSpec(*block)

    return pl.pallas_call(
        body,
        grid_spec=pltpu.PrefetchScalarGridSpec(
            num_scalar_prefetch=1,
            grid=grid,
            in_specs=[spec(b) for b in in_blocks],
            out_specs=[spec(b) for b in out_blocks],
        ),
        out_shape=list(outs),
        input_output_aliases=aliases or {},
        compiler_params=pltpu.CompilerParams(vmem_limit_bytes=VMEM_BYTES),
        cost_estimate=pl.CostEstimate(flops=1, bytes_accessed=1, transcendentals=0),
    )(scalars, *operands)


def whole(array):
    return (array.shape, lambda i, s: (0,) * array.ndim)


def columns(parity_of, matrix, shard, halves=2):
    rows = matrix.shape[0]
    blocks = [
        ((rows, shard), lambda i, s, j=j: (0, halves * j + parity_of(s))) for j in range(EXP_DEV)
    ]
    return [matrix] * EXP_DEV, blocks


def mine_of(s):
    return lax.rem(s[0], 2)


def other_of(s):
    return 1 - lax.rem(s[0], 2)


def contract(rows_ref, w_refs):
    shard = w_refs[0].shape[1]
    parts = [
        dot(rows_ref[:, j * shard : (j + 1) * shard], w_ref[...], LAST)
        for j, w_ref in enumerate(w_refs)
    ]
    return sum(parts[1:], parts[0])


def gather_body(shard, s_ref, select_ref, *refs):
    out_ref = refs[-1]
    local_expert = s_ref[0] // 2
    select = select_ref[...]
    for r, ref in enumerate(refs[:-1]):
        start = pl.multiple_of(lax.rem(local_expert - r + EXP_DEV, EXP_DEV) * shard, shard)
        out_ref[:, pl.ds(start, shard)] = dot(select, ref[...], TALL).astype(BF16)


def scaled_body(s_ref, select_ref, grad_ref, weight_ref, out_ref):
    out_ref[...] = (dot(select_ref[...], grad_ref[...], TALL) * weight_ref[...]).astype(BF16)


def first_body(s_ref, rows_ref, *refs):
    gate_out, up_out = refs[-2:]
    gate_out[...] = contract(rows_ref, refs[:EXP_DEV])
    up_out[...] = contract(rows_ref, refs[EXP_DEV:-2])


def second_body(s_ref, rows_ref, gate_in, up_in, down_ref, *refs):
    hidden_out, gate_slope, up_slope, part_out = refs[-4:]
    gate_act = gate_in[...] + contract(rows_ref, refs[:EXP_DEV])
    up_act = up_in[...] + contract(rows_ref, refs[EXP_DEV:-4])
    sig = jax.nn.sigmoid(gate_act)
    gated = gate_act * sig
    hidden = (gated * up_act).astype(BF16)
    hidden_out[...] = hidden
    up_slope[...] = gated
    gate_slope[...] = up_act * sig * (1.0 + gate_act * (1.0 - sig))
    part_out[...] = dot(hidden, down_ref[...], FLAT).astype(BF16)


def third_body(s_ref, grad_ref, gate_slope, up_slope, down_ref, *refs):
    gate_out, up_out, other_out = refs[-3:]
    grad_hidden = dot(grad_ref[...], down_ref[...], LAST)
    grad_gate = (grad_hidden * gate_slope[...]).astype(BF16)
    grad_up = (grad_hidden * up_slope[...]).astype(BF16)
    gate_out[...] = grad_gate
    up_out[...] = grad_up
    shard = refs[0].shape[1]
    for j in range(EXP_DEV):
        other_out[:, j * shard : (j + 1) * shard] = (
            dot(grad_gate, refs[j][...], FLAT) + dot(grad_up, refs[EXP_DEV + j][...], FLAT)
        ).astype(BF16)


def fourth_body(s_ref, grad_gate, grad_up, swapped, *refs):
    out_ref = refs[-1]
    shard = refs[0].shape[1]
    for j in range(EXP_DEV):
        here = slice(j * shard, (j + 1) * shard)
        out_ref[:, here] = (
            dot(grad_gate[...], refs[j][...], FLAT)
            + dot(grad_up[...], refs[EXP_DEV + j][...], FLAT)
            + swapped[:, here].astype(F32)
        ).astype(BF16)


def weights_body(s_ref, *refs):
    hidden, other_ref, mine_ref, grad_ref, gate_out, up_out, down_out = refs[-7:]
    cuts = (len(refs) - 7) // 2
    grad_gate, grad_up = refs[:cuts], refs[cuts : 2 * cuts]
    size = grad_gate[0].shape[0]

    def total(lefts, ref):
        parts = [
            dot(left[...], ref[k * size : (k + 1) * size, :], TALL)
            for k, left in enumerate(lefts)
        ]
        return sum(parts[1:], parts[0]).astype(BF16)

    down_out[0] = dot(hidden[...], grad_ref[...], TALL).astype(BF16)
    here = lax.rem(pl.program_id(0), 2) == lax.rem(s_ref[0], 2)

    @pl.when(here)
    def _():
        gate_out[0] = total(grad_gate, mine_ref)
        up_out[0] = total(grad_up, mine_ref)

    @pl.when(jnp.logical_not(here))
    def _():
        gate_out[0] = total(grad_gate, other_ref)
        up_out[0] = total(grad_up, other_ref)


def mix_body(s_ref, weight_ref, rows_ref, out_ref):
    both = dot(weight_ref[...], rows_ref[...], FLAT)
    tok_count = both.shape[0] // 2
    out_ref[...] = both[:tok_count] + both[tok_count:]


def route_body(s_ref, rows_ref, grad_ref, picked_ref, ids_ref, expert_ref, route_out):
    products = dot(rows_ref[...], grad_ref[...], LAST) * picked_ref[...].astype(F32)
    experts = expert_ref[...]
    for k in range(route_out.shape[0]):
        chosen = jnp.where(ids_ref[k : k + 1, :] == experts, products, 0.0)
        route_out[k : k + 1, :] = jnp.sum(chosen, axis=0, keepdims=True)


def spread_body(s_ref, select_ref, rows_ref, mine_out, piece_out):
    count, tok_count, shard = piece_out.shape
    select = select_ref[...]
    for r in range(count):
        start = pl.multiple_of(lax.rem(s_ref[0] // 2 + r, count) * shard, shard)
        part = dot(select, rows_ref[:, pl.ds(start, shard)], FLAT)
        if r == 0:
            mine_out[...] = part
        piece_out[r] = part.astype(BF16)


def per_device(tokens, expert_ids, route_weights, gate_weight, up_weight, down_weight, grad_out):
    tok_count, top_count = expert_ids.shape
    units, model_width = gate_weight.shape[1:]
    shard = tokens.shape[1]
    groups = lax.axis_size("expert")
    lanes = lax.axis_size("etp")
    halves = lanes // EXP_DEV
    experts = EXP_DEV * groups
    capacity = max(2, tok_count * top_count * 3 // (2 * experts))
    slots = groups * capacity
    half = model_width // halves
    lane = lax.axis_index("etp")
    local_expert = lane // halves
    scalars = lane.astype(jnp.int32).reshape(1)
    w_gate = gate_weight[0]
    w_up = up_weight[0]
    w_down = down_weight[0]
    block = slots // ROW_CUTS
    unit_flops = 2 * slots * units * half

    def shape(rows, width, kind=BF16):
        return jax.ShapeDtypeStruct((rows, width), kind)

    def row_block(width, k=None):
        return ((block, width), lambda i, s: (i if k is None else k, 0))

    grad_full = lax.all_gather(grad_out, "etp", axis=1, tiled=True)
    own = [tokens] + [shift(tokens, halves * r, lanes) for r in range(1, EXP_DEV)]

    column = lax.broadcasted_iota(jnp.int32, (1, slots), 1)
    col_expert = column // capacity * EXP_DEV + local_expert
    col_slot = (column % capacity).astype(F32)
    hits = [expert_ids[:, k : k + 1] == col_expert for k in range(top_count)]
    member = hits[0]
    for hit in hits[1:]:
        member = member | hit
    member = member.astype(BF16)
    row = lax.broadcasted_iota(jnp.int32, (tok_count, tok_count), 0)
    earlier = (lax.broadcasted_iota(jnp.int32, (tok_count, tok_count), 1) < row).astype(BF16)
    rank = dot(earlier, member, FLAT)
    chosen = (member > 0) & (rank == col_slot)
    select = chosen.astype(BF16)
    weight = jnp.zeros((tok_count, slots), F32)
    for k in range(top_count):
        weight = jnp.where(hits[k], route_weights[:, k : k + 1], weight)
    weight = jnp.where(chosen, weight, 0.0)
    slot_weight = jnp.sum(weight, axis=0)[:, None]
    weight_high = lax.reduce_precision(weight, 8, 7)
    weight_low = (weight - weight_high).astype(BF16)
    weight_high = weight_high.astype(BF16)

    (sent,) = call(
        functools.partial(gather_body, shard), scalars, (1,),
        [select, *own], [whole(select)] + [whole(x) for x in own],
        [shape(slots, half)], [((slots, half), lambda i, s: (0, 0))],
        2 * slots * tok_count * half,
    )
    rows_mine = across(sent, groups)
    rows_other = swap(rows_mine, lanes)

    (scaled,) = call(
        scaled_body, scalars, (ROW_CUTS,),
        [select, grad_full, slot_weight],
        [((tok_count, block), lambda i, s: (0, i)), whole(grad_full), row_block(1)],
        [shape(slots, model_width)], [row_block(model_width)],
        2 * slots * tok_count * model_width,
    )
    grad_rows = across(scaled, groups)

    f32_rows = shape(slots, units, F32)
    unit_block = row_block(units)
    gate_mine, mine_blocks = columns(mine_of, w_gate, shard)
    gate_other, other_blocks = columns(other_of, w_gate, shard)
    weights_mine = gate_mine + [w_up] * EXP_DEV
    weights_other = gate_other + [w_up] * EXP_DEV
    mine_blocks, other_blocks = mine_blocks * 2, other_blocks * 2
    gate_first, up_first = call(
        first_body, scalars, (ROW_CUTS,),
        [rows_mine, *weights_mine], [row_block(half)] + mine_blocks,
        [f32_rows, f32_rows], [unit_block, unit_block], 2 * unit_flops,
    )
    hidden, gate_slope, up_slope, expert_part = call(
        second_body, scalars, (ROW_CUTS,),
        [rows_other, gate_first, up_first, w_down, *weights_other],
        [row_block(half), unit_block, unit_block, whole(w_down)] + other_blocks,
        [shape(slots, units), f32_rows, f32_rows, shape(slots, model_width)],
        [unit_block, unit_block, unit_block, row_block(model_width)], 4 * unit_flops,
    )

    size = slots // SWAP_CUTS
    cut_units = shape(size, units)
    cut_half = shape(size, half)

    def cut_block(width, k):
        return ((size, width), lambda i, s: (k, 0))

    grad_gate_act, grad_up_act, swapped = [], [], []
    for k in range(SWAP_CUTS):
        got = call(
            third_body, scalars, (1,),
            [grad_rows, gate_slope, up_slope, w_down, *weights_other],
            [cut_block(model_width, k), cut_block(units, k), cut_block(units, k)]
            + [whole(w_down)] + other_blocks,
            [cut_units, cut_units, cut_half],
            [whole(cut_units), whole(cut_units), whole(cut_half)],
            4 * unit_flops // SWAP_CUTS,
        )
        grad_gate_act.append(got[0])
        grad_up_act.append(got[1])
        if k == 0:
            expert_part, first = lax.optimization_barrier((expert_part, got[2]))
            swapped.append(swap(first, lanes))
        else:
            swapped.append(swap(got[2], lanes))
    returned = across(expert_part, groups)

    pair_block = ((slots, shard), lambda i, s: (0, i // 2))
    grad_shape = jax.ShapeDtypeStruct((1, units, model_width), BF16)
    grad_block = ((1, units, shard), lambda i, s: (0, 0, i))
    grad_gate, grad_up, grad_down = call(
        weights_body, scalars, (lanes,),
        [*grad_gate_act, *grad_up_act, hidden, rows_other, rows_mine, grad_rows],
        [whole(cut_units)] * (2 * SWAP_CUTS) + [whole(hidden)]
        + [pair_block, pair_block, ((slots, shard), lambda i, s: (0, i))],
        [grad_shape] * 3, [grad_block] * 3, 6 * unit_flops,
    )

    input_half = []
    for k in range(SWAP_CUTS):
        operands = [grad_gate_act[k], grad_up_act[k], swapped[k], *weights_mine]
        blocks = [whole(cut_units), whole(cut_units), whole(cut_half)] + mine_blocks
        outs, out_blocks, aliases = shape(slots, half), cut_block(half, k), None
        if k > 0:
            aliases = {len(operands) + 1: 0}
            operands.append(input_half)
            blocks.append((pl.BlockSpec(memory_space=pl.ANY),))
        (input_half,) = call(
            fourth_body, scalars, (1,), operands, blocks,
            [outs], [out_blocks], 2 * unit_flops // SWAP_CUTS, aliases,
        )
    input_half, returned, grad_gate, grad_up, grad_down = lax.optimization_barrier(
        (input_half, returned, grad_gate, grad_up, grad_down)
    )
    grad_back = across(input_half, groups)

    both_weights = jnp.concatenate([weight_high, weight_low], axis=0)
    picked = select.T
    ids = expert_ids.T
    row_expert = col_expert.reshape(slots, 1)
    (mixed_part,) = call(
        mix_body, scalars, (2,), [both_weights, returned],
        [whole(both_weights), ((slots, half), lambda i, s: (0, i))],
        [shape(tok_count, model_width, F32)], [((tok_count, half), lambda i, s: (0, i))],
        4 * tok_count * slots * model_width,
    )
    mixed = lax.psum_scatter(mixed_part, "etp", scatter_dimension=1, tiled=True).astype(BF16)
    route_operands = [returned, grad_full, picked, ids, row_expert]
    (route_sum,) = call(
        route_body, scalars, (1,), route_operands, [whole(x) for x in route_operands],
        [shape(top_count, tok_count, F32)], [whole(ids)],
        2 * tok_count * slots * model_width,
    )
    route_sum = route_sum + swap(route_sum, lanes)
    route_1 = lax.reduce_precision(route_sum, 8, 7)
    rest = route_sum - route_1
    route_2 = lax.reduce_precision(rest, 8, 7)
    route_3 = rest - route_2
    route_pack = jnp.concatenate([route_1, route_2, route_3], axis=0).astype(BF16)
    pack_rows = -(-3 * top_count // 16) * 16
    route_pack = jnp.pad(
        route_pack, ((0, pack_rows - 3 * top_count), (0, shard - tok_count))
    )

    spread_outs = [
        shape(tok_count, shard, F32),
        jax.ShapeDtypeStruct((EXP_DEV, tok_count, shard), BF16),
    ]
    grad_tokens, token_pieces = call(
        spread_body, scalars, (1,), [select, grad_back], [whole(select), whole(grad_back)],
        spread_outs, [whole(x) for x in spread_outs], 2 * tok_count * slots * half,
    )
    pieces = [
        shift(jnp.concatenate([token_pieces[r], route_pack], axis=0), halves * r, lanes)
        for r in range(1, EXP_DEV)
    ]
    for piece in pieces:
        piece = piece.astype(F32)
        grad_tokens = grad_tokens + piece[:tok_count]
        got = piece[tok_count:, :tok_count]
        route_sum = route_sum + (
            got[:top_count] + got[top_count : 2 * top_count] + got[2 * top_count : 3 * top_count]
        )
    grad_tokens = grad_tokens.astype(BF16)
    grad_route = route_sum.T
    return (mixed, grad_tokens, grad_route, grad_gate, grad_up, grad_down)


def solution(mesh):
    placed = (
        P("expert", "etp"),
        P("expert", None),
        P("expert", None),
        P(("expert", "etp"), None, None),
        P(("expert", "etp"), None, None),
        P(("expert", "etp"), None, None),
        P("expert", "etp"),
    )
    return jax.shard_map(
        per_device,
        mesh=mesh,
        in_specs=placed,
        out_specs=(
            P("expert", "etp"),
            P("expert", "etp"),
            P("expert", None),
            P(("expert", "etp"), None, None),
            P(("expert", "etp"), None, None),
            P(("expert", "etp"), None, None),
        ),
        check_vma=False,
    )
```

time: 258 us -> 237 us (0.919)
  Pallas kernels: 35 us -> 62.9 us
  waiting for transfers between devices: 110 us -> 89 us
  local copies, waits for them, and re-layouts: 19.8 us -> 7.75 us
  starting transfers between devices: 62.3 us -> 50.9 us
  matrix products: 6.61 us -> 2.65 us
    pallas_call x8 -> x12, Pallas kernels: 35 us -> 62.9 us  [call(): pl.pallas_call(body, grid_spec=pltpu.PrefetchScalarGridSpec(num_scalar_pr...]
    ppermute x3 -> x4, waiting for transfers between devices: 63.4 us -> 45.4 us  [swap(): return lax.ppermute(value, 'etp', [(i, i ^ 1) for i in range(lanes)])]
    unnamed x74 -> x46, local copies, waits for them, and re-layouts: 16.9 us -> 1.64 us
    ppermute x13 -> x6, waiting for transfers between devices: 28.6 us -> 16.6 us  [shift(): lax.ppermute(value, 'etp', [(i, (i + step) % lanes) for i in range(lanes)])]
    all_to_all x4, waiting for transfers between devices: 0.67 us -> 12.3 us  [across(): lax.all_to_all(cut, 'expert', split_axis=0, concat_axis=0, tiled=True)]
    ppermute x13 -> x6, starting transfers between devices: 28.1 us -> 18.7 us  [shift(): lax.ppermute(value, 'etp', [(i, (i + step) % lanes) for i in range(lanes)])]
    dot_general x2 -> x1, matrix products: 6.61 us -> 2.65 us  [dot(): return lax.dot_general(a, b, (dims, ((), ())), preferred_element_type=F32)]
    all_gather x1, waiting for transfers between devices: 17.4 us -> 14.7 us  [per_device(): grad_full = lax.all_gather(grad_out, 'etp', axis=1, tiled=True)]
  transfers between devices with their start and end apart: 21 -> 16, of which waited for: 12 -> 9; matrix products, arithmetic and copies ran while one was open for 6% -> 7% of each run, Pallas kernels for 14% -> 22%
where the time goes in v1:
time: 237 us; the launch traced here: 236 us
  waiting for transfers between devices  89 us (38%)
  Pallas kernels  62.9 us (27%)
  starting transfers between devices  50.9 us (21%)
  between operations  14.4 us (6%)
  other arithmetic  8.24 us (3%)
  local copies, waits for them, and re-layouts  7.75 us (3%)
  matrix products  2.65 us (1%)
    pallas_call x12, Pallas kernels, call(): pl.pallas_call(body, grid_spec=pltpu.PrefetchScalarGridSpec(num_scalar_pr...  62.9 us
    ppermute x4, waiting for transfers between devices, swap(): return lax.ppermute(value, 'etp', [(i, i ^ 1) for i in range(lanes)])  45.4 us
    all_to_all x4, starting transfers between devices, across(): lax.all_to_all(cut, 'expert', split_axis=0, concat_axis=0, tiled=True)  29.2 us
    ppermute x6, starting transfers between devices, shift(): lax.ppermute(value, 'etp', [(i, (i + step) % lanes) for i in range(lanes)])  18.7 us
    ppermute x6, waiting for transfers between devices, shift(): lax.ppermute(value, 'etp', [(i, (i + step) % lanes) for i in range(lanes)])  16.6 us
    all_gather x1, waiting for transfers between devices, per_device(): grad_full = lax.all_gather(grad_out, 'etp', axis=1, tiled=True)  14.7 us
    all_to_all x4, waiting for transfers between devices, across(): lax.all_to_all(cut, 'expert', split_axis=0, concat_axis=0, tiled=True)  12.3 us
  transfers between devices with their start and end apart: 16, of which 9 were waited for; matrix products, arithmetic and copies ran while one was open for 7% of the time, Pallas kernels for 22%

profile of v1, /device:TPU:2, one launch (start us, length us, event | category | flops | bytes accessed | tf_op | source)
XLA Modules:
  0.0 235.9 jit_solution(4450178607413088156)
XLA Ops:
  7.2 3.3 %collective-permute-start = (bf16[256,256]{1,0:T(8,128)(2,1)}, bf16[256,256]{1,0:T(8,128)(2,1)S(1)}, u32[]{:S(2)}, u32[]{:S(2)}) collective-permute-start(bf16[256,256]{1,0:T(8,128)(2,1)} %refs_0_.1), channel_id=1, source_target_pairs={{0,2},{1,3},{2,4},{3,5},{4,6},{5,7},{6,0},{7,1},{8,10},{9,11},{10,... | collective-permute-start | bytes 393224 | tf_op jit(solution)/shard_map/ppermute | solution.py:22
  10.6 5.4 %collective-permute-start.1 = (bf16[256,256]{1,0:T(8,128)(2,1)}, bf16[256,256]{1,0:T(8,128)(2,1)S(1)}, u32[]{:S(2)}, u32[]{:S(2)}) collective-permute-start(bf16[256,256]{1,0:T(8,128)(2,1)} %refs_0_.1), channel_id=1, source_target_pairs={{0,4},{1,5},{2,6},{3,7},{4,0},{5,1},{6,2},{7,3},{8,12},{9,13},{10,... | collective-permute-start | bytes 393224 | tf_op jit(solution)/shard_map/ppermute | solution.py:22
  15.9 2.7 %collective-permute-start.2 = (bf16[256,256]{1,0:T(8,128)(2,1)}, bf16[256,256]{1,0:T(8,128)(2,1)S(1)}, u32[]{:S(2)}, u32[]{:S(2)}) collective-permute-start(bf16[256,256]{1,0:T(8,128)(2,1)} %refs_0_.1), channel_id=1, source_target_pairs={{0,6},{1,7},{2,0},{3,1},{4,2},{5,3},{6,4},{7,5},{8,14},{9,15},{10,... | collective-permute-start | bytes 393224 | tf_op jit(solution)/shard_map/ppermute | solution.py:22
  20.8 2.6 %fusion.30 = (f32[768]{0:T(1024)S(1)}, f32[256,768]{0,1:T(8,128)}, pred[256,768]{0,1:T(8,128)(4,1)S(1)}) fusion(f32[256]{0:T(256)S(1)} %bitcast.126, f32[256]{0:T(256)S(1)} %bitcast.127, f32[256]{0:T(256)S(1)} %bitcast.121, f32[256]{0:T(256)S(1)} %bitcast.122, f32[256]{0:T(256)S(1)} %bitcast.123, f32[256]{0:T(256)S(1)} %bitcast.124, f32[256]{0:T(256)S(1)} %bitcast.125, ...), kind=kOutput, calls=%fused_computation.81 | convolution fusion | flops 109772032 | bytes 1008640 | tf_op jit(solution)/shard_map/dot_general | solution.py:30
  25.3 3.1 %collective-permute-done.2.refs_3_ = bf16[256,256]{1,0:T(8,128)(2,1)S(1)} collective-permute-done((bf16[256,256]{1,0:T(8,128)(2,1)}, bf16[256,256]{1,0:T(8,128)(2,1)S(1)}, u32[]{:S(2)}, u32[]{:S(2)}) %collective-permute-start.2) | collective-permute-done | bytes 131104 | tf_op jit(solution)/shard_map/ppermute | solution.py:22
  29.0 2.9 %shard_map.119 = bf16[768,1024]{1,0:T(8,128)(2,1)} custom-call(s32[1]{0:T(128)} %bitcast.s_ref, bf16[256,768]{1,0:T(8,128)(2,1)} %copy.20.select_ref, bf16[256,256]{1,0:T(8,128)(2,1)} %refs_0_.1, bf16[256,256]{1,0:T(8,128)(2,1)} %copy-done.2, bf16[256,256]{1,0:T(8,128)(2,1)} %copy-done.3, bf16[256,256]{1,0:T(8,128)(2,1)} %copy-done.4), custom_call_target="tpu_custom_call" | custom-call | flops 1 | bytes 1 | tf_op jit(solution)/shard_map/pallas_call | solution.py:44
  31.9 7.7 %all-to-all-start.1 = ((bf16[32,24,1024]{2,1,0:T(8,128)(2,1)}), bf16[32,24,1024]{2,1,0:T(8,128)(2,1)}, u32[]{:S(2)}, u32[]{:S(2)}) async-start(bf16[32,24,1024]{2,1,0:T(8,128)(2,1)} %bitcast.93), calls=%async_computation.1 | async-start | bytes 3145728 | tf_op jit(solution)/shard_map/all_to_all | solution.py:36
  40.5 14.7 %all-gather.2.cloned.1.call-done.grad_ref = bf16[256,2048]{1,0:T(8,128)(2,1)} async-done(((bf16[256,256]{1,0:T(8,128)(2,1)}), bf16[256,2048]{1,0:T(8,128)(2,1)}) %all-gather.2.cloned.1.call-update) | async-done | bytes 1048592 | tf_op jit(solution)/shard_map/all_gather | solution.py:224
  55.3 4.6 %shard_map.118 = bf16[768,2048]{1,0:T(8,128)(2,1)} custom-call(s32[1]{0:T(128)} %bitcast.s_ref, bf16[256,768]{1,0:T(8,128)(2,1)} %copy.20.select_ref, bf16[256,2048]{1,0:T(8,128)(2,1)} %all-gather.2.cloned.1.call-done.grad_ref, f32[768,1]{1,0:T(8,128)} %broadcast_in_dim.85.weight_ref), custom_call_target="tpu_custom_call" | custom-call | flops 1 | bytes 1 | tf_op jit(solution)/shard_map/pallas_call | solution.py:44
  59.8 1.9 all-to-all-done.1
  61.7 6.5 %all-to-all-start = ((bf16[32,24,2048]{2,1,0:T(8,128)(2,1)}), bf16[32,24,2048]{2,1,0:T(8,128)(2,1)}, u32[]{:S(2)}, u32[]{:S(2)}) async-start(bf16[32,24,2048]{2,1,0:T(8,128)(2,1)} %bitcast.92), calls=%async_computation | async-start | bytes 6291456 | tf_op jit(solution)/shard_map/all_to_all | solution.py:36
  68.8 4.9 %shard_map.120 = (f32[768,384]{1,0:T(8,128)}, f32[768,384]{1,0:T(8,128)}) custom-call(s32[1]{0:T(128)} %bitcast.s_ref, bf16[768,1024]{1,0:T(8,128)(2,1)} %bitcast.20.rows_ref.refs_6_, bf16[384,2048]{1,0:T(8,128)(2,1)} %bitcast.41, bf16[384,2048]{1,0:T(8,128)(2,1)} %bitcast.42, bf16[384,2048]{1,0:T(8,128)(2,1)} %bitcast.43, bf16[384,2048]{1,0:T(8,128)(2,1)} %bitcast.44, ...), custom_call_target="tpu_custom_call" | custom-call | flops 1 | bytes 1 | tf_op jit(solution)/shard_map/pallas_call | solution.py:44
  73.7 31.4 %collective-permute-done.3.rows_ref.refs_5_ = bf16[768,1024]{1,0:T(8,128)(2,1)} collective-permute-done((bf16[768,1024]{1,0:T(8,128)(2,1)}, bf16[768,1024]{1,0:T(8,128)(2,1)}, u32[]{:S(2)}, u32[]{:S(2)}) %collective-permute-start.3) | collective-permute-done | bytes 1572896 | tf_op jit(solution)/shard_map/ppermute | solution.py:26
  105.1 7.8 %shard_map.121 = (bf16[768,384]{1,0:T(8,128)(2,1)}, f32[768,384]{1,0:T(8,128)}, f32[768,384]{1,0:T(8,128)}, bf16[768,2048]{1,0:T(8,128)(2,1)}) custom-call(s32[1]{0:T(128)} %bitcast.s_ref, bf16[768,1024]{1,0:T(8,128)(2,1)} %collective-permute-done.3.rows_ref.refs_5_, f32[768,384]{1,0:T(8,128)} %get-tuple-element.30.gate_in, ...), custom_call_target="tpu_custom_call" | custom-call | flops 1 | bytes 1 | tf_op jit(solution)/shard_map/pallas_call | solution.py:44
  113.0 5.5 %shard_map.123 = (bf16[384,384]{1,0:T(8,128)(2,1)}, bf16[384,384]{1,0:T(8,128)(2,1)}, bf16[384,1024]{1,0:T(8,128)(2,1)}) custom-call(s32[1]{0:T(128)} %bitcast.s_ref, bf16[768,2048]{1,0:T(8,128)(2,1)} %bitcast.18.grad_ref.refs_7_, f32[768,384]{1,0:T(8,128)} %get-tuple-element.32.gate_slope, f32[768,384]{1,0:T(8,128)} %get-tuple-element.33.up_slope, ...), custom_call_target="tpu_custom_call" | custom-call | flops 1 | bytes 1 | tf_op jit(solution)/shard_map/pallas_call | solution.py:44
  118.4 7.5 %all-to-all-start.2 = ((bf16[32,24,2048]{2,1,0:T(8,128)(2,1)}), bf16[32,24,2048]{2,1,0:T(8,128)(2,1)}, u32[]{:S(2)}, u32[]{:S(2)}) async-start(bf16[32,24,2048]{2,1,0:T(8,128)(2,1)} %bitcast.94), calls=%async_computation.2 | async-start | bytes 6291456 | tf_op jit(solution)/shard_map/all_to_all | solution.py:36
  126.6 5.5 %shard_map.122 = (bf16[384,384]{1,0:T(8,128)(2,1)}, bf16[384,384]{1,0:T(8,128)(2,1)}, bf16[384,1024]{1,0:T(8,128)(2,1)}) custom-call(s32[1]{0:T(128)} %bitcast.s_ref, bf16[768,2048]{1,0:T(8,128)(2,1)} %bitcast.18.grad_ref.refs_7_, f32[768,384]{1,0:T(8,128)} %get-tuple-element.32.gate_slope, f32[768,384]{1,0:T(8,128)} %get-tuple-element.33.up_slope, ...), custom_call_target="tpu_custom_call" | custom-call | flops 1 | bytes 1 | tf_op jit(solution)/shard_map/pallas_call | solution.py:44
  132.1 1.7 collective-permute-start.4
  136.3 12.0 %shard_map.126 = (bf16[1,384,2048]{2,1,0:T(8,128)(2,1)}, bf16[1,384,2048]{2,1,0:T(8,128)(2,1)}, bf16[1,384,2048]{2,1,0:T(8,128)(2,1)}) custom-call(s32[1]{0:T(128)} %bitcast.s_ref, bf16[384,384]{1,0:T(8,128)(2,1)} %get-tuple-element.37.grad_gate.refs_0_, bf16[384,384]{1,0:T(8,128)(2,1)} %get-tuple-element.34.grad_gate.refs_1_, ...), custom_call_target="tpu_custom_call" | custom-call | flops 1 | bytes 1 | tf_op jit(solution)/shard_map/pallas_call | solution.py:44
  149.1 3.7 %shard_map.124.refs_8_ = bf16[768,1024]{1,0:T(8,128)(2,1)} custom-call(s32[1]{0:T(128)} %bitcast.s_ref, bf16[384,384]{1,0:T(8,128)(2,1)} %get-tuple-element.37.grad_gate.refs_0_, bf16[384,384]{1,0:T(8,128)(2,1)} %get-tuple-element.38.grad_up.refs_2_, bf16[384,1024]{1,0:T(8,128)(2,1)} %copy-done, bf16[384,2048]{1,0:T(8,128)(2,1)} %bitcast.57, ...), custom_call_target="tpu_custom_call" | custom-call | flops 1 | bytes 1 | tf_op jit(solution)/shard_map/pallas_call | solution.py:44
  152.9 10.2 %collective-permute-done.4.swapped = bf16[384,1024]{1,0:T(8,128)(2,1)} collective-permute-done((bf16[384,1024]{1,0:T(8,128)(2,1)}, bf16[384,1024]{1,0:T(8,128)(2,1)}, u32[]{:S(2)}, u32[]{:S(2)}) %collective-permute-start.4) | collective-permute-done | bytes 786464 | tf_op jit(solution)/shard_map/ppermute | solution.py:26
  163.1 3.8 %shard_map.125 = bf16[768,1024]{1,0:T(8,128)(2,1)} custom-call(s32[1]{0:T(128)} %bitcast.s_ref, bf16[384,384]{1,0:T(8,128)(2,1)} %get-tuple-element.34.grad_gate.refs_1_, bf16[384,384]{1,0:T(8,128)(2,1)} %get-tuple-element.35.grad_up.refs_3_, bf16[384,1024]{1,0:T(8,128)(2,1)} %collective-permute-done.4.swapped, ...), custom_call_target="tpu_custom_call", output_to_operand_aliasing={{}: (12, {})} | custom-call | flops 1 | bytes 1 | tf_op jit(solution)/shard_map/pallas_call | solution.py:44
  166.8 4.6 %shard_map.127 = f32[256,2048]{1,0:T(8,128)} custom-call(s32[1]{0:T(128)} %bitcast.s_ref, bf16[512,768]{1,0:T(8,128)(2,1)} %copy.23.weight_ref, bf16[768,2048]{1,0:T(8,128)(2,1)} %bitcast.25.rows_ref), custom_call_target="tpu_custom_call" | custom-call | flops 1 | bytes 1 | tf_op jit(solution)/shard_map/pallas_call | solution.py:44
  171.5 7.4 %all-to-all-start.3 = ((bf16[32,24,1024]{2,1,0:T(8,128)(2,1)}), bf16[32,24,1024]{2,1,0:T(8,128)(2,1)}, u32[]{:S(2)}, u32[]{:S(2)}) async-start(bf16[32,24,1024]{2,1,0:T(8,128)(2,1)} %bitcast.26), calls=%async_computation.4 | async-start | bytes 3145728 | tf_op jit(solution)/shard_map/all_to_all | solution.py:36
  181.4 4.7 %shard_map.129 = f32[8,256]{1,0:T(8,128)} custom-call(s32[1]{0:T(128)} %bitcast.s_ref, bf16[768,2048]{1,0:T(8,128)(2,1)} %bitcast.25.rows_ref, bf16[256,2048]{1,0:T(8,128)(2,1)} %all-gather.2.cloned.1.call-done.grad_ref, bf16[768,256]{1,0:T(8,128)(2,1)} %fusion.2.picked_ref, s32[8,256]{1,0:T(8,128)} %bitcast.95, s32[768,1]{1,0:T(8,128)} %fusion.4.expert_ref), custom_call_target="tpu_custom_call" | custom-call | flops 1 | bytes 1 | tf_op jit(solution)/shard_map/pallas_call | solution.py:44
  186.3 3.7 %collective-permute-done.6 = f32[8,256]{1,0:T(8,128)S(1)} collective-permute-done((f32[8,256]{1,0:T(8,128)}, f32[8,256]{1,0:T(8,128)S(1)}, u32[]{:S(2)}, u32[]{:S(2)}) %collective-permute-start.6) | collective-permute-done | bytes 8224 | tf_op jit(solution)/shard_map/ppermute | solution.py:26
  190.7 10.4 %all-to-all-done.3 = bf16[32,24,1024]{2,1,0:T(8,128)(2,1)} async-done(((bf16[32,24,1024]{2,1,0:T(8,128)(2,1)}), bf16[32,24,1024]{2,1,0:T(8,128)(2,1)}, u32[]{:S(2)}, u32[]{:S(2)}) %all-to-all-start.3) | async-done | bytes 1572896 | tf_op jit(solution)/shard_map/all_to_all | solution.py:36
  201.1 3.0 %shard_map.128 = (f32[256,256]{1,0:T(8,128)}, bf16[4,256,256]{2,1,0:T(8,128)(2,1)}) custom-call(s32[1]{0:T(128)} %bitcast.s_ref, bf16[256,768]{1,0:T(8,128)(2,1)} %copy.20.select_ref, bf16[768,1024]{1,0:T(8,128)(2,1)} %bitcast.27.rows_ref), custom_call_target="tpu_custom_call" | custom-call | flops 1 | bytes 1 | tf_op jit(solution)/shard_map/pallas_call | solution.py:44
  205.2 4.5 %collective-permute-start.9 = (bf16[288,256]{1,0:T(8,128)(2,1)S(1)}, bf16[288,256]{1,0:T(8,128)(2,1)S(1)}, u32[]{:S(2)}, u32[]{:S(2)}) collective-permute-start(bf16[288,256]{1,0:T(8,128)(2,1)S(1)} %get-tuple-element.65), channel_id=1, source_target_pairs={{0,6},{1,7},{2,0},{3,1},{4,2},{5,3},{6,4},{7,5},{8,14},{9,15},{10,... | collective-permute-start | bytes 442376 | tf_op jit(solution)/shard_map/ppermute | solution.py:22
  210.5 2.0 collective-permute-start.7
  212.5 10.3 %collective-permute-done.9 = bf16[288,256]{1,0:T(8,128)(2,1)S(1)} collective-permute-done((bf16[288,256]{1,0:T(8,128)(2,1)S(1)}, bf16[288,256]{1,0:T(8,128)(2,1)S(1)}, u32[]{:S(2)}, u32[]{:S(2)}) %collective-permute-start.9) | collective-permute-done | bytes 147488 | tf_op jit(solution)/shard_map/ppermute | solution.py:22
  222.8 3.2 %collective-permute-done.8 = bf16[288,256]{1,0:T(8,128)(2,1)S(1)} collective-permute-done((bf16[288,256]{1,0:T(8,128)(2,1)S(1)}, bf16[288,256]{1,0:T(8,128)(2,1)S(1)}, u32[]{:S(2)}, u32[]{:S(2)}) %collective-permute-start.8) | collective-permute-done | bytes 147488 | tf_op jit(solution)/shard_map/ppermute | solution.py:22
  (84 shorter events, 18.1 us)
Async XLA Ops:
  7.2 48.1 %all-gather.2.cloned.1.call-start = ((), (), s32[]{:S(2)}) async-start(), calls=%async_computation.5 | async-start | bytes 1179648 | tf_op jit(solution)/shard_map/all_gather | solution.py:224
  7.2 18.0 %collective-permute-start = (bf16[256,256]{1,0:T(8,128)(2,1)}, bf16[256,256]{1,0:T(8,128)(2,1)S(1)}, u32[]{:S(2)}, u32[]{:S(2)}) collective-permute-start(bf16[256,256]{1,0:T(8,128)(2,1)} %refs_0_.1), channel_id=1, source_target_pairs={{0,2},{1,3},{2,4},{3,5},{4,6},{5,7},{6,0},{7,1},{8,10},{9,11},{10,... | collective-permute-start | bytes 393224 | tf_op jit(solution)/shard_map/ppermute | solution.py:22
  10.6 14.7 %collective-permute-start.1 = (bf16[256,256]{1,0:T(8,128)(2,1)}, bf16[256,256]{1,0:T(8,128)(2,1)S(1)}, u32[]{:S(2)}, u32[]{:S(2)}) collective-permute-start(bf16[256,256]{1,0:T(8,128)(2,1)} %refs_0_.1), channel_id=1, source_target_pairs={{0,4},{1,5},{2,6},{3,7},{4,0},{5,1},{6,2},{7,3},{8,12},{9,13},{10,... | collective-permute-start | bytes 393224 | tf_op jit(solution)/shard_map/ppermute | solution.py:22
  15.9 12.4 %collective-permute-start.2 = (bf16[256,256]{1,0:T(8,128)(2,1)}, bf16[256,256]{1,0:T(8,128)(2,1)S(1)}, u32[]{:S(2)}, u32[]{:S(2)}) collective-permute-start(bf16[256,256]{1,0:T(8,128)(2,1)} %refs_0_.1), channel_id=1, source_target_pairs={{0,6},{1,7},{2,0},{3,1},{4,2},{5,3},{6,4},{7,5},{8,14},{9,15},{10,... | collective-permute-start | bytes 393224 | tf_op jit(solution)/shard_map/ppermute | solution.py:22
  20.7 2.8 %copy-start.7 = (s32[256,1]{0,1:T(1,128)}, s32[256,1]{0,1:T(1,128)S(1)}, u32[]{:S(2)}) copy-start(s32[256,1]{0,1:T(1,128)S(1)} %get-tuple-element.68) | copy-start | bytes 3076
  20.7 2.8 %copy-start.9 = (s32[256,1]{0,1:T(1,128)}, s32[256,1]{0,1:T(1,128)S(1)}, u32[]{:S(2)}) copy-start(s32[256,1]{0,1:T(1,128)S(1)} %get-tuple-element.69) | copy-start | bytes 3076
  20.7 2.8 %copy-start.11 = (s32[256,1]{0,1:T(1,128)}, s32[256,1]{0,1:T(1,128)S(1)}, u32[]{:S(2)}) copy-start(s32[256,1]{0,1:T(1,128)S(1)} %get-tuple-element.70) | copy-start | bytes 3076
  20.7 2.8 %copy-start.13 = (s32[256,1]{0,1:T(1,128)}, s32[256,1]{0,1:T(1,128)S(1)}, u32[]{:S(2)}) copy-start(s32[256,1]{0,1:T(1,128)S(1)} %get-tuple-element.71) | copy-start | bytes 3076
  25.2 3.1 %copy-start.2 = (bf16[256,256]{1,0:T(8,128)(2,1)}, bf16[256,256]{1,0:T(8,128)(2,1)S(1)}, u32[]{:S(2)}) copy-start(bf16[256,256]{1,0:T(8,128)(2,1)S(1)} %collective-permute-done.refs_1_) | copy-start | bytes 393220
  25.2 3.1 %copy-start.3 = (bf16[256,256]{1,0:T(8,128)(2,1)}, bf16[256,256]{1,0:T(8,128)(2,1)S(1)}, u32[]{:S(2)}) copy-start(bf16[256,256]{1,0:T(8,128)(2,1)S(1)} %collective-permute-done.1.refs_2_) | copy-start | bytes 393220
  31.9 29.8 %all-to-all-start.1 = ((bf16[32,24,1024]{2,1,0:T(8,128)(2,1)}), bf16[32,24,1024]{2,1,0:T(8,128)(2,1)}, u32[]{:S(2)}, u32[]{:S(2)}) async-start(bf16[32,24,1024]{2,1,0:T(8,128)(2,1)} %bitcast.93), calls=%async_computation.1 | async-start | bytes 3145728 | tf_op jit(solution)/shard_map/all_to_all | solution.py:36
  61.7 51.2 %all-to-all-start = ((bf16[32,24,2048]{2,1,0:T(8,128)(2,1)}), bf16[32,24,2048]{2,1,0:T(8,128)(2,1)}, u32[]{:S(2)}, u32[]{:S(2)}) async-start(bf16[32,24,2048]{2,1,0:T(8,128)(2,1)} %bitcast.92), calls=%async_computation | async-start | bytes 6291456 | tf_op jit(solution)/shard_map/all_to_all | solution.py:36
  68.3 36.9 %collective-permute-start.3 = (bf16[768,1024]{1,0:T(8,128)(2,1)}, bf16[768,1024]{1,0:T(8,128)(2,1)}, u32[]{:S(2)}, u32[]{:S(2)}) collective-permute-start(bf16[768,1024]{1,0:T(8,128)(2,1)} %bitcast.20.rows_ref.refs_6_), channel_id=1, source_target_pairs={{0,1},{1,0},{2,3},{3,2},{4,5},{5,4},{6,7},{7,6},{8,9},{9,8},{10,11... | collective-permute-start | bytes 4718600 | tf_op jit(solution)/shard_map/ppermute | solution.py:26
  118.4 48.4 %all-to-all-start.2 = ((bf16[32,24,2048]{2,1,0:T(8,128)(2,1)}), bf16[32,24,2048]{2,1,0:T(8,128)(2,1)}, u32[]{:S(2)}, u32[]{:S(2)}) async-start(bf16[32,24,2048]{2,1,0:T(8,128)(2,1)} %bitcast.94), calls=%async_computation.2 | async-start | bytes 6291456 | tf_op jit(solution)/shard_map/all_to_all | solution.py:36
  126.0 101.4 %reduce-scatter.2.cloned.1.call-start = ((), (), s32[]{:S(2)}) async-start(), calls=%async_computation.6 | async-start | bytes 2359296 | tf_op jit(solution)/shard_map/reduce_scatter | solution.py:353
  126.0 22.2 %collective-permute-start.5 = (bf16[384,1024]{1,0:T(8,128)(2,1)}, bf16[384,1024]{1,0:T(8,128)(2,1)S(1)}, u32[]{:S(2)}, u32[]{:S(2)}) collective-permute-start(bf16[384,1024]{1,0:T(8,128)(2,1)} %get-tuple-element.41), channel_id=1, source_target_pairs={{0,1},{1,0},{2,3},{3,2},{4,5},{5,4},{6,7},{7,6},{8,9},{9,8},{10,11... | collective-permute-start | bytes 2359304 | tf_op jit(solution)/shard_map/ppermute | solution.py:26
  132.1 31.0 %collective-permute-start.4 = (bf16[384,1024]{1,0:T(8,128)(2,1)}, bf16[384,1024]{1,0:T(8,128)(2,1)}, u32[]{:S(2)}, u32[]{:S(2)}) collective-permute-start(bf16[384,1024]{1,0:T(8,128)(2,1)} %get-tuple-element.36), channel_id=1, source_target_pairs={{0,1},{1,0},{2,3},{3,2},{4,5},{5,4},{6,7},{7,6},{8,9},{9,8},{10,11... | collective-permute-start | bytes 2359304 | tf_op jit(solution)/shard_map/ppermute | solution.py:26
  171.4 8.4 %copy-start.6 = (s32[768]{0:T(1024)S(1)}, s32[768]{0:T(1024)}, u32[]{:S(2)}) copy-start(s32[768]{0:T(1024)} %copy-done.5) | copy-start | bytes 9220
  171.5 8.4 %copy-start.8 = (s32[256,1]{0,1:T(1,128)S(1)}, s32[256,1]{0,1:T(1,128)}, u32[]{:S(2)}) copy-start(s32[256,1]{0,1:T(1,128)} %copy-done.7) | copy-start | bytes 3076
  171.5 8.4 %copy-start.10 = (s32[256,1]{0,1:T(1,128)S(1)}, s32[256,1]{0,1:T(1,128)}, u32[]{:S(2)}) copy-start(s32[256,1]{0,1:T(1,128)} %copy-done.9) | copy-start | bytes 3076
  171.5 8.4 %copy-start.12 = (s32[256,1]{0,1:T(1,128)S(1)}, s32[256,1]{0,1:T(1,128)}, u32[]{:S(2)}) copy-start(s32[256,1]{0,1:T(1,128)} %copy-done.11) | copy-start | bytes 3076
  171.5 8.4 %copy-start.14 = (s32[256,1]{0,1:T(1,128)S(1)}, s32[256,1]{0,1:T(1,128)}, u32[]{:S(2)}) copy-start(s32[256,1]{0,1:T(1,128)} %copy-done.13) | copy-start | bytes 3076
  171.5 8.4 %copy-start.16 = (s32[256,1]{0,1:T(1,128)S(1)}, s32[256,1]{0,1:T(1,128)}, u32[]{:S(2)}) copy-start(s32[256,1]{0,1:T(1,128)} %copy-done.15) | copy-start | bytes 3076
  171.5 8.4 %copy-start.18 = (s32[256,1]{0,1:T(1,128)S(1)}, s32[256,1]{0,1:T(1,128)}, u32[]{:S(2)}) copy-start(s32[256,1]{0,1:T(1,128)} %copy-done.17) | copy-start | bytes 3076
  171.5 8.4 %copy-start.20 = (s32[256,1]{0,1:T(1,128)S(1)}, s32[256,1]{0,1:T(1,128)}, u32[]{:S(2)}) copy-start(s32[256,1]{0,1:T(1,128)} %copy-done.19) | copy-start | bytes 3076
  171.5 8.4 %copy-start.22 = (s32[256,1]{0,1:T(1,128)S(1)}, s32[256,1]{0,1:T(1,128)}, u32[]{:S(2)}) copy-start(s32[256,1]{0,1:T(1,128)} %copy-done.21) | copy-start | bytes 3076
  171.5 29.6 %all-to-all-start.3 = ((bf16[32,24,1024]{2,1,0:T(8,128)(2,1)}), bf16[32,24,1024]{2,1,0:T(8,128)(2,1)}, u32[]{:S(2)}, u32[]{:S(2)}) async-start(bf16[32,24,1024]{2,1,0:T(8,128)(2,1)} %bitcast.26), calls=%async_computation.4 | async-start | bytes 3145728 | tf_op jit(solution)/shard_map/all_to_all | solution.py:36
  186.1 3.9 %collective-permute-start.6 = (f32[8,256]{1,0:T(8,128)}, f32[8,256]{1,0:T(8,128)S(1)}, u32[]{:S(2)}, u32[]{:S(2)}) collective-permute-start(f32[8,256]{1,0:T(8,128)} %shard_map.129), channel_id=1, source_target_pairs={{0,1},{1,0},{2,3},{3,2},{4,5},{5,4},{6,7},{7,6},{8,9},{9,8},{10,11... | collective-permute-start | bytes 24584 | tf_op jit(solution)/shard_map/ppermute | solution.py:26
  204.0 22.7 %copy-start.1 = (f32[256,256]{1,0:T(8,128)S(1)}, f32[256,256]{1,0:T(8,128)}, u32[]{:S(2)}) copy-start(f32[256,256]{1,0:T(8,128)} %get-tuple-element.49) | copy-start | bytes 786436
  205.2 17.6 %collective-permute-start.9 = (bf16[288,256]{1,0:T(8,128)(2,1)S(1)}, bf16[288,256]{1,0:T(8,128)(2,1)S(1)}, u32[]{:S(2)}, u32[]{:S(2)}) collective-permute-start(bf16[288,256]{1,0:T(8,128)(2,1)S(1)} %get-tuple-element.65), channel_id=1, source_target_pairs={{0,6},{1,7},{2,0},{3,1},{4,2},{5,3},{6,4},{7,5},{8,14},{9,15},{10,... | collective-permute-start | bytes 442376 | tf_op jit(solution)/shard_map/ppermute | solution.py:22
  209.7 16.3 %collective-permute-start.8 = (bf16[288,256]{1,0:T(8,128)(2,1)S(1)}, bf16[288,256]{1,0:T(8,128)(2,1)S(1)}, u32[]{:S(2)}, u32[]{:S(2)}) collective-permute-start(bf16[288,256]{1,0:T(8,128)(2,1)S(1)} %get-tuple-element.64), channel_id=1, source_target_pairs={{0,4},{1,5},{2,6},{3,7},{4,0},{5,1},{6,2},{7,3},{8,12},{9,13},{10,... | collective-permute-start | bytes 442376 | tf_op jit(solution)/shard_map/ppermute | solution.py:22
  210.5 15.6 %collective-permute-start.7 = (bf16[288,256]{1,0:T(8,128)(2,1)S(1)}, bf16[288,256]{1,0:T(8,128)(2,1)S(1)}, u32[]{:S(2)}, u32[]{:S(2)}) collective-permute-start(bf16[288,256]{1,0:T(8,128)(2,1)S(1)} %get-tuple-element.63), channel_id=1, source_target_pairs={{0,2},{1,3},{2,4},{3,5},{4,6},{5,7},{6,0},{7,1},{8,10},{9,11},{10,... | collective-permute-start | bytes 442376 | tf_op jit(solution)/shard_map/ppermute | solution.py:22
  (7 other events, 15.3 us)
Sparse Core Ops, SparseCore 0:
  18.8 36.4 all-gather.1
  171.6 42.3 reduce-scatter.1

commit v2 on v1

--- a/solution.py
+++ b/solution.py
@@ -8,9 +8,9 @@
 from jax.sharding import PartitionSpec as P
 
 EXP_DEV = 4
-ROW_CUTS = 3
+ROW_CUTS = 2
 SWAP_CUTS = 2
-VMEM_BYTES = 63 * 1024 * 1024
+VMEM_BYTES = 28 * 1024 * 1024
 F32 = jnp.float32
 BF16 = jnp.bfloat16
 LAST = ((1,), (1,))
@@ -37,10 +37,15 @@
     return moved.reshape(slots, width)
 
 
-def call(body, scalars, grid, operands, in_blocks, outs, out_blocks, flops, aliases=None):
+def in_hbm(operand):
+    return pltpu.with_memory_space_constraint(operand, pltpu.HBM)
+
+
+def call(body, scalars, grid, operands, in_blocks, outs, out_blocks, flops, aliases=None, near=()):
     def spec(block):
         return block[0] if len(block) == 1 else pl.BlockSpec(*block)
 
+    operands = [x if any(x is n for n in near) else in_hbm(x) for x in operands]
     return pl.pallas_call(
         body,
         grid_spec=pltpu.PrefetchScalarGridSpec(
@@ -49,7 +54,7 @@
             in_specs=[spec(b) for b in in_blocks],
             out_specs=[spec(b) for b in out_blocks],
         ),
-        out_shape=list(outs),
+        out_shape=[pltpu.HBM(x.shape, x.dtype) for x in outs],
         input_output_aliases=aliases or {},
         compiler_params=pltpu.CompilerParams(vmem_limit_bytes=VMEM_BYTES),
         cost_estimate=pl.CostEstimate(flops=1, bytes_accessed=1, transcendentals=0),
@@ -107,7 +112,7 @@
 def second_body(s_ref, rows_ref, gate_in, up_in, down_ref, *refs):
     hidden_out, gate_slope, up_slope, part_out = refs[-4:]
     gate_act = gate_in[...] + contract(rows_ref, refs[:EXP_DEV])
-    up_act = up_in[...] + contract(rows_ref, refs[EXP_DEV:-4])
+    up_act = up_in[...] + contract(rows_ref, refs[EXP_DEV : 2 * EXP_DEV])
     sig = jax.nn.sigmoid(gate_act)
     gated = gate_act * sig
     hidden = (gated * up_act).astype(BF16)
@@ -144,30 +149,32 @@
 
 
 def weights_body(s_ref, *refs):
-    hidden, other_ref, mine_ref, grad_ref, gate_out, up_out, down_out = refs[-7:]
-    cuts = (len(refs) - 7) // 2
-    grad_gate, grad_up = refs[:cuts], refs[cuts : 2 * cuts]
-    size = grad_gate[0].shape[0]
-
-    def total(lefts, ref):
-        parts = [
-            dot(left[...], ref[k * size : (k + 1) * size, :], TALL)
-            for k, left in enumerate(lefts)
-        ]
+    mine_ref, grad_ref, gate_out, up_out, down_out = refs[-5:]
+    cuts = (len(refs) - 5) // 4
+    grad_gate, grad_up, hidden, other = (refs[i * cuts : (i + 1) * cuts] for i in range(4))
+    size = hidden[0].shape[0]
+
+    def total(lefts, rights):
+        parts = [dot(left[...], right, TALL) for left, right in zip(lefts, rights)]
         return sum(parts[1:], parts[0]).astype(BF16)
 
-    down_out[0] = dot(hidden[...], grad_ref[...], TALL).astype(BF16)
+    def split(ref):
+        return [ref[k * size : (k + 1) * size, :] for k in range(cuts)]
+
+    down_out[0] = total(hidden, split(grad_ref))
     here = lax.rem(pl.program_id(0), 2) == lax.rem(s_ref[0], 2)
 
     @pl.when(here)
     def _():
-        gate_out[0] = total(grad_gate, mine_ref)
-        up_out[0] = total(grad_up, mine_ref)
+        rows = split(mine_ref)
+        gate_out[0] = total(grad_gate, rows)
+        up_out[0] = total(grad_up, rows)
 
     @pl.when(jnp.logical_not(here))
     def _():
-        gate_out[0] = total(grad_gate, other_ref)
-        up_out[0] = total(grad_up, other_ref)
+        rows = [ref[...] for ref in other]
+        gate_out[0] = total(grad_gate, rows)
+        up_out[0] = total(grad_up, rows)
 
 
 def mix_body(s_ref, weight_ref, rows_ref, out_ref):
@@ -184,15 +191,18 @@
         route_out[k : k + 1, :] = jnp.sum(chosen, axis=0, keepdims=True)
 
 
-def spread_body(s_ref, select_ref, rows_ref, mine_out, piece_out):
-    count, tok_count, shard = piece_out.shape
+def spread_body(s_ref, select_ref, rows_ref, pack_ref, mine_out, *outs):
+    count, shard = len(outs) + 1, outs[0].shape[1]
     select = select_ref[...]
+    tok_count = select.shape[0]
     for r in range(count):
         start = pl.multiple_of(lax.rem(s_ref[0] // 2 + r, count) * shard, shard)
         part = dot(select, rows_ref[:, pl.ds(start, shard)], FLAT)
         if r == 0:
             mine_out[...] = part
-        piece_out[r] = part.astype(BF16)
+        else:
+            outs[r - 1][:tok_count, :] = part.astype(BF16)
+            outs[r - 1][tok_count:, :] = pack_ref[...]
 
 
 def per_device(tokens, expert_ids, route_weights, gate_weight, up_weight, down_weight, grad_out):
@@ -251,9 +261,11 @@
         [select, *own], [whole(select)] + [whole(x) for x in own],
         [shape(slots, half)], [((slots, half), lambda i, s: (0, 0))],
         2 * slots * tok_count * half,
+        near=(select, *own),
     )
     rows_mine = across(sent, groups)
-    rows_other = swap(rows_mine, lanes)
+    size = slots // SWAP_CUTS
+    rows_other = [swap(rows_mine[k * size : (k + 1) * size], lanes) for k in range(SWAP_CUTS)]
 
     (scaled,) = call(
         scaled_body, scalars, (ROW_CUTS,),
@@ -275,51 +287,68 @@
         first_body, scalars, (ROW_CUTS,),
         [rows_mine, *weights_mine], [row_block(half)] + mine_blocks,
         [f32_rows, f32_rows], [unit_block, unit_block], 2 * unit_flops,
-    )
-    hidden, gate_slope, up_slope, expert_part = call(
-        second_body, scalars, (ROW_CUTS,),
-        [rows_other, gate_first, up_first, w_down, *weights_other],
-        [row_block(half), unit_block, unit_block, whole(w_down)] + other_blocks,
-        [shape(slots, units), f32_rows, f32_rows, shape(slots, model_width)],
-        [unit_block, unit_block, unit_block, row_block(model_width)], 4 * unit_flops,
-    )
-
-    size = slots // SWAP_CUTS
+        near=(w_gate, w_up, w_down, rows_mine),
+    )
+
     cut_units = shape(size, units)
+    cut_wide = shape(size, units, F32)
     cut_half = shape(size, half)
 
     def cut_block(width, k):
         return ((size, width), lambda i, s: (k, 0))
+
+    def placed(operands, blocks, array, position):
+        if array is None:
+            return None
+        operands.append(array)
+        blocks.append((pl.BlockSpec(memory_space=pl.ANY),))
+        return {len(operands): position}
+
+    hidden, slopes, expert_part = [], [], None
+    for k in range(SWAP_CUTS):
+        operands = [rows_other[k], gate_first, up_first, w_down, *weights_other]
+        blocks = [whole(cut_half), cut_block(units, k), cut_block(units, k), whole(w_down)]
+        blocks = blocks + other_blocks
+        aliases = placed(operands, blocks, expert_part, 3)
+        got = call(
+            second_body, scalars, (1,), operands, blocks,
+            [cut_units, cut_wide, cut_wide, shape(slots, model_width)],
+            [whole(cut_units), whole(cut_wide), whole(cut_wide), cut_block(model_width, k)],
+            4 * unit_flops // SWAP_CUTS, aliases,
+            near=(w_gate, w_up, w_down, rows_other[k]),
+        )
+        hidden.append(got[0])
+        slopes.append(got[1:3])
+        expert_part = got[3]
 
     grad_gate_act, grad_up_act, swapped = [], [], []
     for k in range(SWAP_CUTS):
         got = call(
             third_body, scalars, (1,),
-            [grad_rows, gate_slope, up_slope, w_down, *weights_other],
-            [cut_block(model_width, k), cut_block(units, k), cut_block(units, k)]
-            + [whole(w_down)] + other_blocks,
+            [grad_rows, *slopes[k], w_down, *weights_other],
+            [cut_block(model_width, k), whole(cut_wide), whole(cut_wide), whole(w_down)]
+            + other_blocks,
             [cut_units, cut_units, cut_half],
             [whole(cut_units), whole(cut_units), whole(cut_half)],
             4 * unit_flops // SWAP_CUTS,
+            near=(w_gate, w_up, w_down),
         )
         grad_gate_act.append(got[0])
         grad_up_act.append(got[1])
-        if k == 0:
-            expert_part, first = lax.optimization_barrier((expert_part, got[2]))
-            swapped.append(swap(first, lanes))
-        else:
-            swapped.append(swap(got[2], lanes))
+        swapped.append(swap(got[2], lanes))
     returned = across(expert_part, groups)
 
     pair_block = ((slots, shard), lambda i, s: (0, i // 2))
+    pair_cut = ((size, shard), lambda i, s: (0, i // 2))
     grad_shape = jax.ShapeDtypeStruct((1, units, model_width), BF16)
     grad_block = ((1, units, shard), lambda i, s: (0, 0, i))
     grad_gate, grad_up, grad_down = call(
         weights_body, scalars, (lanes,),
-        [*grad_gate_act, *grad_up_act, hidden, rows_other, rows_mine, grad_rows],
-        [whole(cut_units)] * (2 * SWAP_CUTS) + [whole(hidden)]
-        + [pair_block, pair_block, ((slots, shard), lambda i, s: (0, i))],
+        [*grad_gate_act, *grad_up_act, *hidden, *rows_other, rows_mine, grad_rows],
+        [whole(cut_units)] * (3 * SWAP_CUTS) + [pair_cut] * SWAP_CUTS
+        + [pair_block, ((slots, shard), lambda i, s: (0, i))],
         [grad_shape] * 3, [grad_block] * 3, 6 * unit_flops,
+        near=(rows_mine, *rows_other),
     )
 
     input_half = []
@@ -334,6 +363,7 @@
         (input_half,) = call(
             fourth_body, scalars, (1,), operands, blocks,
             [outs], [out_blocks], 2 * unit_flops // SWAP_CUTS, aliases,
+            near=(w_gate, w_up, w_down, swapped[k]),
         )
     input_half, returned, grad_gate, grad_up, grad_down = lax.optimization_barrier(
         (input_half, returned, grad_gate, grad_up, grad_down)
@@ -345,9 +375,10 @@
     ids = expert_ids.T
     row_expert = col_expert.reshape(slots, 1)
     (mixed_part,) = call(
-        mix_body, scalars, (2,), [both_weights, returned],
+        mix_body, scalars, (halves,), [both_weights, returned],
         [whole(both_weights), ((slots, half), lambda i, s: (0, i))],
-        [shape(tok_count, model_width, F32)], [((tok_count, half), lambda i, s: (0, i))],
+        [shape(tok_count, model_width, F32)],
+        [((tok_count, half), lambda i, s: (0, i))],
         4 * tok_count * slots * model_width,
     )
     mixed = lax.psum_scatter(mixed_part, "etp", scatter_dimension=1, tiled=True).astype(BF16)
@@ -368,18 +399,15 @@
         route_pack, ((0, pack_rows - 3 * top_count), (0, shard - tok_count))
     )
 
-    spread_outs = [
-        shape(tok_count, shard, F32),
-        jax.ShapeDtypeStruct((EXP_DEV, tok_count, shard), BF16),
-    ]
-    grad_tokens, token_pieces = call(
-        spread_body, scalars, (1,), [select, grad_back], [whole(select), whole(grad_back)],
+    spread_operands = [select, grad_back, route_pack]
+    spread_outs = [shape(tok_count, shard, F32)]
+    spread_outs += [shape(tok_count + pack_rows, shard)] * (EXP_DEV - 1)
+    grad_tokens, *pieces = call(
+        spread_body, scalars, (1,), spread_operands, [whole(x) for x in spread_operands],
         spread_outs, [whole(x) for x in spread_outs], 2 * tok_count * slots * half,
-    )
-    pieces = [
-        shift(jnp.concatenate([token_pieces[r], route_pack], axis=0), halves * r, lanes)
-        for r in range(1, EXP_DEV)
-    ]
+        near=(select, grad_back, route_pack),
+    )
+    pieces = [shift(pieces[r - 1], halves * r, lanes) for r in range(1, EXP_DEV)]
     for piece in pieces:
         piece = piece.astype(F32)
         grad_tokens = grad_tokens + piece[:tok_count]

time: 237 us -> 232 us (0.979)
  Pallas kernels: 62.9 us -> 54.9 us
  local copies, waits for them, and re-layouts: 7.75 us -> 11.5 us
  waiting for transfers between devices: 89 us -> 86.2 us
  starting transfers between devices: 50.9 us -> 53.3 us
    pallas_call x12 -> x13, Pallas kernels: 62.9 us -> 54.9 us  [call(): pl.pallas_call(body, grid_spec=pltpu.PrefetchScalarGridSpec(num_scalar_pr...]
    unnamed x46 -> x32, local copies, waits for them, and re-layouts: 1.64 us -> 5.96 us
    ppermute x4 -> x5, waiting for transfers between devices: 45.4 us -> 41.1 us  [swap(): return lax.ppermute(value, 'etp', [(i, i ^ 1) for i in range(lanes)])]
    ppermute x4 -> x5, starting transfers between devices: 2.94 us -> 5.53 us  [swap(): return lax.ppermute(value, 'etp', [(i, i ^ 1) for i in range(lanes)])]
  transfers between devices with their start and end apart: 16 -> 17, of which waited for: 9 -> 13; matrix products, arithmetic and copies ran while one was open for 7% -> 6% of each run, Pallas kernels for 22% -> 22%
where the time goes in v2:
time: 232 us; the launch traced here: 230 us
  waiting for transfers between devices  86.2 us (37%)
  Pallas kernels  54.9 us (24%)
  starting transfers between devices  53.3 us (23%)
  between operations  14.2 us (6%)
  local copies, waits for them, and re-layouts  11.5 us (5%)
  other arithmetic  7.51 us (3%)
  matrix products  2.57 us (1%)
    pallas_call x13, Pallas kernels, call(): pl.pallas_call(body, grid_spec=pltpu.PrefetchScalarGridSpec(num_scalar_pr...  54.9 us
    ppermute x5, waiting for transfers between devices, swap(): return lax.ppermute(value, 'etp', [(i, i ^ 1) for i in range(lanes)])  41.1 us
    all_to_all x4, starting transfers between devices, across(): lax.all_to_all(cut, 'expert', split_axis=0, concat_axis=0, tiled=True)  29.2 us
    ppermute x6, starting transfers between devices, shift(): lax.ppermute(value, 'etp', [(i, (i + step) % lanes) for i in range(lanes)])  18.5 us
    ppermute x6, waiting for transfers between devices, shift(): lax.ppermute(value, 'etp', [(i, (i + step) % lanes) for i in range(lanes)])  17.8 us
    all_gather x1, waiting for transfers between devices, per_device(): grad_full = lax.all_gather(grad_out, 'etp', axis=1, tiled=True)  16.5 us
    all_to_all x4, waiting for transfers between devices, across(): lax.all_to_all(cut, 'expert', split_axis=0, concat_axis=0, tiled=True)  10.7 us
    unnamed x32, local copies, waits for them, and re-layouts  5.96 us
  transfers between devices with their start and end apart: 17, of which 13 were waited for; matrix products, arithmetic and copies ran while one was open for 6% of the time, Pallas kernels for 22%

profile of v2, /device:TPU:2, one launch (start us, length us, event | category | flops | bytes accessed | tf_op | source)
XLA Modules:
  0.0 230.1 jit_solution(13466398624687932310)
XLA Ops:
  7.2 3.3 %collective-permute-start = (bf16[256,256]{1,0:T(8,128)(2,1)}, bf16[256,256]{1,0:T(8,128)(2,1)S(1)}, u32[]{:S(2)}, u32[]{:S(2)}) collective-permute-start(bf16[256,256]{1,0:T(8,128)(2,1)} %refs_0_.1), channel_id=1, source_target_pairs={{0,2},{1,3},{2,4},{3,5},{4,6},{5,7},{6,0},{7,1},{8,10},{9,11},{10,... | collective-permute-start | bytes 393224 | tf_op jit(solution)/shard_map/ppermute | solution.py:22
  10.6 5.4 %collective-permute-start.1 = (bf16[256,256]{1,0:T(8,128)(2,1)}, bf16[256,256]{1,0:T(8,128)(2,1)S(1)}, u32[]{:S(2)}, u32[]{:S(2)}) collective-permute-start(bf16[256,256]{1,0:T(8,128)(2,1)} %refs_0_.1), channel_id=1, source_target_pairs={{0,4},{1,5},{2,6},{3,7},{4,0},{5,1},{6,2},{7,3},{8,12},{9,13},{10,... | collective-permute-start | bytes 393224 | tf_op jit(solution)/shard_map/ppermute | solution.py:22
  15.9 2.7 %collective-permute-start.2 = (bf16[256,256]{1,0:T(8,128)(2,1)}, bf16[256,256]{1,0:T(8,128)(2,1)S(1)}, u32[]{:S(2)}, u32[]{:S(2)}) collective-permute-start(bf16[256,256]{1,0:T(8,128)(2,1)} %refs_0_.1), channel_id=1, source_target_pairs={{0,6},{1,7},{2,0},{3,1},{4,2},{5,3},{6,4},{7,5},{8,14},{9,15},{10,... | collective-permute-start | bytes 393224 | tf_op jit(solution)/shard_map/ppermute | solution.py:22
  20.7 2.6 %fusion.30 = (f32[768]{0:T(1024)S(1)}, f32[256,768]{1,0:T(8,128)}, pred[256,768]{1,0:T(8,128)(4,1)S(1)}) fusion(f32[256]{0:T(256)S(1)} %bitcast.136, f32[256]{0:T(256)S(1)} %bitcast.137, f32[256]{0:T(256)S(1)} %bitcast.131, f32[256]{0:T(256)S(1)} %bitcast.132, f32[256]{0:T(256)S(1)} %bitcast.133, f32[256]{0:T(256)S(1)} %bitcast.134, f32[256]{0:T(256)S(1)} %bitcast.135, ...), kind=kOutput, calls=%fused_computation.75 | convolution fusion | flops 109772032 | bytes 1008640 | tf_op jit(solution)/shard_map/dot_general | solution.py:30
  25.1 3.3 %collective-permute-done.2.refs_3_ = bf16[256,256]{1,0:T(8,128)(2,1)S(1)} collective-permute-done((bf16[256,256]{1,0:T(8,128)(2,1)}, bf16[256,256]{1,0:T(8,128)(2,1)S(1)}, u32[]{:S(2)}, u32[]{:S(2)}) %collective-permute-start.2) | collective-permute-done | bytes 131104 | tf_op jit(solution)/shard_map/ppermute | solution.py:22
  28.4 1.7 shard_map.119
  30.1 7.6 %all-to-all-start.1 = ((bf16[32,24,1024]{2,1,0:T(8,128)(2,1)}), bf16[32,24,1024]{2,1,0:T(8,128)(2,1)S(1)}, u32[]{:S(2)}, u32[]{:S(2)}) async-start(bf16[32,24,1024]{2,1,0:T(8,128)(2,1)} %bitcast.102), calls=%async_computation.1 | async-start | bytes 3145728 | tf_op jit(solution)/shard_map/all_to_all | solution.py:36
  38.6 16.5 %all-gather.2.cloned.1.call-done.grad_ref = bf16[256,2048]{1,0:T(8,128)(2,1)} async-done(((bf16[256,256]{1,0:T(8,128)(2,1)}), bf16[256,2048]{1,0:T(8,128)(2,1)}) %all-gather.2.cloned.1.call-update) | async-done | bytes 1048592 | tf_op jit(solution)/shard_map/all_gather | solution.py:234
  55.2 3.8 %shard_map.118 = bf16[768,2048]{1,0:T(8,128)(2,1)} custom-call(s32[1]{0:T(128)} %bitcast.s_ref, bf16[256,768]{1,0:T(8,128)(2,1)} %copy-done.7, bf16[256,2048]{1,0:T(8,128)(2,1)} %all-gather.2.cloned.1.call-done.grad_ref, f32[768,1]{1,0:T(8,128)} %broadcast_in_dim.85.weight_ref), custom_call_target="tpu_custom_call" | custom-call | flops 1 | bytes 1 | tf_op jit(solution)/shard_map/pallas_call | solution.py:49
  60.9 6.8 %all-to-all-start = ((bf16[32,24,2048]{2,1,0:T(8,128)(2,1)}), bf16[32,24,2048]{2,1,0:T(8,128)(2,1)}, u32[]{:S(2)}, u32[]{:S(2)}) async-start(bf16[32,24,2048]{2,1,0:T(8,128)(2,1)} %bitcast.100), calls=%async_computation | async-start | bytes 6291456 | tf_op jit(solution)/shard_map/all_to_all | solution.py:36
  67.7 1.7 fusion.32
  72.9 3.1 %shard_map.120 = (f32[768,384]{1,0:T(8,128)}, f32[768,384]{1,0:T(8,128)}) custom-call(s32[1]{0:T(128)} %bitcast.s_ref, bf16[768,1024]{1,0:T(8,128)(2,1)S(1)} %bitcast.93, bf16[384,2048]{1,0:T(8,128)(2,1)S(1)} %bitcast.37, bf16[384,2048]{1,0:T(8,128)(2,1)S(1)} %bitcast.38, bf16[384,2048]{1,0:T(8,128)(2,1)S(1)} %bitcast.39, bf16[384,2048]{1,0:T(8,128)(2,1)S(1)} %bitcast.40, ...), custom_call_target="tpu_custom_call" | custom-call | flops 1 | bytes 1 | tf_op jit(solution)/shard_map/pallas_call | solution.py:49
  76.0 13.8 %collective-permute-done.4.rows_ref.refs_6_ = bf16[384,1024]{1,0:T(8,128)(2,1)S(1)} collective-permute-done((bf16[384,1024]{1,0:T(8,128)(2,1)S(1)}, bf16[384,1024]{1,0:T(8,128)(2,1)S(1)}, u32[]{:S(2)}, u32[]{:S(2)}) %collective-permute-start.4) | collective-permute-done | bytes 786464 | tf_op jit(solution)/shard_map/ppermute | solution.py:26
  89.9 4.7 %shard_map.121 = (bf16[384,384]{1,0:T(8,128)(2,1)}, f32[384,384]{1,0:T(8,128)}, f32[384,384]{1,0:T(8,128)}, bf16[768,2048]{1,0:T(8,128)(2,1)}) custom-call(s32[1]{0:T(128)} %bitcast.s_ref, bf16[384,1024]{1,0:T(8,128)(2,1)S(1)} %collective-permute-done.4.rows_ref.refs_6_, f32[768,384]{1,0:T(8,128)} %get-tuple-element.34.gate_in, ...), custom_call_target="tpu_custom_call" | custom-call | flops 1 | bytes 1 | tf_op jit(solution)/shard_map/pallas_call | solution.py:49
  94.6 11.3 %collective-permute-done.3.rows_ref.refs_7_ = bf16[384,1024]{1,0:T(8,128)(2,1)S(1)} collective-permute-done((bf16[384,1024]{1,0:T(8,128)(2,1)S(1)}, bf16[384,1024]{1,0:T(8,128)(2,1)S(1)}, u32[]{:S(2)}, u32[]{:S(2)}) %collective-permute-start.3) | collective-permute-done | bytes 786464 | tf_op jit(solution)/shard_map/ppermute | solution.py:26
  105.9 4.4 %shard_map.122 = (bf16[384,384]{1,0:T(8,128)(2,1)}, f32[384,384]{1,0:T(8,128)}, f32[384,384]{1,0:T(8,128)}, bf16[768,2048]{1,0:T(8,128)(2,1)}) custom-call(s32[1]{0:T(128)} %bitcast.s_ref, bf16[384,1024]{1,0:T(8,128)(2,1)S(1)} %collective-permute-done.3.rows_ref.refs_7_, f32[768,384]{1,0:T(8,128)} %get-tuple-element.34.gate_in, ...), custom_call_target="tpu_custom_call", output_to_operand_aliasing={{3}: (13, {})} | custom-call | flops 1 | bytes 1 | tf_op jit(solution)/shard_map/pallas_call | solution.py:49
  111.2 7.4 %all-to-all-start.2 = ((bf16[32,24,2048]{2,1,0:T(8,128)(2,1)}), bf16[32,24,2048]{2,1,0:T(8,128)(2,1)}, u32[]{:S(2)}, u32[]{:S(2)}) async-start(bf16[32,24,2048]{2,1,0:T(8,128)(2,1)} %bitcast.101), calls=%async_computation.2 | async-start | bytes 6291456 | tf_op jit(solution)/shard_map/all_to_all | solution.py:36
  120.1 4.5 %shard_map.124 = (bf16[384,384]{1,0:T(8,128)(2,1)}, bf16[384,384]{1,0:T(8,128)(2,1)}, bf16[384,1024]{1,0:T(8,128)(2,1)}) custom-call(s32[1]{0:T(128)} %bitcast.s_ref, bf16[768,2048]{1,0:T(8,128)(2,1)} %bitcast.18.grad_ref.refs_9_, f32[384,384]{1,0:T(8,128)} %get-tuple-element.42.gate_slope, f32[384,384]{1,0:T(8,128)} %get-tuple-element.43.up_slope, ...), custom_call_target="tpu_custom_call" | custom-call | flops 1 | bytes 1 | tf_op jit(solution)/shard_map/pallas_call | solution.py:49
  126.0 4.6 %shard_map.123 = (bf16[384,384]{1,0:T(8,128)(2,1)}, bf16[384,384]{1,0:T(8,128)(2,1)}, bf16[384,1024]{1,0:T(8,128)(2,1)}) custom-call(s32[1]{0:T(128)} %bitcast.s_ref, bf16[768,2048]{1,0:T(8,128)(2,1)} %bitcast.18.grad_ref.refs_9_, f32[384,384]{1,0:T(8,128)} %get-tuple-element.37.gate_slope, f32[384,384]{1,0:T(8,128)} %get-tuple-element.38.up_slope, ...), custom_call_target="tpu_custom_call" | custom-call | flops 1 | bytes 1 | tf_op jit(solution)/shard_map/pallas_call | solution.py:49
  133.3 11.5 %shard_map.127 = (bf16[1,384,2048]{2,1,0:T(8,128)(2,1)}, bf16[1,384,2048]{2,1,0:T(8,128)(2,1)}, bf16[1,384,2048]{2,1,0:T(8,128)(2,1)}) custom-call(s32[1]{0:T(128)} %bitcast.s_ref, bf16[384,384]{1,0:T(8,128)(2,1)} %get-tuple-element.44.grad_gate.refs_0_, bf16[384,384]{1,0:T(8,128)(2,1)} %get-tuple-element.39.grad_gate.refs_1_, ...), custom_call_target="tpu_custom_call" | custom-call | flops 1 | bytes 1 | tf_op jit(solution)/shard_map/pallas_call | solution.py:49
  145.2 3.0 %shard_map.125.refs_8_ = bf16[768,1024]{1,0:T(8,128)(2,1)} custom-call(s32[1]{0:T(128)} %bitcast.s_ref, bf16[384,384]{1,0:T(8,128)(2,1)} %get-tuple-element.44.grad_gate.refs_0_, bf16[384,384]{1,0:T(8,128)(2,1)} %get-tuple-element.45.grad_up.refs_2_, bf16[384,1024]{1,0:T(8,128)(2,1)S(1)} %collective-permute-done.6.swapped, bf16[384,2048]{1,0:T(8,128)(2,1)S(1)} %bitcast.57, ...), custom_call_target="tpu_custom_call" | custom-call | flops 1 | bytes 1 | tf_op jit(solution)/shard_map/pallas_call | solution.py:49
  148.1 13.1 %collective-permute-done.5.swapped = bf16[384,1024]{1,0:T(8,128)(2,1)S(1)} collective-permute-done((bf16[384,1024]{1,0:T(8,128)(2,1)}, bf16[384,1024]{1,0:T(8,128)(2,1)S(1)}, u32[]{:S(2)}, u32[]{:S(2)}) %collective-permute-start.5) | collective-permute-done | bytes 786464 | tf_op jit(solution)/shard_map/ppermute | solution.py:26
  161.2 2.9 %shard_map.126 = bf16[768,1024]{1,0:T(8,128)(2,1)} custom-call(s32[1]{0:T(128)} %bitcast.s_ref, bf16[384,384]{1,0:T(8,128)(2,1)} %get-tuple-element.39.grad_gate.refs_1_, bf16[384,384]{1,0:T(8,128)(2,1)} %get-tuple-element.40.grad_up.refs_3_, bf16[384,1024]{1,0:T(8,128)(2,1)S(1)} %collective-permute-done.5.swapped, ...), custom_call_target="tpu_custom_call", output_to_operand_aliasing={{}: (12, {})} | custom-call | flops 1 | bytes 1 | tf_op jit(solution)/shard_map/pallas_call | solution.py:49
  164.1 4.6 %shard_map.128 = f32[256,2048]{1,0:T(8,128)} custom-call(s32[1]{0:T(128)} %bitcast.s_ref, bf16[512,768]{1,0:T(8,128)(2,1)} %pad_maximum_fusion.weight_ref, bf16[768,2048]{1,0:T(8,128)(2,1)} %bitcast.27.rows_ref), custom_call_target="tpu_custom_call" | custom-call | flops 1 | bytes 1 | tf_op jit(solution)/shard_map/pallas_call | solution.py:49
  168.7 7.4 %all-to-all-start.3 = ((bf16[32,24,1024]{2,1,0:T(8,128)(2,1)}), bf16[32,24,1024]{2,1,0:T(8,128)(2,1)S(1)}, u32[]{:S(2)}, u32[]{:S(2)}) async-start(bf16[32,24,1024]{2,1,0:T(8,128)(2,1)} %bitcast.28), calls=%async_computation.4 | async-start | bytes 3145728 | tf_op jit(solution)/shard_map/all_to_all | solution.py:36
  178.9 4.8 %shard_map.129 = f32[8,256]{1,0:T(8,128)} custom-call(s32[1]{0:T(128)} %bitcast.s_ref, bf16[768,2048]{1,0:T(8,128)(2,1)} %bitcast.27.rows_ref, bf16[256,2048]{1,0:T(8,128)(2,1)} %all-gather.2.cloned.1.call-done.grad_ref, bf16[768,256]{1,0:T(8,128)(2,1)} %copy.17.picked_ref, s32[8,256]{1,0:T(8,128)} %bitcast.105, s32[768,1]{1,0:T(8,128)} %fusion.4.expert_ref), custom_call_target="tpu_custom_call" | custom-call | flops 1 | bytes 1 | tf_op jit(solution)/shard_map/pallas_call | solution.py:49
  185.0 2.5 %collective-permute-done.7 = f32[8,256]{1,0:T(8,128)S(1)} collective-permute-done((f32[8,256]{1,0:T(8,128)}, f32[8,256]{1,0:T(8,128)S(1)}, u32[]{:S(2)}, u32[]{:S(2)}) %collective-permute-start.7) | collective-permute-done | bytes 8224 | tf_op jit(solution)/shard_map/ppermute | solution.py:26
  188.2 10.0 %all-to-all-done.3 = bf16[32,24,1024]{2,1,0:T(8,128)(2,1)S(1)} async-done(((bf16[32,24,1024]{2,1,0:T(8,128)(2,1)}), bf16[32,24,1024]{2,1,0:T(8,128)(2,1)S(1)}, u32[]{:S(2)}, u32[]{:S(2)}) %all-to-all-start.3) | async-done | bytes 1572896 | tf_op jit(solution)/shard_map/all_to_all | solution.py:36
  199.5 4.3 %collective-permute-start.10 = (bf16[288,256]{1,0:T(8,128)(2,1)}, bf16[288,256]{1,0:T(8,128)(2,1)S(1)}, u32[]{:S(2)}, u32[]{:S(2)}) collective-permute-start(bf16[288,256]{1,0:T(8,128)(2,1)} %get-tuple-element.58), channel_id=1, source_target_pairs={{0,6},{1,7},{2,0},{3,1},{4,2},{5,3},{6,4},{7,5},{8,14},{9,15},{10,... | collective-permute-start | bytes 442376 | tf_op jit(solution)/shard_map/ppermute | solution.py:22
  206.6 8.0 %collective-permute-done.10 = bf16[288,256]{1,0:T(8,128)(2,1)S(1)} collective-permute-done((bf16[288,256]{1,0:T(8,128)(2,1)}, bf16[288,256]{1,0:T(8,128)(2,1)S(1)}, u32[]{:S(2)}, u32[]{:S(2)}) %collective-permute-start.10) | collective-permute-done | bytes 147488 | tf_op jit(solution)/shard_map/ppermute | solution.py:22
  214.6 4.4 %collective-permute-done.9 = bf16[288,256]{1,0:T(8,128)(2,1)S(1)} collective-permute-done((bf16[288,256]{1,0:T(8,128)(2,1)}, bf16[288,256]{1,0:T(8,128)(2,1)S(1)}, u32[]{:S(2)}, u32[]{:S(2)}) %collective-permute-start.9) | collective-permute-done | bytes 147488 | tf_op jit(solution)/shard_map/ppermute | solution.py:22
  221.7 1.6 convert_element_type.49
  (71 shorter events, 28.7 us)
Async XLA Ops:
  7.2 48.0 %all-gather.2.cloned.1.call-start = ((), (), s32[]{:S(2)}) async-start(), calls=%async_computation.5 | async-start | bytes 1179648 | tf_op jit(solution)/shard_map/all_gather | solution.py:234
  7.2 17.0 %collective-permute-start = (bf16[256,256]{1,0:T(8,128)(2,1)}, bf16[256,256]{1,0:T(8,128)(2,1)S(1)}, u32[]{:S(2)}, u32[]{:S(2)}) collective-permute-start(bf16[256,256]{1,0:T(8,128)(2,1)} %refs_0_.1), channel_id=1, source_target_pairs={{0,2},{1,3},{2,4},{3,5},{4,6},{5,7},{6,0},{7,1},{8,10},{9,11},{10,... | collective-permute-start | bytes 393224 | tf_op jit(solution)/shard_map/ppermute | solution.py:22
  10.6 14.5 %collective-permute-start.1 = (bf16[256,256]{1,0:T(8,128)(2,1)}, bf16[256,256]{1,0:T(8,128)(2,1)S(1)}, u32[]{:S(2)}, u32[]{:S(2)}) collective-permute-start(bf16[256,256]{1,0:T(8,128)(2,1)} %refs_0_.1), channel_id=1, source_target_pairs={{0,4},{1,5},{2,6},{3,7},{4,0},{5,1},{6,2},{7,3},{8,12},{9,13},{10,... | collective-permute-start | bytes 393224 | tf_op jit(solution)/shard_map/ppermute | solution.py:22
  15.9 12.4 %collective-permute-start.2 = (bf16[256,256]{1,0:T(8,128)(2,1)}, bf16[256,256]{1,0:T(8,128)(2,1)S(1)}, u32[]{:S(2)}, u32[]{:S(2)}) collective-permute-start(bf16[256,256]{1,0:T(8,128)(2,1)} %refs_0_.1), channel_id=1, source_target_pairs={{0,6},{1,7},{2,0},{3,1},{4,2},{5,3},{6,4},{7,5},{8,14},{9,15},{10,... | collective-permute-start | bytes 393224 | tf_op jit(solution)/shard_map/ppermute | solution.py:22
  20.7 7.7 %copy-start.13 = (bf16[256,256]{1,0:T(8,128)(2,1)S(1)}, bf16[256,256]{1,0:T(8,128)(2,1)}, u32[]{:S(2)}) copy-start(bf16[256,256]{1,0:T(8,128)(2,1)} %refs_0_.1) | copy-start | bytes 393220
  24.2 5.9 %copy-start.7 = (bf16[256,768]{1,0:T(8,128)(2,1)}, bf16[256,768]{1,0:T(8,128)(2,1)S(1)}, u32[]{:S(2)}) copy-start(bf16[256,768]{1,0:T(8,128)(2,1)S(1)} %fusion.12.select_ref) | copy-start | bytes 1179652
  30.1 29.7 %all-to-all-start.1 = ((bf16[32,24,1024]{2,1,0:T(8,128)(2,1)}), bf16[32,24,1024]{2,1,0:T(8,128)(2,1)S(1)}, u32[]{:S(2)}, u32[]{:S(2)}) async-start(bf16[32,24,1024]{2,1,0:T(8,128)(2,1)} %bitcast.102), calls=%async_computation.1 | async-start | bytes 3145728 | tf_op jit(solution)/shard_map/all_to_all | solution.py:36
  59.8 1.1 copy-start.2
  60.9 50.2 %all-to-all-start = ((bf16[32,24,2048]{2,1,0:T(8,128)(2,1)}), bf16[32,24,2048]{2,1,0:T(8,128)(2,1)}, u32[]{:S(2)}, u32[]{:S(2)}) async-start(bf16[32,24,2048]{2,1,0:T(8,128)(2,1)} %bitcast.100), calls=%async_computation | async-start | bytes 6291456 | tf_op jit(solution)/shard_map/all_to_all | solution.py:36
  67.7 3.8 %copy-start = (bf16[1,384,2048]{2,1,0:T(8,128)(2,1)S(1)}, bf16[1,384,2048]{2,1,0:T(8,128)(2,1)}, u32[]{:S(2)}) copy-start(bf16[1,384,2048]{2,1,0:T(8,128)(2,1)} %param.10) | copy-start | bytes 4718596
  67.7 3.8 %copy-start.1 = (bf16[1,384,2048]{2,1,0:T(8,128)(2,1)S(1)}, bf16[1,384,2048]{2,1,0:T(8,128)(2,1)}, u32[]{:S(2)}) copy-start(bf16[1,384,2048]{2,1,0:T(8,128)(2,1)} %param.11) | copy-start | bytes 4718596
  69.4 20.5 %collective-permute-start.4 = (bf16[384,1024]{1,0:T(8,128)(2,1)S(1)}, bf16[384,1024]{1,0:T(8,128)(2,1)S(1)}, u32[]{:S(2)}, u32[]{:S(2)}) collective-permute-start(bf16[384,1024]{1,0:T(8,128)(2,1)S(1)} %bitcast.104), channel_id=1, source_target_pairs={{0,1},{1,0},{2,3},{3,2},{4,5},{5,4},{6,7},{7,6},{8,9},{9,8},{10,11... | collective-permute-start | bytes 2359304 | tf_op jit(solution)/shard_map/ppermute | solution.py:26
  70.9 35.1 %collective-permute-start.3 = (bf16[384,1024]{1,0:T(8,128)(2,1)S(1)}, bf16[384,1024]{1,0:T(8,128)(2,1)S(1)}, u32[]{:S(2)}, u32[]{:S(2)}) collective-permute-start(bf16[384,1024]{1,0:T(8,128)(2,1)S(1)} %bitcast.103), channel_id=1, source_target_pairs={{0,1},{1,0},{2,3},{3,2},{4,5},{5,4},{6,7},{7,6},{8,9},{9,8},{10,11... | collective-permute-start | bytes 2359304 | tf_op jit(solution)/shard_map/ppermute | solution.py:26
  71.5 1.4 copy-start.3
  72.9 16.9 %copy-start.5 = (bf16[1,384,2048]{2,1,0:T(8,128)(2,1)S(1)}, bf16[1,384,2048]{2,1,0:T(8,128)(2,1)}, u32[]{:S(2)}) copy-start(bf16[1,384,2048]{2,1,0:T(8,128)(2,1)} %param.12) | copy-start | bytes 4718596
  89.9 4.7 %copy-start.9 = (bf16[384,1024]{1,0:T(8,128)(2,1)}, bf16[384,1024]{1,0:T(8,128)(2,1)S(1)}, u32[]{:S(2)}) copy-start(bf16[384,1024]{1,0:T(8,128)(2,1)S(1)} %collective-permute-done.4.rows_ref.refs_6_) | copy-start | bytes 2359300
  111.2 53.0 %all-to-all-start.2 = ((bf16[32,24,2048]{2,1,0:T(8,128)(2,1)}), bf16[32,24,2048]{2,1,0:T(8,128)(2,1)}, u32[]{:S(2)}, u32[]{:S(2)}) async-start(bf16[32,24,2048]{2,1,0:T(8,128)(2,1)} %bitcast.101), calls=%async_computation.2 | async-start | bytes 6291456 | tf_op jit(solution)/shard_map/all_to_all | solution.py:36
  118.6 103.1 %reduce-scatter.2.cloned.1.call-start = ((), (), s32[]{:S(2)}) async-start(), calls=%async_computation.6 | async-start | bytes 2359296 | tf_op jit(solution)/shard_map/reduce_scatter | solution.py:384
  118.7 1.4 copy-start.6
  124.6 20.6 %collective-permute-start.6 = (bf16[384,1024]{1,0:T(8,128)(2,1)}, bf16[384,1024]{1,0:T(8,128)(2,1)S(1)}, u32[]{:S(2)}, u32[]{:S(2)}) collective-permute-start(bf16[384,1024]{1,0:T(8,128)(2,1)} %get-tuple-element.46), channel_id=1, source_target_pairs={{0,1},{1,0},{2,3},{3,2},{4,5},{5,4},{6,7},{7,6},{8,9},{9,8},{10,11... | collective-permute-start | bytes 2359304 | tf_op jit(solution)/shard_map/ppermute | solution.py:26
  126.0 5.2 %copy-start.14 = (f32[256,768]{1,0:T(8,128)S(1)}, f32[256,768]{1,0:T(8,128)}, u32[]{:S(2)}) copy-start(f32[256,768]{1,0:T(8,128)} %get-tuple-element.65) | copy-start | bytes 2359300
  130.5 30.7 %collective-permute-start.5 = (bf16[384,1024]{1,0:T(8,128)(2,1)}, bf16[384,1024]{1,0:T(8,128)(2,1)S(1)}, u32[]{:S(2)}, u32[]{:S(2)}) collective-permute-start(bf16[384,1024]{1,0:T(8,128)(2,1)} %get-tuple-element.41), channel_id=1, source_target_pairs={{0,1},{1,0},{2,3},{3,2},{4,5},{5,4},{6,7},{7,6},{8,9},{9,8},{10,11... | collective-permute-start | bytes 2359304 | tf_op jit(solution)/shard_map/ppermute | solution.py:26
  131.2 1.7 copy-start.4
  131.2 1.9 copy-start.10
  131.2 2.1 copy-start.12
  168.7 29.4 %all-to-all-start.3 = ((bf16[32,24,1024]{2,1,0:T(8,128)(2,1)}), bf16[32,24,1024]{2,1,0:T(8,128)(2,1)S(1)}, u32[]{:S(2)}, u32[]{:S(2)}) async-start(bf16[32,24,1024]{2,1,0:T(8,128)(2,1)} %bitcast.28), calls=%async_computation.4 | async-start | bytes 3145728 | tf_op jit(solution)/shard_map/all_to_all | solution.py:36
  178.9 19.3 %copy-start.8 = (bf16[256,768]{1,0:T(8,128)(2,1)S(1)}, bf16[256,768]{1,0:T(8,128)(2,1)}, u32[]{:S(2)}) copy-start(bf16[256,768]{1,0:T(8,128)(2,1)} %copy-done.7) | copy-start | bytes 1179652
  183.6 3.9 %collective-permute-start.7 = (f32[8,256]{1,0:T(8,128)}, f32[8,256]{1,0:T(8,128)S(1)}, u32[]{:S(2)}, u32[]{:S(2)}) collective-permute-start(f32[8,256]{1,0:T(8,128)} %shard_map.129), channel_id=1, source_target_pairs={{0,1},{1,0},{2,3},{3,2},{4,5},{5,4},{6,7},{7,6},{8,9},{9,8},{10,11... | collective-permute-start | bytes 24584 | tf_op jit(solution)/shard_map/ppermute | solution.py:26
  199.5 21.4 %copy-start.15 = (f32[256,256]{1,0:T(8,128)S(1)}, f32[256,256]{1,0:T(8,128)}, u32[]{:S(2)}) copy-start(f32[256,256]{1,0:T(8,128)} %get-tuple-element.55) | copy-start | bytes 786436
  199.5 15.0 %collective-permute-start.10 = (bf16[288,256]{1,0:T(8,128)(2,1)}, bf16[288,256]{1,0:T(8,128)(2,1)S(1)}, u32[]{:S(2)}, u32[]{:S(2)}) collective-permute-start(bf16[288,256]{1,0:T(8,128)(2,1)} %get-tuple-element.58), channel_id=1, source_target_pairs={{0,6},{1,7},{2,0},{3,1},{4,2},{5,3},{6,4},{7,5},{8,14},{9,15},{10,... | collective-permute-start | bytes 442376 | tf_op jit(solution)/shard_map/ppermute | solution.py:22
  203.9 15.1 %collective-permute-start.9 = (bf16[288,256]{1,0:T(8,128)(2,1)}, bf16[288,256]{1,0:T(8,128)(2,1)S(1)}, u32[]{:S(2)}, u32[]{:S(2)}) collective-permute-start(bf16[288,256]{1,0:T(8,128)(2,1)} %get-tuple-element.57), channel_id=1, source_target_pairs={{0,4},{1,5},{2,6},{3,7},{4,0},{5,1},{6,2},{7,3},{8,12},{9,13},{10,... | collective-permute-start | bytes 442376 | tf_op jit(solution)/shard_map/ppermute | solution.py:22
  205.2 15.1 %collective-permute-start.8 = (bf16[288,256]{1,0:T(8,128)(2,1)}, bf16[288,256]{1,0:T(8,128)(2,1)S(1)}, u32[]{:S(2)}, u32[]{:S(2)}) collective-permute-start(bf16[288,256]{1,0:T(8,128)(2,1)} %get-tuple-element.56), channel_id=1, source_target_pairs={{0,2},{1,3},{2,4},{3,5},{4,6},{5,7},{6,0},{7,1},{8,10},{9,11},{10,... | collective-permute-start | bytes 442376 | tf_op jit(solution)/shard_map/ppermute | solution.py:22
  (1 other events, 0.9 us)
Sparse Core Ops, SparseCore 0:
  18.8 36.3 all-gather.1
  168.9 47.4 reduce-scatter.1

commit v3 on v2

--- a/solution.py
+++ b/solution.py
@@ -331,7 +331,7 @@
             [cut_units, cut_units, cut_half],
             [whole(cut_units), whole(cut_units), whole(cut_half)],
             4 * unit_flops // SWAP_CUTS,
-            near=(w_gate, w_up, w_down),
+            near=(w_gate, w_up),
         )
         grad_gate_act.append(got[0])
         grad_up_act.append(got[1])
@@ -353,6 +353,19 @@
 
     input_half = []
     for k in range(SWAP_CUTS):
+        if k == SWAP_CUTS - 1:
+            returned, input_half, grad_gate, grad_up, grad_down = lax.optimization_barrier(
+                (returned, input_half, grad_gate, grad_up, grad_down)
+            )
+            both_weights = jnp.concatenate([weight_high, weight_low], axis=0)
+            (mixed_part,) = call(
+                mix_body, scalars, (halves,), [both_weights, returned],
+                [whole(both_weights), ((slots, half), lambda i, s: (0, i))],
+                [shape(tok_count, model_width, F32)],
+                [((tok_count, half), lambda i, s: (0, i))],
+                4 * tok_count * slots * model_width,
+            )
+            swapped[k], mixed_part = lax.optimization_barrier((swapped[k], mixed_part))
         operands = [grad_gate_act[k], grad_up_act[k], swapped[k], *weights_mine]
         blocks = [whole(cut_units), whole(cut_units), whole(cut_half)] + mine_blocks
         outs, out_blocks, aliases = shape(slots, half), cut_block(half, k), None
@@ -370,17 +383,9 @@
     )
     grad_back = across(input_half, groups)
 
-    both_weights = jnp.concatenate([weight_high, weight_low], axis=0)
     picked = select.T
     ids = expert_ids.T
     row_expert = col_expert.reshape(slots, 1)
-    (mixed_part,) = call(
-        mix_body, scalars, (halves,), [both_weights, returned],
-        [whole(both_weights), ((slots, half), lambda i, s: (0, i))],
-        [shape(tok_count, model_width, F32)],
-        [((tok_count, half), lambda i, s: (0, i))],
-        4 * tok_count * slots * model_width,
-    )
     mixed = lax.psum_scatter(mixed_part, "etp", scatter_dimension=1, tiled=True).astype(BF16)
     route_operands = [returned, grad_full, picked, ids, row_expert]
     (route_sum,) = call(
@@ -408,6 +413,7 @@
         near=(select, grad_back, route_pack),
     )
     pieces = [shift(pieces[r - 1], halves * r, lanes) for r in range(1, EXP_DEV)]
+    mixed, pieces[-1] = lax.optimization_barrier((mixed, pieces[-1]))
     for piece in pieces:
         piece = piece.astype(F32)
         grad_tokens = grad_tokens + piece[:tok_count]

time: 232 us -> 227 us (0.978)
  local copies, waits for them, and re-layouts: 11.5 us -> 8.09 us
  waiting for transfers between devices: 86.2 us -> 82.8 us
    ppermute x5, waiting for transfers between devices: 41.1 us -> 28.5 us  [swap(): return lax.ppermute(value, 'etp', [(i, i ^ 1) for i in range(lanes)])]
    all_to_all x4, waiting for transfers between devices: 10.7 us -> 22.2 us  [across(): lax.all_to_all(cut, 'expert', split_axis=0, concat_axis=0, tiled=True)]
    unnamed x32 -> x56, local copies, waits for them, and re-layouts: 5.96 us -> 3.54 us
  transfers between devices with their start and end apart: 17 -> 17, of which waited for: 13 -> 12; matrix products, arithmetic and copies ran while one was open for 6% -> 6% of each run, Pallas kernels for 22% -> 25%
where the time goes in v3:
time: 227 us; the launch traced here: 225 us
  waiting for transfers between devices  82.8 us (36%)
  Pallas kernels  56.3 us (25%)
  starting transfers between devices  53.4 us (24%)
  between operations  14.4 us (6%)
  other arithmetic  8.57 us (4%)
  local copies, waits for them, and re-layouts  8.09 us (4%)
    pallas_call x13, Pallas kernels, call(): pl.pallas_call(body, grid_spec=pltpu.PrefetchScalarGridSpec(num_scalar_pr...  56.3 us
    ppermute x5, waiting for transfers between devices, swap(): return lax.ppermute(value, 'etp', [(i, i ^ 1) for i in range(lanes)])  28.5 us
    all_to_all x4, starting transfers between devices, across(): lax.all_to_all(cut, 'expert', split_axis=0, concat_axis=0, tiled=True)  27.9 us
    all_to_all x4, waiting for transfers between devices, across(): lax.all_to_all(cut, 'expert', split_axis=0, concat_axis=0, tiled=True)  22.2 us
    ppermute x6, starting transfers between devices, shift(): lax.ppermute(value, 'etp', [(i, (i + step) % lanes) for i in range(lanes)])  19.8 us
    ppermute x6, waiting for transfers between devices, shift(): lax.ppermute(value, 'etp', [(i, (i + step) % lanes) for i in range(lanes)])  17.8 us
    all_gather x1, waiting for transfers between devices, per_device(): grad_full = lax.all_gather(grad_out, 'etp', axis=1, tiled=True)  14.3 us
    ppermute x5, starting transfers between devices, swap(): return lax.ppermute(value, 'etp', [(i, i ^ 1) for i in range(lanes)])  5.57 us
  transfers between devices with their start and end apart: 17, of which 12 were waited for; matrix products, arithmetic and copies ran while one was open for 6% of the time, Pallas kernels for 25%

profile of v3, /device:TPU:2, one launch (start us, length us, event | category | flops | bytes accessed | tf_op | source)
XLA Modules:
  0.0 225.1 jit_solution(258804450166398855)
XLA Ops:
  7.2 3.3 %collective-permute-start = (bf16[256,256]{1,0:T(8,128)(2,1)}, bf16[256,256]{1,0:T(8,128)(2,1)S(1)}, u32[]{:S(2)}, u32[]{:S(2)}) collective-permute-start(bf16[256,256]{1,0:T(8,128)(2,1)} %refs_0_.1), channel_id=1, source_target_pairs={{0,2},{1,3},{2,4},{3,5},{4,6},{5,7},{6,0},{7,1},{8,10},{9,11},{10,... | collective-permute-start | bytes 393224 | tf_op jit(solution)/shard_map/ppermute | solution.py:22
  10.6 5.4 %collective-permute-start.1 = (bf16[256,256]{1,0:T(8,128)(2,1)}, bf16[256,256]{1,0:T(8,128)(2,1)S(1)}, u32[]{:S(2)}, u32[]{:S(2)}) collective-permute-start(bf16[256,256]{1,0:T(8,128)(2,1)} %refs_0_.1), channel_id=1, source_target_pairs={{0,4},{1,5},{2,6},{3,7},{4,0},{5,1},{6,2},{7,3},{8,12},{9,13},{10,... | collective-permute-start | bytes 393224 | tf_op jit(solution)/shard_map/ppermute | solution.py:22
  15.9 2.7 %collective-permute-start.2 = (bf16[256,256]{1,0:T(8,128)(2,1)}, bf16[256,256]{1,0:T(8,128)(2,1)S(1)}, u32[]{:S(2)}, u32[]{:S(2)}) collective-permute-start(bf16[256,256]{1,0:T(8,128)(2,1)} %refs_0_.1), channel_id=1, source_target_pairs={{0,6},{1,7},{2,0},{3,1},{4,2},{5,3},{6,4},{7,5},{8,14},{9,15},{10,... | collective-permute-start | bytes 393224 | tf_op jit(solution)/shard_map/ppermute | solution.py:22
  21.3 3.8 %collective-permute-done.1.refs_2_ = bf16[256,256]{1,0:T(8,128)(2,1)S(1)} collective-permute-done((bf16[256,256]{1,0:T(8,128)(2,1)}, bf16[256,256]{1,0:T(8,128)(2,1)S(1)}, u32[]{:S(2)}, u32[]{:S(2)}) %collective-permute-start.1) | collective-permute-done | bytes 131104 | tf_op jit(solution)/shard_map/ppermute | solution.py:22
  25.1 3.3 %collective-permute-done.2.refs_3_ = bf16[256,256]{1,0:T(8,128)(2,1)S(1)} collective-permute-done((bf16[256,256]{1,0:T(8,128)(2,1)}, bf16[256,256]{1,0:T(8,128)(2,1)S(1)}, u32[]{:S(2)}, u32[]{:S(2)}) %collective-permute-start.2) | collective-permute-done | bytes 131104 | tf_op jit(solution)/shard_map/ppermute | solution.py:22
  28.4 1.7 shard_map.119
  30.1 7.8 %all-to-all-start.1 = ((bf16[32,24,1024]{2,1,0:T(8,128)(2,1)}), bf16[32,24,1024]{2,1,0:T(8,128)(2,1)S(1)}, u32[]{:S(2)}, u32[]{:S(2)}) async-start(bf16[32,24,1024]{2,1,0:T(8,128)(2,1)} %bitcast.103), calls=%async_computation.1 | async-start | bytes 3145728 | tf_op jit(solution)/shard_map/all_to_all | solution.py:36
  40.9 14.3 %all-gather.2.cloned.1.call-done.grad_ref = bf16[256,2048]{1,0:T(8,128)(2,1)} async-done(((bf16[256,256]{1,0:T(8,128)(2,1)}), bf16[256,2048]{1,0:T(8,128)(2,1)}) %all-gather.2.cloned.1.call-update) | async-done | bytes 1048592 | tf_op jit(solution)/shard_map/all_gather | solution.py:234
  55.2 3.8 %shard_map.118 = bf16[768,2048]{1,0:T(8,128)(2,1)} custom-call(s32[1]{0:T(128)} %bitcast.s_ref, bf16[256,768]{1,0:T(8,128)(2,1)} %copy-done.6, bf16[256,2048]{1,0:T(8,128)(2,1)} %all-gather.2.cloned.1.call-done.grad_ref, f32[768,1]{1,0:T(8,128)} %broadcast_in_dim.85.weight_ref), custom_call_target="tpu_custom_call" | custom-call | flops 1 | bytes 1 | tf_op jit(solution)/shard_map/pallas_call | solution.py:49
  61.1 6.6 %all-to-all-start = ((bf16[32,24,2048]{2,1,0:T(8,128)(2,1)}), bf16[32,24,2048]{2,1,0:T(8,128)(2,1)}, u32[]{:S(2)}, u32[]{:S(2)}) async-start(bf16[32,24,2048]{2,1,0:T(8,128)(2,1)} %bitcast.101), calls=%async_computation | async-start | bytes 6291456 | tf_op jit(solution)/shard_map/all_to_all | solution.py:36
  67.7 1.7 fusion.31
  72.9 3.1 %shard_map.120 = (f32[768,384]{1,0:T(8,128)}, f32[768,384]{1,0:T(8,128)}) custom-call(s32[1]{0:T(128)} %bitcast.s_ref, bf16[768,1024]{1,0:T(8,128)(2,1)S(1)} %bitcast.93, bf16[384,2048]{1,0:T(8,128)(2,1)S(1)} %bitcast.37, bf16[384,2048]{1,0:T(8,128)(2,1)S(1)} %bitcast.38, bf16[384,2048]{1,0:T(8,128)(2,1)S(1)} %bitcast.39, bf16[384,2048]{1,0:T(8,128)(2,1)S(1)} %bitcast.40, ...), custom_call_target="tpu_custom_call" | custom-call | flops 1 | bytes 1 | tf_op jit(solution)/shard_map/pallas_call | solution.py:49
  76.0 13.8 %collective-permute-done.4.rows_ref.refs_6_ = bf16[384,1024]{1,0:T(8,128)(2,1)S(1)} collective-permute-done((bf16[384,1024]{1,0:T(8,128)(2,1)S(1)}, bf16[384,1024]{1,0:T(8,128)(2,1)S(1)}, u32[]{:S(2)}, u32[]{:S(2)}) %collective-permute-start.4) | collective-permute-done | bytes 786464 | tf_op jit(solution)/shard_map/ppermute | solution.py:26
  89.9 4.7 %shard_map.121 = (bf16[384,384]{1,0:T(8,128)(2,1)}, f32[384,384]{1,0:T(8,128)}, f32[384,384]{1,0:T(8,128)}, bf16[768,2048]{1,0:T(8,128)(2,1)}) custom-call(s32[1]{0:T(128)} %bitcast.s_ref, bf16[384,1024]{1,0:T(8,128)(2,1)S(1)} %collective-permute-done.4.rows_ref.refs_6_, f32[768,384]{1,0:T(8,128)} %get-tuple-element.43.gate_in, ...), custom_call_target="tpu_custom_call" | custom-call | flops 1 | bytes 1 | tf_op jit(solution)/shard_map/pallas_call | solution.py:49
  94.6 11.4 %collective-permute-done.3.rows_ref.refs_7_ = bf16[384,1024]{1,0:T(8,128)(2,1)S(1)} collective-permute-done((bf16[384,1024]{1,0:T(8,128)(2,1)S(1)}, bf16[384,1024]{1,0:T(8,128)(2,1)S(1)}, u32[]{:S(2)}, u32[]{:S(2)}) %collective-permute-start.3) | collective-permute-done | bytes 786464 | tf_op jit(solution)/shard_map/ppermute | solution.py:26
  105.9 4.5 %shard_map.122 = (bf16[384,384]{1,0:T(8,128)(2,1)}, f32[384,384]{1,0:T(8,128)}, f32[384,384]{1,0:T(8,128)}, bf16[768,2048]{1,0:T(8,128)(2,1)}) custom-call(s32[1]{0:T(128)} %bitcast.s_ref, bf16[384,1024]{1,0:T(8,128)(2,1)S(1)} %collective-permute-done.3.rows_ref.refs_7_, f32[768,384]{1,0:T(8,128)} %get-tuple-element.43.gate_in, ...), custom_call_target="tpu_custom_call", output_to_operand_aliasing={{3}: (13, {})} | custom-call | flops 1 | bytes 1 | tf_op jit(solution)/shard_map/pallas_call | solution.py:49
  111.3 7.5 %all-to-all-start.2 = ((bf16[32,24,2048]{2,1,0:T(8,128)(2,1)}), bf16[32,24,2048]{2,1,0:T(8,128)(2,1)}, u32[]{:S(2)}, u32[]{:S(2)}) async-start(bf16[32,24,2048]{2,1,0:T(8,128)(2,1)} %bitcast.102), calls=%async_computation.2 | async-start | bytes 6291456 | tf_op jit(solution)/shard_map/all_to_all | solution.py:36
  118.8 5.0 %shard_map.124 = (bf16[384,384]{1,0:T(8,128)(2,1)}, bf16[384,384]{1,0:T(8,128)(2,1)}, bf16[384,1024]{1,0:T(8,128)(2,1)}) custom-call(s32[1]{0:T(128)} %bitcast.s_ref, bf16[768,2048]{1,0:T(8,128)(2,1)} %bitcast.18.grad_ref.refs_9_, f32[384,384]{1,0:T(8,128)} %get-tuple-element.50.gate_slope, f32[384,384]{1,0:T(8,128)} %get-tuple-element.51.up_slope, ...), custom_call_target="tpu_custom_call" | custom-call | flops 1 | bytes 1 | tf_op jit(solution)/shard_map/pallas_call | solution.py:49
  125.2 5.2 %shard_map.123 = (bf16[384,384]{1,0:T(8,128)(2,1)}, bf16[384,384]{1,0:T(8,128)(2,1)}, bf16[384,1024]{1,0:T(8,128)(2,1)}) custom-call(s32[1]{0:T(128)} %bitcast.s_ref, bf16[768,2048]{1,0:T(8,128)(2,1)} %bitcast.18.grad_ref.refs_9_, f32[384,384]{1,0:T(8,128)} %get-tuple-element.46.gate_slope, f32[384,384]{1,0:T(8,128)} %get-tuple-element.47.up_slope, ...), custom_call_target="tpu_custom_call" | custom-call | flops 1 | bytes 1 | tf_op jit(solution)/shard_map/pallas_call | solution.py:49
  132.0 11.5 %shard_map.126 = (bf16[1,384,2048]{2,1,0:T(8,128)(2,1)}, bf16[1,384,2048]{2,1,0:T(8,128)(2,1)}, bf16[1,384,2048]{2,1,0:T(8,128)(2,1)}) custom-call(s32[1]{0:T(128)} %bitcast.s_ref, bf16[384,384]{1,0:T(8,128)(2,1)} %get-tuple-element.52.grad_gate.refs_0_, bf16[384,384]{1,0:T(8,128)(2,1)} %get-tuple-element.55.refs_1_.grad_gate, ...), custom_call_target="tpu_custom_call" | custom-call | flops 1 | bytes 1 | tf_op jit(solution)/shard_map/pallas_call | solution.py:49
  144.4 3.0 %shard_map.125.refs_8_ = bf16[768,1024]{1,0:T(8,128)(2,1)} custom-call(s32[1]{0:T(128)} %bitcast.s_ref, bf16[384,384]{1,0:T(8,128)(2,1)} %get-tuple-element.52.grad_gate.refs_0_, bf16[384,384]{1,0:T(8,128)(2,1)} %get-tuple-element.53.grad_up.refs_2_, bf16[384,1024]{1,0:T(8,128)(2,1)S(1)} %collective-permute-done.6.swapped, bf16[384,2048]{1,0:T(8,128)(2,1)S(1)} %bitcast.57, ...), custom_call_target="tpu_custom_call" | custom-call | flops 1 | bytes 1 | tf_op jit(solution)/shard_map/pallas_call | solution.py:49
  147.4 11.1 %all-to-all-done.2 = bf16[32,24,2048]{2,1,0:T(8,128)(2,1)} async-done(((bf16[32,24,2048]{2,1,0:T(8,128)(2,1)}), bf16[32,24,2048]{2,1,0:T(8,128)(2,1)}, u32[]{:S(2)}, u32[]{:S(2)}) %all-to-all-start.2) | async-done | bytes 3145760 | tf_op jit(solution)/shard_map/all_to_all | solution.py:36
  158.5 4.7 %shard_map.127 = f32[256,2048]{1,0:T(8,128)} custom-call(s32[1]{0:T(128)} %bitcast.s_ref, bf16[512,768]{1,0:T(8,128)(2,1)} %pad_maximum_fusion.weight_ref, bf16[768,2048]{1,0:T(8,128)(2,1)} %bitcast.27.rows_ref), custom_call_target="tpu_custom_call" | custom-call | flops 1 | bytes 1 | tf_op jit(solution)/shard_map/pallas_call | solution.py:49
  163.2 3.2 %shard_map.128 = bf16[768,1024]{1,0:T(8,128)(2,1)} custom-call(s32[1]{0:T(128)} %bitcast.s_ref, bf16[384,384]{1,0:T(8,128)(2,1)} %get-tuple-element.55.refs_1_.grad_gate, bf16[384,384]{1,0:T(8,128)(2,1)} %get-tuple-element.56.refs_3_.grad_up, bf16[384,1024]{1,0:T(8,128)(2,1)} %collective-permute-done.5.swapped, ...), custom_call_target="tpu_custom_call", output_to_operand_aliasing={{}: (12, {})} | custom-call | flops 1 | bytes 1 | tf_op jit(solution)/shard_map/pallas_call | solution.py:49
  166.4 6.1 %all-to-all-start.3 = ((bf16[32,24,1024]{2,1,0:T(8,128)(2,1)}), bf16[32,24,1024]{2,1,0:T(8,128)(2,1)S(1)}, u32[]{:S(2)}, u32[]{:S(2)}) async-start(bf16[32,24,1024]{2,1,0:T(8,128)(2,1)} %bitcast.100), calls=%async_computation.4 | async-start | bytes 3145728 | tf_op jit(solution)/shard_map/all_to_all | solution.py:36
  175.4 4.6 %shard_map.129 = f32[8,256]{1,0:T(8,128)} custom-call(s32[1]{0:T(128)} %bitcast.s_ref, bf16[768,2048]{1,0:T(8,128)(2,1)} %bitcast.27.rows_ref, bf16[256,2048]{1,0:T(8,128)(2,1)} %all-gather.2.cloned.1.call-done.grad_ref, bf16[768,256]{1,0:T(8,128)(2,1)} %copy.17.picked_ref, s32[8,256]{1,0:T(8,128)} %bitcast.106, s32[768,1]{1,0:T(8,128)} %fusion.4.expert_ref), custom_call_target="tpu_custom_call" | custom-call | flops 1 | bytes 1 | tf_op jit(solution)/shard_map/pallas_call | solution.py:49
  181.4 2.4 %collective-permute-done.7 = f32[8,256]{1,0:T(8,128)S(1)} collective-permute-done((f32[8,256]{1,0:T(8,128)}, f32[8,256]{1,0:T(8,128)S(1)}, u32[]{:S(2)}, u32[]{:S(2)}) %collective-permute-start.7) | collective-permute-done | bytes 8224 | tf_op jit(solution)/shard_map/ppermute | solution.py:26
  184.5 10.2 %all-to-all-done.3 = bf16[32,24,1024]{2,1,0:T(8,128)(2,1)S(1)} async-done(((bf16[32,24,1024]{2,1,0:T(8,128)(2,1)}), bf16[32,24,1024]{2,1,0:T(8,128)(2,1)S(1)}, u32[]{:S(2)}, u32[]{:S(2)}) %all-to-all-start.3) | async-done | bytes 1572896 | tf_op jit(solution)/shard_map/all_to_all | solution.py:36
  196.0 2.1 collective-permute-start.9
  198.1 4.7 %collective-permute-start.10 = (bf16[288,256]{1,0:T(8,128)(2,1)}, bf16[288,256]{1,0:T(8,128)(2,1)S(1)}, u32[]{:S(2)}, u32[]{:S(2)}) collective-permute-start(bf16[288,256]{1,0:T(8,128)(2,1)} %get-tuple-element.75), channel_id=1, source_target_pairs={{0,4},{1,5},{2,6},{3,7},{4,0},{5,1},{6,2},{7,3},{8,12},{9,13},{10,... | collective-permute-start | bytes 442376 | tf_op jit(solution)/shard_map/ppermute | solution.py:22
  204.4 4.4 %collective-permute-done.9 = bf16[288,256]{1,0:T(8,128)(2,1)S(1)} collective-permute-done((bf16[288,256]{1,0:T(8,128)(2,1)}, bf16[288,256]{1,0:T(8,128)(2,1)S(1)}, u32[]{:S(2)}, u32[]{:S(2)}) %collective-permute-start.9) | collective-permute-done | bytes 147488 | tf_op jit(solution)/shard_map/ppermute | solution.py:22
  208.9 6.4 %collective-permute-done.10 = bf16[288,256]{1,0:T(8,128)(2,1)S(1)} collective-permute-done((bf16[288,256]{1,0:T(8,128)(2,1)}, bf16[288,256]{1,0:T(8,128)(2,1)S(1)}, u32[]{:S(2)}, u32[]{:S(2)}) %collective-permute-start.10) | collective-permute-done | bytes 147488 | tf_op jit(solution)/shard_map/ppermute | solution.py:22
  (94 shorter events, 26.9 us)
Async XLA Ops:
  7.2 48.0 %all-gather.2.cloned.1.call-start = ((), (), s32[]{:S(2)}) async-start(), calls=%async_computation.5 | async-start | bytes 1179648 | tf_op jit(solution)/shard_map/all_gather | solution.py:234
  7.2 14.1 %collective-permute-start = (bf16[256,256]{1,0:T(8,128)(2,1)}, bf16[256,256]{1,0:T(8,128)(2,1)S(1)}, u32[]{:S(2)}, u32[]{:S(2)}) collective-permute-start(bf16[256,256]{1,0:T(8,128)(2,1)} %refs_0_.1), channel_id=1, source_target_pairs={{0,2},{1,3},{2,4},{3,5},{4,6},{5,7},{6,0},{7,1},{8,10},{9,11},{10,... | collective-permute-start | bytes 393224 | tf_op jit(solution)/shard_map/ppermute | solution.py:22
  10.6 14.5 %collective-permute-start.1 = (bf16[256,256]{1,0:T(8,128)(2,1)}, bf16[256,256]{1,0:T(8,128)(2,1)S(1)}, u32[]{:S(2)}, u32[]{:S(2)}) collective-permute-start(bf16[256,256]{1,0:T(8,128)(2,1)} %refs_0_.1), channel_id=1, source_target_pairs={{0,4},{1,5},{2,6},{3,7},{4,0},{5,1},{6,2},{7,3},{8,12},{9,13},{10,... | collective-permute-start | bytes 393224 | tf_op jit(solution)/shard_map/ppermute | solution.py:22
  15.9 12.4 %collective-permute-start.2 = (bf16[256,256]{1,0:T(8,128)(2,1)}, bf16[256,256]{1,0:T(8,128)(2,1)S(1)}, u32[]{:S(2)}, u32[]{:S(2)}) collective-permute-start(bf16[256,256]{1,0:T(8,128)(2,1)} %refs_0_.1), channel_id=1, source_target_pairs={{0,6},{1,7},{2,0},{3,1},{4,2},{5,3},{6,4},{7,5},{8,14},{9,15},{10,... | collective-permute-start | bytes 393224 | tf_op jit(solution)/shard_map/ppermute | solution.py:22
  19.6 18.2 %copy-start.17 = (s32[256,1]{0,1:T(1,128)}, s32[256,1]{0,1:T(1,128)S(1)}, u32[]{:S(2)}) copy-start(s32[256,1]{0,1:T(1,128)S(1)} %get-tuple-element.101) | copy-start | bytes 3076
  19.7 18.2 %copy-start.19 = (s32[256,1]{0,1:T(1,128)}, s32[256,1]{0,1:T(1,128)S(1)}, u32[]{:S(2)}) copy-start(s32[256,1]{0,1:T(1,128)S(1)} %get-tuple-element.102) | copy-start | bytes 3076
  19.7 18.2 %copy-start.21 = (s32[256,1]{0,1:T(1,128)}, s32[256,1]{0,1:T(1,128)S(1)}, u32[]{:S(2)}) copy-start(s32[256,1]{0,1:T(1,128)S(1)} %get-tuple-element.103) | copy-start | bytes 3076
  19.7 18.2 %copy-start.23 = (s32[256,1]{0,1:T(1,128)}, s32[256,1]{0,1:T(1,128)S(1)}, u32[]{:S(2)}) copy-start(s32[256,1]{0,1:T(1,128)S(1)} %get-tuple-element.104) | copy-start | bytes 3076
  19.7 18.2 %copy-start.25 = (s32[256,1]{0,1:T(1,128)}, s32[256,1]{0,1:T(1,128)S(1)}, u32[]{:S(2)}) copy-start(s32[256,1]{0,1:T(1,128)S(1)} %get-tuple-element.105) | copy-start | bytes 3076
  19.7 8.6 %copy-start.12 = (bf16[256,256]{1,0:T(8,128)(2,1)S(1)}, bf16[256,256]{1,0:T(8,128)(2,1)}, u32[]{:S(2)}) copy-start(bf16[256,256]{1,0:T(8,128)(2,1)} %refs_0_.1) | copy-start | bytes 393220
  21.3 8.8 %copy-start.6 = (bf16[256,768]{1,0:T(8,128)(2,1)}, bf16[256,768]{1,0:T(8,128)(2,1)S(1)}, u32[]{:S(2)}) copy-start(bf16[256,768]{1,0:T(8,128)(2,1)S(1)} %get-tuple-element.106.select_ref) | copy-start | bytes 1179652
  21.3 16.6 %copy-start.14 = (pred[256,768]{1,0:T(8,128)(4,1)}, pred[256,768]{1,0:T(8,128)(4,1)S(1)}, u32[]{:S(2)}) copy-start(pred[256,768]{1,0:T(8,128)(4,1)S(1)} %get-tuple-element.107) | copy-start | bytes 589828
  30.1 7.8 %copy-start.27 = (f32[256,8]{0,1:T(8,128)S(1)}, f32[256,8]{0,1:T(8,128)}, u32[]{:S(2)}) copy-start(f32[256,8]{0,1:T(8,128)} %param.9) | copy-start | bytes 24580
  30.1 29.8 %all-to-all-start.1 = ((bf16[32,24,1024]{2,1,0:T(8,128)(2,1)}), bf16[32,24,1024]{2,1,0:T(8,128)(2,1)S(1)}, u32[]{:S(2)}, u32[]{:S(2)}) async-start(bf16[32,24,1024]{2,1,0:T(8,128)(2,1)} %bitcast.103), calls=%async_computation.1 | async-start | bytes 3145728 | tf_op jit(solution)/shard_map/all_to_all | solution.py:36
  61.1 50.3 %all-to-all-start = ((bf16[32,24,2048]{2,1,0:T(8,128)(2,1)}), bf16[32,24,2048]{2,1,0:T(8,128)(2,1)}, u32[]{:S(2)}, u32[]{:S(2)}) async-start(bf16[32,24,2048]{2,1,0:T(8,128)(2,1)} %bitcast.101), calls=%async_computation | async-start | bytes 6291456 | tf_op jit(solution)/shard_map/all_to_all | solution.py:36
  69.4 20.5 %collective-permute-start.4 = (bf16[384,1024]{1,0:T(8,128)(2,1)S(1)}, bf16[384,1024]{1,0:T(8,128)(2,1)S(1)}, u32[]{:S(2)}, u32[]{:S(2)}) collective-permute-start(bf16[384,1024]{1,0:T(8,128)(2,1)S(1)} %bitcast.105), channel_id=1, source_target_pairs={{0,1},{1,0},{2,3},{3,2},{4,5},{5,4},{6,7},{7,6},{8,9},{9,8},{10,11... | collective-permute-start | bytes 2359304 | tf_op jit(solution)/shard_map/ppermute | solution.py:26
  70.9 35.1 %collective-permute-start.3 = (bf16[384,1024]{1,0:T(8,128)(2,1)S(1)}, bf16[384,1024]{1,0:T(8,128)(2,1)S(1)}, u32[]{:S(2)}, u32[]{:S(2)}) collective-permute-start(bf16[384,1024]{1,0:T(8,128)(2,1)S(1)} %bitcast.104), channel_id=1, source_target_pairs={{0,1},{1,0},{2,3},{3,2},{4,5},{5,4},{6,7},{7,6},{8,9},{9,8},{10,11... | collective-permute-start | bytes 2359304 | tf_op jit(solution)/shard_map/ppermute | solution.py:26
  72.9 16.9 %copy-start.5 = (bf16[1,384,2048]{2,1,0:T(8,128)(2,1)S(1)}, bf16[1,384,2048]{2,1,0:T(8,128)(2,1)}, u32[]{:S(2)}) copy-start(bf16[1,384,2048]{2,1,0:T(8,128)(2,1)} %param.12) | copy-start | bytes 4718596
  111.3 47.2 %all-to-all-start.2 = ((bf16[32,24,2048]{2,1,0:T(8,128)(2,1)}), bf16[32,24,2048]{2,1,0:T(8,128)(2,1)}, u32[]{:S(2)}, u32[]{:S(2)}) async-start(bf16[32,24,2048]{2,1,0:T(8,128)(2,1)} %bitcast.102), calls=%async_computation.2 | async-start | bytes 6291456 | tf_op jit(solution)/shard_map/all_to_all | solution.py:36
  118.8 96.5 %reduce-scatter.2.cloned.1.call-start = ((), (), s32[]{:S(2)}) async-start(), calls=%async_computation.6 | async-start | bytes 2359296 | tf_op jit(solution)/shard_map/reduce_scatter | solution.py:389
  123.8 20.6 %collective-permute-start.6 = (bf16[384,1024]{1,0:T(8,128)(2,1)}, bf16[384,1024]{1,0:T(8,128)(2,1)S(1)}, u32[]{:S(2)}, u32[]{:S(2)}) collective-permute-start(bf16[384,1024]{1,0:T(8,128)(2,1)} %get-tuple-element.54), channel_id=1, source_target_pairs={{0,1},{1,0},{2,3},{3,2},{4,5},{5,4},{6,7},{7,6},{8,9},{9,8},{10,11... | collective-permute-start | bytes 2359304 | tf_op jit(solution)/shard_map/ppermute | solution.py:26
  125.2 6.8 %copy-start.9 = (bf16[384,1024]{1,0:T(8,128)(2,1)S(1)}, bf16[384,1024]{1,0:T(8,128)(2,1)}, u32[]{:S(2)}) copy-start(bf16[384,1024]{1,0:T(8,128)(2,1)} %copy-done.8) | copy-start | bytes 2359300
  125.2 6.8 %copy-start.11 = (bf16[384,1024]{1,0:T(8,128)(2,1)S(1)}, bf16[384,1024]{1,0:T(8,128)(2,1)}, u32[]{:S(2)}) copy-start(bf16[384,1024]{1,0:T(8,128)(2,1)} %copy-done.10) | copy-start | bytes 2359300
  130.4 32.8 %collective-permute-start.5 = (bf16[384,1024]{1,0:T(8,128)(2,1)}, bf16[384,1024]{1,0:T(8,128)(2,1)}, u32[]{:S(2)}, u32[]{:S(2)}) collective-permute-start(bf16[384,1024]{1,0:T(8,128)(2,1)} %get-tuple-element.48), channel_id=1, source_target_pairs={{0,1},{1,0},{2,3},{3,2},{4,5},{5,4},{6,7},{7,6},{8,9},{9,8},{10,11... | collective-permute-start | bytes 2359304 | tf_op jit(solution)/shard_map/ppermute | solution.py:26
  166.4 6.2 %copy-start.24 = (s32[256,1]{0,1:T(1,128)S(1)}, s32[256,1]{0,1:T(1,128)}, u32[]{:S(2)}) copy-start(s32[256,1]{0,1:T(1,128)} %copy-done.23) | copy-start | bytes 3076
  166.4 28.3 %all-to-all-start.3 = ((bf16[32,24,1024]{2,1,0:T(8,128)(2,1)}), bf16[32,24,1024]{2,1,0:T(8,128)(2,1)S(1)}, u32[]{:S(2)}, u32[]{:S(2)}) async-start(bf16[32,24,1024]{2,1,0:T(8,128)(2,1)} %bitcast.100), calls=%async_computation.4 | async-start | bytes 3145728 | tf_op jit(solution)/shard_map/all_to_all | solution.py:36
  175.4 19.3 %copy-start.7 = (bf16[256,768]{1,0:T(8,128)(2,1)S(1)}, bf16[256,768]{1,0:T(8,128)(2,1)}, u32[]{:S(2)}) copy-start(bf16[256,768]{1,0:T(8,128)(2,1)} %copy-done.6) | copy-start | bytes 1179652
  179.9 3.9 %collective-permute-start.7 = (f32[8,256]{1,0:T(8,128)}, f32[8,256]{1,0:T(8,128)S(1)}, u32[]{:S(2)}, u32[]{:S(2)}) collective-permute-start(f32[8,256]{1,0:T(8,128)} %shard_map.129), channel_id=1, source_target_pairs={{0,1},{1,0},{2,3},{3,2},{4,5},{5,4},{6,7},{7,6},{8,9},{9,8},{10,11... | collective-permute-start | bytes 24584 | tf_op jit(solution)/shard_map/ppermute | solution.py:26
  196.0 21.6 %copy-start.16 = (f32[256,256]{1,0:T(8,128)S(1)}, f32[256,256]{1,0:T(8,128)}, u32[]{:S(2)}) copy-start(f32[256,256]{1,0:T(8,128)} %get-tuple-element.73) | copy-start | bytes 786436
  196.0 12.8 %collective-permute-start.9 = (bf16[288,256]{1,0:T(8,128)(2,1)}, bf16[288,256]{1,0:T(8,128)(2,1)S(1)}, u32[]{:S(2)}, u32[]{:S(2)}) collective-permute-start(bf16[288,256]{1,0:T(8,128)(2,1)} %get-tuple-element.74), channel_id=1, source_target_pairs={{0,2},{1,3},{2,4},{3,5},{4,6},{5,7},{6,0},{7,1},{8,10},{9,11},{10,... | collective-permute-start | bytes 442376 | tf_op jit(solution)/shard_map/ppermute | solution.py:22
  198.1 17.1 %collective-permute-start.10 = (bf16[288,256]{1,0:T(8,128)(2,1)}, bf16[288,256]{1,0:T(8,128)(2,1)S(1)}, u32[]{:S(2)}, u32[]{:S(2)}) collective-permute-start(bf16[288,256]{1,0:T(8,128)(2,1)} %get-tuple-element.75), channel_id=1, source_target_pairs={{0,4},{1,5},{2,6},{3,7},{4,0},{5,1},{6,2},{7,3},{8,12},{9,13},{10,... | collective-permute-start | bytes 442376 | tf_op jit(solution)/shard_map/ppermute | solution.py:22
  202.8 14.1 %collective-permute-start.8 = (bf16[288,256]{1,0:T(8,128)(2,1)}, bf16[288,256]{1,0:T(8,128)(2,1)S(1)}, u32[]{:S(2)}, u32[]{:S(2)}) collective-permute-start(bf16[288,256]{1,0:T(8,128)(2,1)} %get-tuple-element.71), channel_id=1, source_target_pairs={{0,6},{1,7},{2,0},{3,1},{4,2},{5,3},{6,4},{7,5},{8,14},{9,15},{10,... | collective-permute-start | bytes 442376 | tf_op jit(solution)/shard_map/ppermute | solution.py:22
  (13 other events, 54.0 us)
Sparse Core Ops, SparseCore 0:
  18.8 36.3 all-gather.1
  163.3 41.1 reduce-scatter.1

commit v4 on v3

--- a/solution.py
+++ b/solution.py
@@ -9,7 +9,7 @@
 
 EXP_DEV = 4
 ROW_CUTS = 2
-SWAP_CUTS = 2
+SWAP_CUTS = 3
 VMEM_BYTES = 28 * 1024 * 1024
 F32 = jnp.float32
 BF16 = jnp.bfloat16

time: 227 us -> 225 us (level)
  waiting for transfers between devices: 82.8 us -> 73.6 us
  Pallas kernels: 56.3 us -> 61.3 us
  starting transfers between devices: 53.4 us -> 56 us
    pallas_call x13 -> x16, Pallas kernels: 56.3 us -> 61.3 us  [call(): pl.pallas_call(body, grid_spec=pltpu.PrefetchScalarGridSpec(num_scalar_pr...]
    ppermute x5 -> x7, waiting for transfers between devices: 28.5 us -> 23.6 us  [swap(): return lax.ppermute(value, 'etp', [(i, i ^ 1) for i in range(lanes)])]
    all_to_all x4, waiting for transfers between devices: 22.2 us -> 17.8 us  [across(): lax.all_to_all(cut, 'expert', split_axis=0, concat_axis=0, tiled=True)]
    ppermute x5 -> x7, starting transfers between devices: 5.57 us -> 8.23 us  [swap(): return lax.ppermute(value, 'etp', [(i, i ^ 1) for i in range(lanes)])]
  transfers between devices with their start and end apart: 17 -> 19, of which waited for: 12 -> 12; matrix products, arithmetic and copies ran while one was open for 6% -> 6% of each run, Pallas kernels for 25% -> 27%
where the time goes in v4:
time: 225 us; the launch traced here: 223 us
  waiting for transfers between devices  73.6 us (33%)
  Pallas kernels  61.3 us (27%)
  starting transfers between devices  56 us (25%)
  between operations  14.4 us (6%)
  other arithmetic  8.58 us (4%)
  local copies, waits for them, and re-layouts  7.97 us (4%)
    pallas_call x16, Pallas kernels, call(): pl.pallas_call(body, grid_spec=pltpu.PrefetchScalarGridSpec(num_scalar_pr...  61.3 us
    all_to_all x4, starting transfers between devices, across(): lax.all_to_all(cut, 'expert', split_axis=0, concat_axis=0, tiled=True)  27.9 us
    ppermute x7, waiting for transfers between devices, swap(): return lax.ppermute(value, 'etp', [(i, i ^ 1) for i in range(lanes)])  23.6 us
    ppermute x6, starting transfers between devices, shift(): lax.ppermute(value, 'etp', [(i, (i + step) % lanes) for i in range(lanes)])  19.8 us
    ppermute x6, waiting for transfers between devices, shift(): lax.ppermute(value, 'etp', [(i, (i + step) % lanes) for i in range(lanes)])  17.8 us
    all_to_all x4, waiting for transfers between devices, across(): lax.all_to_all(cut, 'expert', split_axis=0, concat_axis=0, tiled=True)  17.8 us
    all_gather x1, waiting for transfers between devices, per_device(): grad_full = lax.all_gather(grad_out, 'etp', axis=1, tiled=True)  14.2 us
    ppermute x7, starting transfers between devices, swap(): return lax.ppermute(value, 'etp', [(i, i ^ 1) for i in range(lanes)])  8.23 us
  transfers between devices with their start and end apart: 19, of which 12 were waited for; matrix products, arithmetic and copies ran while one was open for 6% of the time, Pallas kernels for 27%

profile of v4, /device:TPU:2, one launch (start us, length us, event | category | flops | bytes accessed | tf_op | source)
XLA Modules:
  0.0 223.4 jit_solution(7807910473521904952)
XLA Ops:
  7.2 3.3 %collective-permute-start = (bf16[256,256]{1,0:T(8,128)(2,1)}, bf16[256,256]{1,0:T(8,128)(2,1)S(1)}, u32[]{:S(2)}, u32[]{:S(2)}) collective-permute-start(bf16[256,256]{1,0:T(8,128)(2,1)} %refs_0_.1), channel_id=1, source_target_pairs={{0,2},{1,3},{2,4},{3,5},{4,6},{5,7},{6,0},{7,1},{8,10},{9,11},{10,... | collective-permute-start | bytes 393224 | tf_op jit(solution)/shard_map/ppermute | solution.py:22
  10.6 5.4 %collective-permute-start.1 = (bf16[256,256]{1,0:T(8,128)(2,1)}, bf16[256,256]{1,0:T(8,128)(2,1)S(1)}, u32[]{:S(2)}, u32[]{:S(2)}) collective-permute-start(bf16[256,256]{1,0:T(8,128)(2,1)} %refs_0_.1), channel_id=1, source_target_pairs={{0,4},{1,5},{2,6},{3,7},{4,0},{5,1},{6,2},{7,3},{8,12},{9,13},{10,... | collective-permute-start | bytes 393224 | tf_op jit(solution)/shard_map/ppermute | solution.py:22
  15.9 2.7 %collective-permute-start.2 = (bf16[256,256]{1,0:T(8,128)(2,1)}, bf16[256,256]{1,0:T(8,128)(2,1)S(1)}, u32[]{:S(2)}, u32[]{:S(2)}) collective-permute-start(bf16[256,256]{1,0:T(8,128)(2,1)} %refs_0_.1), channel_id=1, source_target_pairs={{0,6},{1,7},{2,0},{3,1},{4,2},{5,3},{6,4},{7,5},{8,14},{9,15},{10,... | collective-permute-start | bytes 393224 | tf_op jit(solution)/shard_map/ppermute | solution.py:22
  21.3 3.8 %collective-permute-done.1.refs_2_ = bf16[256,256]{1,0:T(8,128)(2,1)S(1)} collective-permute-done((bf16[256,256]{1,0:T(8,128)(2,1)}, bf16[256,256]{1,0:T(8,128)(2,1)S(1)}, u32[]{:S(2)}, u32[]{:S(2)}) %collective-permute-start.1) | collective-permute-done | bytes 131104 | tf_op jit(solution)/shard_map/ppermute | solution.py:22
  25.1 3.3 %collective-permute-done.2.refs_3_ = bf16[256,256]{1,0:T(8,128)(2,1)S(1)} collective-permute-done((bf16[256,256]{1,0:T(8,128)(2,1)}, bf16[256,256]{1,0:T(8,128)(2,1)S(1)}, u32[]{:S(2)}, u32[]{:S(2)}) %collective-permute-start.2) | collective-permute-done | bytes 131104 | tf_op jit(solution)/shard_map/ppermute | solution.py:22
  30.1 7.8 %all-to-all-start.1 = ((bf16[32,24,1024]{2,1,0:T(8,128)(2,1)}), bf16[32,24,1024]{2,1,0:T(8,128)(2,1)S(1)}, u32[]{:S(2)}, u32[]{:S(2)}) async-start(bf16[32,24,1024]{2,1,0:T(8,128)(2,1)} %bitcast.128), calls=%async_computation.1 | async-start | bytes 3145728 | tf_op jit(solution)/shard_map/all_to_all | solution.py:36
  40.9 14.2 %all-gather.2.cloned.1.call-done.grad_ref = bf16[256,2048]{1,0:T(8,128)(2,1)} async-done(((bf16[256,256]{1,0:T(8,128)(2,1)}), bf16[256,2048]{1,0:T(8,128)(2,1)}) %all-gather.2.cloned.1.call-update) | async-done | bytes 1048592 | tf_op jit(solution)/shard_map/all_gather | solution.py:234
  55.2 3.8 %shard_map.118 = bf16[768,2048]{1,0:T(8,128)(2,1)} custom-call(s32[1]{0:T(128)} %bitcast.s_ref, bf16[256,768]{1,0:T(8,128)(2,1)} %copy-done.6, bf16[256,2048]{1,0:T(8,128)(2,1)} %all-gather.2.cloned.1.call-done.grad_ref, f32[768,1]{1,0:T(8,128)} %broadcast_in_dim.85.weight_ref), custom_call_target="tpu_custom_call" | custom-call | flops 1 | bytes 1 | tf_op jit(solution)/shard_map/pallas_call | solution.py:49
  61.1 6.6 %all-to-all-start = ((bf16[32,24,2048]{2,1,0:T(8,128)(2,1)}), bf16[32,24,2048]{2,1,0:T(8,128)(2,1)}, u32[]{:S(2)}, u32[]{:S(2)}) async-start(bf16[32,24,2048]{2,1,0:T(8,128)(2,1)} %bitcast.127), calls=%async_computation | async-start | bytes 6291456 | tf_op jit(solution)/shard_map/all_to_all | solution.py:36
  74.2 3.1 %shard_map.120 = (f32[768,384]{1,0:T(8,128)}, f32[768,384]{1,0:T(8,128)}) custom-call(s32[1]{0:T(128)} %bitcast.s_ref, bf16[768,1024]{1,0:T(8,128)(2,1)S(1)} %bitcast.122, bf16[384,2048]{1,0:T(8,128)(2,1)S(1)} %bitcast.35, bf16[384,2048]{1,0:T(8,128)(2,1)S(1)} %bitcast.36, bf16[384,2048]{1,0:T(8,128)(2,1)S(1)} %bitcast.37, bf16[384,2048]{1,0:T(8,128)(2,1)S(1)} %bitcast.38, ...), custom_call_target="tpu_custom_call" | custom-call | flops 1 | bytes 1 | tf_op jit(solution)/shard_map/pallas_call | solution.py:49
  77.3 6.8 %collective-permute-done.5.rows_ref.refs_9_ = bf16[256,1024]{1,0:T(8,128)(2,1)S(1)} collective-permute-done((bf16[256,1024]{1,0:T(8,128)(2,1)S(1)}, bf16[256,1024]{1,0:T(8,128)(2,1)S(1)}, u32[]{:S(2)}, u32[]{:S(2)}) %collective-permute-start.5) | collective-permute-done | bytes 524320 | tf_op jit(solution)/shard_map/ppermute | solution.py:26
  84.2 3.7 %shard_map.121 = (bf16[256,384]{1,0:T(8,128)(2,1)}, f32[256,384]{1,0:T(8,128)}, f32[256,384]{1,0:T(8,128)}, bf16[768,2048]{1,0:T(8,128)(2,1)}) custom-call(s32[1]{0:T(128)} %bitcast.s_ref, bf16[256,1024]{1,0:T(8,128)(2,1)S(1)} %collective-permute-done.5.rows_ref.refs_9_, f32[768,384]{1,0:T(8,128)} %get-tuple-element.50.gate_in, ...), custom_call_target="tpu_custom_call" | custom-call | flops 1 | bytes 1 | tf_op jit(solution)/shard_map/pallas_call | solution.py:49
  87.9 7.5 %collective-permute-done.4.rows_ref.refs_10_ = bf16[256,1024]{1,0:T(8,128)(2,1)S(1)} collective-permute-done((bf16[256,1024]{1,0:T(8,128)(2,1)S(1)}, bf16[256,1024]{1,0:T(8,128)(2,1)S(1)}, u32[]{:S(2)}, u32[]{:S(2)}) %collective-permute-start.4) | collective-permute-done | bytes 524320 | tf_op jit(solution)/shard_map/ppermute | solution.py:26
  95.4 3.8 %shard_map.122 = (bf16[256,384]{1,0:T(8,128)(2,1)}, f32[256,384]{1,0:T(8,128)}, f32[256,384]{1,0:T(8,128)}, bf16[768,2048]{1,0:T(8,128)(2,1)}) custom-call(s32[1]{0:T(128)} %bitcast.s_ref, bf16[256,1024]{1,0:T(8,128)(2,1)S(1)} %collective-permute-done.4.rows_ref.refs_10_, f32[768,384]{1,0:T(8,128)} %get-tuple-element.50.gate_in, ...), custom_call_target="tpu_custom_call", output_to_operand_aliasing={{3}: (13, {})} | custom-call | flops 1 | bytes 1 | tf_op jit(solution)/shard_map/pallas_call | solution.py:49
  99.2 6.6 %collective-permute-done.3.rows_ref.refs_11_ = bf16[256,1024]{1,0:T(8,128)(2,1)S(1)} collective-permute-done((bf16[256,1024]{1,0:T(8,128)(2,1)S(1)}, bf16[256,1024]{1,0:T(8,128)(2,1)S(1)}, u32[]{:S(2)}, u32[]{:S(2)}) %collective-permute-start.3) | collective-permute-done | bytes 524320 | tf_op jit(solution)/shard_map/ppermute | solution.py:26
  105.8 3.5 %shard_map.123 = (bf16[256,384]{1,0:T(8,128)(2,1)}, f32[256,384]{1,0:T(8,128)}, f32[256,384]{1,0:T(8,128)}, bf16[768,2048]{1,0:T(8,128)(2,1)}) custom-call(s32[1]{0:T(128)} %bitcast.s_ref, bf16[256,1024]{1,0:T(8,128)(2,1)S(1)} %collective-permute-done.3.rows_ref.refs_11_, f32[768,384]{1,0:T(8,128)} %get-tuple-element.50.gate_in, ...), custom_call_target="tpu_custom_call", output_to_operand_aliasing={{3}: (13, {})} | custom-call | flops 1 | bytes 1 | tf_op jit(solution)/shard_map/pallas_call | solution.py:49
  110.1 7.5 %all-to-all-start.2 = ((bf16[32,24,2048]{2,1,0:T(8,128)(2,1)}), bf16[32,24,2048]{2,1,0:T(8,128)(2,1)}, u32[]{:S(2)}, u32[]{:S(2)}) async-start(bf16[32,24,2048]{2,1,0:T(8,128)(2,1)} %bitcast.125), calls=%async_computation.2 | async-start | bytes 6291456 | tf_op jit(solution)/shard_map/all_to_all | solution.py:36
  117.6 4.2 %shard_map.126 = (bf16[256,384]{1,0:T(8,128)(2,1)}, bf16[256,384]{1,0:T(8,128)(2,1)}, bf16[256,1024]{1,0:T(8,128)(2,1)}) custom-call(s32[1]{0:T(128)} %bitcast.s_ref, bf16[768,2048]{1,0:T(8,128)(2,1)} %bitcast.18.grad_ref.refs_13_, f32[256,384]{1,0:T(8,128)} %get-tuple-element.63.gate_slope, f32[256,384]{1,0:T(8,128)} %get-tuple-element.64.up_slope, ...), custom_call_target="tpu_custom_call" | custom-call | flops 1 | bytes 1 | tf_op jit(solution)/shard_map/pallas_call | solution.py:49
  123.1 4.2 %shard_map.125 = (bf16[256,384]{1,0:T(8,128)(2,1)}, bf16[256,384]{1,0:T(8,128)(2,1)}, bf16[256,1024]{1,0:T(8,128)(2,1)}) custom-call(s32[1]{0:T(128)} %bitcast.s_ref, bf16[768,2048]{1,0:T(8,128)(2,1)} %bitcast.18.grad_ref.refs_13_, f32[256,384]{1,0:T(8,128)} %get-tuple-element.58.gate_slope, f32[256,384]{1,0:T(8,128)} %get-tuple-element.59.up_slope, ...), custom_call_target="tpu_custom_call" | custom-call | flops 1 | bytes 1 | tf_op jit(solution)/shard_map/pallas_call | solution.py:49
  128.0 4.3 %shard_map.124 = (bf16[256,384]{1,0:T(8,128)(2,1)}, bf16[256,384]{1,0:T(8,128)(2,1)}, bf16[256,1024]{1,0:T(8,128)(2,1)}) custom-call(s32[1]{0:T(128)} %bitcast.s_ref, bf16[768,2048]{1,0:T(8,128)(2,1)} %bitcast.18.grad_ref.refs_13_, f32[256,384]{1,0:T(8,128)} %get-tuple-element.54.gate_slope, f32[256,384]{1,0:T(8,128)} %get-tuple-element.55.up_slope, ...), custom_call_target="tpu_custom_call" | custom-call | flops 1 | bytes 1 | tf_op jit(solution)/shard_map/pallas_call | solution.py:49
  134.6 10.8 %shard_map.129 = (bf16[1,384,2048]{2,1,0:T(8,128)(2,1)}, bf16[1,384,2048]{2,1,0:T(8,128)(2,1)}, bf16[1,384,2048]{2,1,0:T(8,128)(2,1)}) custom-call(s32[1]{0:T(128)} %bitcast.s_ref, bf16[256,384]{1,0:T(8,128)(2,1)} %get-tuple-element.65.grad_gate.refs_0_, bf16[256,384]{1,0:T(8,128)(2,1)} %get-tuple-element.60.grad_gate.refs_1_, ...), custom_call_target="tpu_custom_call" | custom-call | flops 1 | bytes 1 | tf_op jit(solution)/shard_map/pallas_call | solution.py:49
  150.5 6.8 %all-to-all-done.2 = bf16[32,24,2048]{2,1,0:T(8,128)(2,1)} async-done(((bf16[32,24,2048]{2,1,0:T(8,128)(2,1)}), bf16[32,24,2048]{2,1,0:T(8,128)(2,1)}, u32[]{:S(2)}, u32[]{:S(2)}) %all-to-all-start.2) | async-done | bytes 3145760 | tf_op jit(solution)/shard_map/all_to_all | solution.py:36
  157.3 4.5 %shard_map.130 = f32[256,2048]{1,0:T(8,128)} custom-call(s32[1]{0:T(128)} %bitcast.s_ref, bf16[512,768]{1,0:T(8,128)(2,1)} %pad_maximum_fusion.weight_ref, bf16[768,2048]{1,0:T(8,128)(2,1)} %bitcast.25.rows_ref), custom_call_target="tpu_custom_call" | custom-call | flops 1 | bytes 1 | tf_op jit(solution)/shard_map/pallas_call | solution.py:49
  161.9 2.7 %shard_map.131 = bf16[768,1024]{1,0:T(8,128)(2,1)} custom-call(s32[1]{0:T(128)} %bitcast.s_ref, bf16[256,384]{1,0:T(8,128)(2,1)} %get-tuple-element.68.refs_2_.grad_gate, bf16[256,384]{1,0:T(8,128)(2,1)} %get-tuple-element.69.refs_5_.grad_up, bf16[256,1024]{1,0:T(8,128)(2,1)} %collective-permute-done.6.swapped, ...), custom_call_target="tpu_custom_call", output_to_operand_aliasing={{}: (12, {})} | custom-call | flops 1 | bytes 1 | tf_op jit(solution)/shard_map/pallas_call | solution.py:49
  164.6 6.1 %all-to-all-start.3 = ((bf16[32,24,1024]{2,1,0:T(8,128)(2,1)}), bf16[32,24,1024]{2,1,0:T(8,128)(2,1)S(1)}, u32[]{:S(2)}, u32[]{:S(2)}) async-start(bf16[32,24,1024]{2,1,0:T(8,128)(2,1)} %bitcast.126), calls=%async_computation.4 | async-start | bytes 3145728 | tf_op jit(solution)/shard_map/all_to_all | solution.py:36
  173.6 4.6 %shard_map.132 = f32[8,256]{1,0:T(8,128)} custom-call(s32[1]{0:T(128)} %bitcast.s_ref, bf16[768,2048]{1,0:T(8,128)(2,1)} %bitcast.25.rows_ref, bf16[256,2048]{1,0:T(8,128)(2,1)} %all-gather.2.cloned.1.call-done.grad_ref, bf16[768,256]{1,0:T(8,128)(2,1)} %copy.19.picked_ref, s32[8,256]{1,0:T(8,128)} %bitcast.129, s32[768,1]{1,0:T(8,128)} %fusion.4.expert_ref), custom_call_target="tpu_custom_call" | custom-call | flops 1 | bytes 1 | tf_op jit(solution)/shard_map/pallas_call | solution.py:49
  179.5 2.6 %collective-permute-done.9 = f32[8,256]{1,0:T(8,128)S(1)} collective-permute-done((f32[8,256]{1,0:T(8,128)}, f32[8,256]{1,0:T(8,128)S(1)}, u32[]{:S(2)}, u32[]{:S(2)}) %collective-permute-start.9) | collective-permute-done | bytes 8224 | tf_op jit(solution)/shard_map/ppermute | solution.py:26
  182.8 10.1 %all-to-all-done.3 = bf16[32,24,1024]{2,1,0:T(8,128)(2,1)S(1)} async-done(((bf16[32,24,1024]{2,1,0:T(8,128)(2,1)}), bf16[32,24,1024]{2,1,0:T(8,128)(2,1)S(1)}, u32[]{:S(2)}, u32[]{:S(2)}) %all-to-all-start.3) | async-done | bytes 1572896 | tf_op jit(solution)/shard_map/all_to_all | solution.py:36
  194.3 4.3 %collective-permute-start.12 = (bf16[288,256]{1,0:T(8,128)(2,1)}, bf16[288,256]{1,0:T(8,128)(2,1)S(1)}, u32[]{:S(2)}, u32[]{:S(2)}) collective-permute-start(bf16[288,256]{1,0:T(8,128)(2,1)} %get-tuple-element.89), channel_id=1, source_target_pairs={{0,4},{1,5},{2,6},{3,7},{4,0},{5,1},{6,2},{7,3},{8,12},{9,13},{10,... | collective-permute-start | bytes 442376 | tf_op jit(solution)/shard_map/ppermute | solution.py:22
  198.5 2.6 %collective-permute-start.11 = (bf16[288,256]{1,0:T(8,128)(2,1)}, bf16[288,256]{1,0:T(8,128)(2,1)S(1)}, u32[]{:S(2)}, u32[]{:S(2)}) collective-permute-start(bf16[288,256]{1,0:T(8,128)(2,1)} %get-tuple-element.88), channel_id=1, source_target_pairs={{0,2},{1,3},{2,4},{3,5},{4,6},{5,7},{6,0},{7,1},{8,10},{9,11},{10,... | collective-permute-start | bytes 442376 | tf_op jit(solution)/shard_map/ppermute | solution.py:22
  202.7 4.2 %collective-permute-done.12 = bf16[288,256]{1,0:T(8,128)(2,1)S(1)} collective-permute-done((bf16[288,256]{1,0:T(8,128)(2,1)}, bf16[288,256]{1,0:T(8,128)(2,1)S(1)}, u32[]{:S(2)}, u32[]{:S(2)}) %collective-permute-start.12) | collective-permute-done | bytes 147488 | tf_op jit(solution)/shard_map/ppermute | solution.py:22
  206.9 6.6 %collective-permute-done.11 = bf16[288,256]{1,0:T(8,128)(2,1)S(1)} collective-permute-done((bf16[288,256]{1,0:T(8,128)(2,1)}, bf16[288,256]{1,0:T(8,128)(2,1)S(1)}, u32[]{:S(2)}, u32[]{:S(2)}) %collective-permute-start.11) | collective-permute-done | bytes 147488 | tf_op jit(solution)/shard_map/ppermute | solution.py:22
  (105 shorter events, 37.2 us)
Async XLA Ops:
  7.2 48.0 %all-gather.2.cloned.1.call-start = ((), (), s32[]{:S(2)}) async-start(), calls=%async_computation.5 | async-start | bytes 1179648 | tf_op jit(solution)/shard_map/all_gather | solution.py:234
  7.2 14.1 %collective-permute-start = (bf16[256,256]{1,0:T(8,128)(2,1)}, bf16[256,256]{1,0:T(8,128)(2,1)S(1)}, u32[]{:S(2)}, u32[]{:S(2)}) collective-permute-start(bf16[256,256]{1,0:T(8,128)(2,1)} %refs_0_.1), channel_id=1, source_target_pairs={{0,2},{1,3},{2,4},{3,5},{4,6},{5,7},{6,0},{7,1},{8,10},{9,11},{10,... | collective-permute-start | bytes 393224 | tf_op jit(solution)/shard_map/ppermute | solution.py:22
  10.6 14.5 %collective-permute-start.1 = (bf16[256,256]{1,0:T(8,128)(2,1)}, bf16[256,256]{1,0:T(8,128)(2,1)S(1)}, u32[]{:S(2)}, u32[]{:S(2)}) collective-permute-start(bf16[256,256]{1,0:T(8,128)(2,1)} %refs_0_.1), channel_id=1, source_target_pairs={{0,4},{1,5},{2,6},{3,7},{4,0},{5,1},{6,2},{7,3},{8,12},{9,13},{10,... | collective-permute-start | bytes 393224 | tf_op jit(solution)/shard_map/ppermute | solution.py:22
  15.9 12.4 %collective-permute-start.2 = (bf16[256,256]{1,0:T(8,128)(2,1)}, bf16[256,256]{1,0:T(8,128)(2,1)S(1)}, u32[]{:S(2)}, u32[]{:S(2)}) collective-permute-start(bf16[256,256]{1,0:T(8,128)(2,1)} %refs_0_.1), channel_id=1, source_target_pairs={{0,6},{1,7},{2,0},{3,1},{4,2},{5,3},{6,4},{7,5},{8,14},{9,15},{10,... | collective-permute-start | bytes 393224 | tf_op jit(solution)/shard_map/ppermute | solution.py:22
  19.6 18.2 %copy-start.19 = (s32[256,1]{0,1:T(1,128)}, s32[256,1]{0,1:T(1,128)S(1)}, u32[]{:S(2)}) copy-start(s32[256,1]{0,1:T(1,128)S(1)} %get-tuple-element.116) | copy-start | bytes 3076
  19.7 18.2 %copy-start.21 = (s32[256,1]{0,1:T(1,128)}, s32[256,1]{0,1:T(1,128)S(1)}, u32[]{:S(2)}) copy-start(s32[256,1]{0,1:T(1,128)S(1)} %get-tuple-element.117) | copy-start | bytes 3076
  19.7 18.2 %copy-start.23 = (s32[256,1]{0,1:T(1,128)}, s32[256,1]{0,1:T(1,128)S(1)}, u32[]{:S(2)}) copy-start(s32[256,1]{0,1:T(1,128)S(1)} %get-tuple-element.118) | copy-start | bytes 3076
  19.7 18.2 %copy-start.25 = (s32[256,1]{0,1:T(1,128)}, s32[256,1]{0,1:T(1,128)S(1)}, u32[]{:S(2)}) copy-start(s32[256,1]{0,1:T(1,128)S(1)} %get-tuple-element.119) | copy-start | bytes 3076
  19.7 18.2 %copy-start.27 = (s32[256,1]{0,1:T(1,128)}, s32[256,1]{0,1:T(1,128)S(1)}, u32[]{:S(2)}) copy-start(s32[256,1]{0,1:T(1,128)S(1)} %get-tuple-element.120) | copy-start | bytes 3076
  19.7 8.6 %copy-start.14 = (bf16[256,256]{1,0:T(8,128)(2,1)S(1)}, bf16[256,256]{1,0:T(8,128)(2,1)}, u32[]{:S(2)}) copy-start(bf16[256,256]{1,0:T(8,128)(2,1)} %refs_0_.1) | copy-start | bytes 393220
  21.3 8.8 %copy-start.6 = (bf16[256,768]{1,0:T(8,128)(2,1)}, bf16[256,768]{1,0:T(8,128)(2,1)S(1)}, u32[]{:S(2)}) copy-start(bf16[256,768]{1,0:T(8,128)(2,1)S(1)} %get-tuple-element.121.select_ref) | copy-start | bytes 1179652
  21.3 16.6 %copy-start.16 = (pred[256,768]{1,0:T(8,128)(4,1)}, pred[256,768]{1,0:T(8,128)(4,1)S(1)}, u32[]{:S(2)}) copy-start(pred[256,768]{1,0:T(8,128)(4,1)S(1)} %get-tuple-element.122) | copy-start | bytes 589828
  30.1 7.8 %copy-start.29 = (f32[256,8]{0,1:T(8,128)S(1)}, f32[256,8]{0,1:T(8,128)}, u32[]{:S(2)}) copy-start(f32[256,8]{0,1:T(8,128)} %param.9) | copy-start | bytes 24580
  30.1 29.8 %all-to-all-start.1 = ((bf16[32,24,1024]{2,1,0:T(8,128)(2,1)}), bf16[32,24,1024]{2,1,0:T(8,128)(2,1)S(1)}, u32[]{:S(2)}, u32[]{:S(2)}) async-start(bf16[32,24,1024]{2,1,0:T(8,128)(2,1)} %bitcast.128), calls=%async_computation.1 | async-start | bytes 3145728 | tf_op jit(solution)/shard_map/all_to_all | solution.py:36
  61.1 49.0 %all-to-all-start = ((bf16[32,24,2048]{2,1,0:T(8,128)(2,1)}), bf16[32,24,2048]{2,1,0:T(8,128)(2,1)}, u32[]{:S(2)}, u32[]{:S(2)}) async-start(bf16[32,24,2048]{2,1,0:T(8,128)(2,1)} %bitcast.127), calls=%async_computation | async-start | bytes 6291456 | tf_op jit(solution)/shard_map/all_to_all | solution.py:36
  69.3 14.9 %collective-permute-start.5 = (bf16[256,1024]{1,0:T(8,128)(2,1)S(1)}, bf16[256,1024]{1,0:T(8,128)(2,1)S(1)}, u32[]{:S(2)}, u32[]{:S(2)}) collective-permute-start(bf16[256,1024]{1,0:T(8,128)(2,1)S(1)} %get-tuple-element.98), channel_id=1, source_target_pairs={{0,1},{1,0},{2,3},{3,2},{4,5},{5,4},{6,7},{7,6},{8,9},{9,8},{10,11... | collective-permute-start | bytes 1572872 | tf_op jit(solution)/shard_map/ppermute | solution.py:26
  70.8 24.6 %collective-permute-start.4 = (bf16[256,1024]{1,0:T(8,128)(2,1)S(1)}, bf16[256,1024]{1,0:T(8,128)(2,1)S(1)}, u32[]{:S(2)}, u32[]{:S(2)}) collective-permute-start(bf16[256,1024]{1,0:T(8,128)(2,1)S(1)} %get-tuple-element.99), channel_id=1, source_target_pairs={{0,1},{1,0},{2,3},{3,2},{4,5},{5,4},{6,7},{7,6},{8,9},{9,8},{10,11... | collective-permute-start | bytes 1572872 | tf_op jit(solution)/shard_map/ppermute | solution.py:26
  71.4 34.4 %collective-permute-start.3 = (bf16[256,1024]{1,0:T(8,128)(2,1)S(1)}, bf16[256,1024]{1,0:T(8,128)(2,1)S(1)}, u32[]{:S(2)}, u32[]{:S(2)}) collective-permute-start(bf16[256,1024]{1,0:T(8,128)(2,1)S(1)} %get-tuple-element.100), channel_id=1, source_target_pairs={{0,1},{1,0},{2,3},{3,2},{4,5},{5,4},{6,7},{7,6},{8,9},{9,8},{10,11... | collective-permute-start | bytes 1572872 | tf_op jit(solution)/shard_map/ppermute | solution.py:26
  74.2 9.9 %copy-start.2 = (bf16[1,384,2048]{2,1,0:T(8,128)(2,1)S(1)}, bf16[1,384,2048]{2,1,0:T(8,128)(2,1)}, u32[]{:S(2)}) copy-start(bf16[1,384,2048]{2,1,0:T(8,128)(2,1)} %param.12) | copy-start | bytes 4718596
  110.1 47.2 %all-to-all-start.2 = ((bf16[32,24,2048]{2,1,0:T(8,128)(2,1)}), bf16[32,24,2048]{2,1,0:T(8,128)(2,1)}, u32[]{:S(2)}, u32[]{:S(2)}) async-start(bf16[32,24,2048]{2,1,0:T(8,128)(2,1)} %bitcast.125), calls=%async_computation.2 | async-start | bytes 6291456 | tf_op jit(solution)/shard_map/all_to_all | solution.py:36
  117.6 96.0 %reduce-scatter.2.cloned.1.call-start = ((), (), s32[]{:S(2)}) async-start(), calls=%async_computation.6 | async-start | bytes 2359296 | tf_op jit(solution)/shard_map/reduce_scatter | solution.py:389
  121.8 23.6 %collective-permute-start.8 = (bf16[256,1024]{1,0:T(8,128)(2,1)}, bf16[256,1024]{1,0:T(8,128)(2,1)S(1)}, u32[]{:S(2)}, u32[]{:S(2)}) collective-permute-start(bf16[256,1024]{1,0:T(8,128)(2,1)} %get-tuple-element.67), channel_id=1, source_target_pairs={{0,1},{1,0},{2,3},{3,2},{4,5},{5,4},{6,7},{7,6},{8,9},{9,8},{10,11... | collective-permute-start | bytes 1572872 | tf_op jit(solution)/shard_map/ppermute | solution.py:26
  127.3 20.7 %collective-permute-start.7 = (bf16[256,1024]{1,0:T(8,128)(2,1)}, bf16[256,1024]{1,0:T(8,128)(2,1)S(1)}, u32[]{:S(2)}, u32[]{:S(2)}) collective-permute-start(bf16[256,1024]{1,0:T(8,128)(2,1)} %get-tuple-element.62), channel_id=1, source_target_pairs={{0,1},{1,0},{2,3},{3,2},{4,5},{5,4},{6,7},{7,6},{8,9},{9,8},{10,11... | collective-permute-start | bytes 1572872 | tf_op jit(solution)/shard_map/ppermute | solution.py:26
  128.0 6.6 %copy-start.13 = (bf16[256,1024]{1,0:T(8,128)(2,1)S(1)}, bf16[256,1024]{1,0:T(8,128)(2,1)}, u32[]{:S(2)}) copy-start(bf16[256,1024]{1,0:T(8,128)(2,1)} %copy-done.12) | copy-start | bytes 1572868
  132.3 29.6 %collective-permute-start.6 = (bf16[256,1024]{1,0:T(8,128)(2,1)}, bf16[256,1024]{1,0:T(8,128)(2,1)}, u32[]{:S(2)}, u32[]{:S(2)}) collective-permute-start(bf16[256,1024]{1,0:T(8,128)(2,1)} %get-tuple-element.56), channel_id=1, source_target_pairs={{0,1},{1,0},{2,3},{3,2},{4,5},{5,4},{6,7},{7,6},{8,9},{9,8},{10,11... | collective-permute-start | bytes 1572872 | tf_op jit(solution)/shard_map/ppermute | solution.py:26
  164.6 28.3 %all-to-all-start.3 = ((bf16[32,24,1024]{2,1,0:T(8,128)(2,1)}), bf16[32,24,1024]{2,1,0:T(8,128)(2,1)S(1)}, u32[]{:S(2)}, u32[]{:S(2)}) async-start(bf16[32,24,1024]{2,1,0:T(8,128)(2,1)} %bitcast.126), calls=%async_computation.4 | async-start | bytes 3145728 | tf_op jit(solution)/shard_map/all_to_all | solution.py:36
  173.6 19.3 %copy-start.7 = (bf16[256,768]{1,0:T(8,128)(2,1)S(1)}, bf16[256,768]{1,0:T(8,128)(2,1)}, u32[]{:S(2)}) copy-start(bf16[256,768]{1,0:T(8,128)(2,1)} %copy-done.6) | copy-start | bytes 1179652
  178.1 3.9 %collective-permute-start.9 = (f32[8,256]{1,0:T(8,128)}, f32[8,256]{1,0:T(8,128)S(1)}, u32[]{:S(2)}, u32[]{:S(2)}) collective-permute-start(f32[8,256]{1,0:T(8,128)} %shard_map.132), channel_id=1, source_target_pairs={{0,1},{1,0},{2,3},{3,2},{4,5},{5,4},{6,7},{7,6},{8,9},{9,8},{10,11... | collective-permute-start | bytes 24584 | tf_op jit(solution)/shard_map/ppermute | solution.py:26
  194.2 21.6 %copy-start.18 = (f32[256,256]{1,0:T(8,128)S(1)}, f32[256,256]{1,0:T(8,128)}, u32[]{:S(2)}) copy-start(f32[256,256]{1,0:T(8,128)} %get-tuple-element.87) | copy-start | bytes 786436
  194.3 12.6 %collective-permute-start.12 = (bf16[288,256]{1,0:T(8,128)(2,1)}, bf16[288,256]{1,0:T(8,128)(2,1)S(1)}, u32[]{:S(2)}, u32[]{:S(2)}) collective-permute-start(bf16[288,256]{1,0:T(8,128)(2,1)} %get-tuple-element.89), channel_id=1, source_target_pairs={{0,4},{1,5},{2,6},{3,7},{4,0},{5,1},{6,2},{7,3},{8,12},{9,13},{10,... | collective-permute-start | bytes 442376 | tf_op jit(solution)/shard_map/ppermute | solution.py:22
  198.5 15.0 %collective-permute-start.11 = (bf16[288,256]{1,0:T(8,128)(2,1)}, bf16[288,256]{1,0:T(8,128)(2,1)S(1)}, u32[]{:S(2)}, u32[]{:S(2)}) collective-permute-start(bf16[288,256]{1,0:T(8,128)(2,1)} %get-tuple-element.88), channel_id=1, source_target_pairs={{0,2},{1,3},{2,4},{3,5},{4,6},{5,7},{6,0},{7,1},{8,10},{9,11},{10,... | collective-permute-start | bytes 442376 | tf_op jit(solution)/shard_map/ppermute | solution.py:22
  201.1 14.1 %collective-permute-start.10 = (bf16[288,256]{1,0:T(8,128)(2,1)}, bf16[288,256]{1,0:T(8,128)(2,1)S(1)}, u32[]{:S(2)}, u32[]{:S(2)}) collective-permute-start(bf16[288,256]{1,0:T(8,128)(2,1)} %get-tuple-element.85), channel_id=1, source_target_pairs={{0,6},{1,7},{2,0},{3,1},{4,2},{5,3},{6,4},{7,5},{8,14},{9,15},{10,... | collective-permute-start | bytes 442376 | tf_op jit(solution)/shard_map/ppermute | solution.py:22
  (17 other events, 79.4 us)
Sparse Core Ops, SparseCore 0:
  18.8 36.3 all-gather.1
  162.0 40.2 reduce-scatter.1
